TPU v7x, 32 devices: a whole 2x2x4 slice. The times are simulated.
32 devices in a mesh: parts: 2 (over y), slab: 4 (over z), cross: 2 (over x), sub: 2 (over core).
Axes of the slice: x: 2, y: 2, z: 4, core: 2. Of those that a mesh axis runs over, the one named last changes fastest.
Arguments:
- populations: float32 [19, 96, 24, 256], P(None, ('parts', 'slab'), 'cross', 'sub'), parts along dimension 1, may hold values from 0 to 1
- membrane: float32 [512, 3, 642], P(('parts', 'slab', 'cross', 'sub')), parts along dimension 0, may hold values from -4 to 4
- anchors: int32 [512, 3], P(('parts', 'slab', 'cross', 'sub')), parts along dimension 0, may hold values from 0 to 255, as said below
- targets: int32 [512], P(('parts', 'slab', 'cross', 'sub')), parts along dimension 0, may hold values from 0 to 255, as said below
Outputs:
- new_populations: float32 [19, 96, 24, 256], P(None, ('parts', 'slab'), 'cross', 'sub'), parts along dimension 1
- vertex_velocity: float32 [512, 3, 642], P(('parts', 'slab', 'cross', 'sub')), parts along dimension 0
There are 2 independent parts, one for each index of `parts`. A program takes and returns all parts, laid end to end along the dimension named above; each array names one. Nothing has to cross between parts.
Inputs may be any that keep to these rules, and one draw needn't show every extreme that they name: `targets`: slot numbers are owner * 16 + slot, owners counted slab-major over slab, cross, sub. The map is a bijection of the 256 slots. A cell keeps its owner or moves to the device one step up or one step down along slab (wrapping) with the same cross and sub indices; one device hands at most 4 cells to each of these two neighbours, and in every draw some device hands exactly 4 to its upper neighbour. `anchors`: the anchor lies inside the lattice block of the device that owns the cell's slot after migration.
All inputs are finite; a program needn't handle non-finite values.
Results may differ from a plain program's by a relative error of at most 0.0003.
Values sent between devices are 32-bit elements; how exact they have to be, the bound alone decides.
No kernel may reach another device: no remote copies, remote signals or barrier semaphores. Data moves between devices by JAX's collectives and lax.ppermute only.
A program may use at most 128 MiB of HBM per device.

v0:
```python
import math

import jax
import jax.numpy as jnp
import numpy as np
from jax import lax
from jax.sharding import PartitionSpec as P

GHOST = 6
MIG = 4


lattice_dirs = np.array(
    [
        [0, 0, 0],
        [1, 0, 0],
        [-1, 0, 0],
        [0, 1, 0],
        [0, -1, 0],
        [0, 0, 1],
        [0, 0, -1],
        [1, 1, 0],
        [-1, -1, 0],
        [1, -1, 0],
        [-1, 1, 0],
        [1, 0, 1],
        [-1, 0, -1],
        [1, 0, -1],
        [-1, 0, 1],
        [0, 1, 1],
        [0, -1, -1],
        [0, 1, -1],
        [0, -1, 1],
    ],
    dtype=np.int32,
)
lattice_weights = [1.0 / 3.0] + [1.0 / 18.0] * 6 + [1.0 / 36.0] * 12
relax_time = 0.8
spring_stiff = 0.05
bend_stiff = 0.002
rest_radius = 3.0
link_strides = (21, 34, 55)
highest = lax.Precision.HIGHEST


def passed_along(block, axis, distance):
    devices = range(lax.axis_size(axis))
    route = [((i - distance) % len(devices), i) for i in devices]
    return lax.ppermute(block, axis, route)


def padded_2(cells, sides, width):
    for axis, dim in sides:
        count = lax.axis_size(axis)
        head = lax.slice_in_dim(cells, 0, width, axis=dim)
        tail = lax.slice_in_dim(cells, cells.shape[dim] - width, cells.shape[dim], axis=dim)
        cells = jnp.concatenate(
            [
                lax.ppermute(tail, axis, [(i, (i + 1) % count) for i in range(count)]),
                cells,
                lax.ppermute(head, axis, [((i + 1) % count, i) for i in range(count)]),
            ],
            axis=dim,
        )
    return cells


def rest_shape(length, dtype):
    position = jnp.arange(length, dtype=jnp.int32)
    height = 1.0 - (2.0 * position.astype(dtype) + 1.0) / length
    across = jnp.sqrt(1.0 - height * height)
    azimuth = (position * 1597 % 2584).astype(dtype) * (2.0 * math.pi / 2584.0)
    return rest_radius * jnp.stack([across * jnp.cos(azimuth), across * jnp.sin(azimuth), height])


def along_chain(values, stride):
    padding = jnp.zeros(values.shape[:-1] + (abs(stride),), values.dtype)
    if stride > 0:
        return jnp.concatenate([values[..., stride:], padding], axis=-1)
    return jnp.concatenate([padding, values[..., :stride]], axis=-1)


def laplace(values, unities):
    total = jnp.zeros_like(values)
    for stride in link_strides:
        for signed in (stride, -stride):
            total = total + along_chain(unities, signed) * (along_chain(values, signed) - values)
    return total


def membrane_force(membrane):
    resting = rest_shape(membrane.shape[-1], membrane.dtype)
    unities = jnp.ones((membrane.shape[-1],), membrane.dtype)
    stretch = jnp.zeros_like(membrane)
    for stride in link_strides:
        for signed in (stride, -stride):
            linked = along_chain(unities, signed)
            difference = along_chain(membrane, signed) - membrane
            rest_gap = along_chain(resting, signed) - resting
            rest_square = jnp.sum(rest_gap * rest_gap, axis=0)
            now_square = jnp.sum(difference * difference, axis=1, keepdims=True)
            stretch = stretch + linked * (now_square - rest_square) / rest_square * difference
    bending = laplace(laplace(membrane - resting, unities), unities)
    return spring_stiff * stretch - bend_stiff * bending


def kernel_rows(membrane, reach):
    node_offsets = jnp.arange(2 * reach, dtype=jnp.int32).astype(membrane.dtype) - reach
    offsets = node_offsets[None, None, :, None] - membrane[:, :, None, :]
    return jnp.where(jnp.abs(offsets) < 2.0, 0.25 * (1.0 + jnp.cos(0.5 * math.pi * offsets)), 0.0)


def planar(weights):
    return (weights[:, 1, :, None, :] * weights[:, 2, None, :, :]).reshape(
        weights.shape[0], -1, weights.shape[-1]
    )


def spread_group(inputs):
    forcing, weights = inputs
    lifted = (forcing[:, :, None, :] * weights[:, 0, None, :, :]).reshape(
        forcing.shape[0], -1, forcing.shape[-1]
    )
    return jnp.einsum("bjv,bmv->bjm", lifted, planar(weights), precision=highest)


def sample_group(inputs):
    patches, weights = inputs
    mixed = jnp.einsum("bjm,bmv->bjv", patches, planar(weights), precision=highest)
    mixed = mixed.reshape(weights.shape[0], 3, weights.shape[2], weights.shape[3])
    return jnp.sum(mixed * weights[:, 0, None, :, :], axis=2)


def drift(pops, forcing):
    heading = jnp.asarray(lattice_dirs.T, pops.dtype)
    density = jnp.sum(pops, axis=0)
    momentum = jnp.einsum("ai,ixyz->axyz", heading, pops, precision=highest)
    return (density, (momentum + 0.5 * forcing) / density)


def collide(pops, forcing):
    density, velocity = drift(pops, forcing)
    heading = jnp.asarray(lattice_dirs, pops.dtype)
    weights = jnp.asarray(lattice_weights, pops.dtype)[:, None, None, None]
    aligned = jnp.einsum("ia,axyz->ixyz", heading, velocity, precision=highest)
    pushed = jnp.einsum("ia,axyz->ixyz", heading, forcing, precision=highest)
    kinetic = jnp.sum(velocity * velocity, axis=0)
    power_in = jnp.sum(velocity * forcing, axis=0)
    equilibrium = (
        weights * density * (1.0 + 3.0 * aligned + 4.5 * aligned * aligned - 1.5 * kinetic)
    )
    source = weights * (3.0 * (pushed - power_in) + 9.0 * aligned * pushed)
    return pops - (pops - equilibrium) / relax_time + (1.0 - 0.5 / relax_time) * source


def propagate(layers, extent):
    pieces = []
    for position in range(19):
        step_x, step_y, step_z = (int(value) for value in lattice_dirs[position])
        lower = (1 - step_x, 1 - step_y, 1 - step_z)
        upper = (lower[0] + extent[0], lower[1] + extent[1], lower[2] + extent[2])
        pieces.append(lax.slice(layers[position], lower, upper))
    return jnp.stack(pieces)


def fold_received(gathered, axis, reach):
    length = gathered.shape[axis] - 4 * reach
    interior = lax.slice_in_dim(gathered, 2 * reach, 2 * reach + length, axis=axis)
    from_lower = lax.slice_in_dim(gathered, 0, reach, axis=axis)
    from_upper = lax.slice_in_dim(gathered, 3 * reach + length, 4 * reach + length, axis=axis)
    middle_shape = list(interior.shape)
    middle_shape[axis] = length - 2 * reach
    return interior + jnp.concatenate(
        [from_lower, jnp.zeros(middle_shape, gathered.dtype), from_upper], axis=axis
    )


def on_device(populations, membrane, anchors, targets):
    reach = GHOST
    capacity = membrane.shape[0]
    vertices = membrane.shape[2]
    extent = populations.shape[1:]
    slab_count = lax.axis_size("slab")
    cross_count = lax.axis_size("cross")
    sub_count = lax.axis_size("sub")
    slab_here = lax.axis_index("slab")
    cross_here = lax.axis_index("cross")
    sub_here = lax.axis_index("sub")
    device_here = (slab_here * cross_count + cross_here) * sub_count + sub_here
    owner = targets // capacity
    slot_index = targets % capacity
    staying = owner == device_here
    leaving = jnp.logical_not(staying)
    columns = jnp.arange(capacity, dtype=jnp.int32)
    packed = jnp.concatenate(
        [
            membrane.reshape(capacity, 3 * vertices),
            anchors.astype(membrane.dtype),
            (targets + 1).astype(membrane.dtype)[:, None],
        ],
        axis=1,
    )
    kept = (staying[:, None] & (slot_index[:, None] == columns[None, :])).astype(packed.dtype)
    renewed_rows = jnp.einsum("cs,cw->sw", kept, packed, precision=highest)
    peer_slab = owner // (cross_count * sub_count)

    def departing(peer):
        marked = (leaving & (peer_slab == peer)).astype(jnp.int32)
        earlier = jnp.cumsum(marked) - marked
        chosen = (
            (marked[:, None] > 0) & (earlier[:, None] == jnp.arange(MIG, dtype=jnp.int32)[None, :])
        ).astype(packed.dtype)
        return jnp.einsum("cr,cw->rw", chosen, packed, precision=highest)

    from_below = passed_along(departing((slab_here + 1) % slab_count), "slab", 1)
    from_above = passed_along(departing((slab_here + slab_count - 1) % slab_count), "slab", -1)
    arrived = jnp.concatenate([from_below, from_above], axis=0)
    present = arrived[:, -1] > 0.5
    arrived_slot = (arrived[:, -1] - 1.0).astype(jnp.int32) % capacity
    placed = (present[:, None] & (arrived_slot[:, None] == columns[None, :])).astype(packed.dtype)
    renewed_rows = renewed_rows + jnp.einsum("rs,rw->sw", placed, arrived, precision=highest)
    moved = renewed_rows[:, : 3 * vertices].reshape(capacity, 3, vertices)
    root = jnp.stack([slab_here * extent[0], cross_here * extent[1], sub_here * extent[2]])
    corners = renewed_rows[:, 3 * vertices : 3 * vertices + 3].astype(jnp.int32) - root[None, :]
    forcing = membrane_force(moved)
    weights = kernel_rows(moved, reach)
    group_size = math.gcd(capacity, 16)
    groups = capacity // group_size
    grouped_weights = weights.reshape(groups, group_size, 3, 2 * reach, vertices)
    patches = lax.map(
        spread_group, (forcing.reshape(groups, group_size, 3, vertices), grouped_weights)
    )
    patches = patches.reshape(capacity, 3, 2 * reach, 2 * reach, 2 * reach)
    padded = jnp.zeros((3,) + tuple((side + 2 * reach for side in extent)), populations.dtype)

    def place(position, total):
        corner = corners[position]
        start_at = (jnp.int32(0), corner[0], corner[1], corner[2])
        current = lax.dynamic_slice(total, start_at, (3, 2 * reach, 2 * reach, 2 * reach))
        return lax.dynamic_update_slice(total, current + patches[position], start_at)

    padded = lax.fori_loop(0, capacity, place, padded)
    gathered = padded_2(padded, (("slab", 1), ("cross", 2), ("sub", 3)), reach)
    body_force = gathered
    for axis in (1, 2, 3):
        body_force = fold_received(body_force, axis, reach)
    post = collide(populations, body_force)
    layers = padded_2(post, (("slab", 1), ("cross", 2), ("sub", 3)), 1)
    renewed = propagate(layers, extent)
    _, velocity = drift(renewed, body_force)
    flow = padded_2(velocity, (("slab", 1), ("cross", 2), ("sub", 3)), reach)
    flow_patches = jax.vmap(
        lambda corner: lax.dynamic_slice(
            flow,
            (jnp.int32(0), corner[0], corner[1], corner[2]),
            (3, 2 * reach, 2 * reach, 2 * reach),
        )
    )(corners)
    vertex_velocity = lax.map(
        sample_group,
        (flow_patches.reshape(groups, group_size, 6 * reach, 4 * reach * reach), grouped_weights),
    )
    return (renewed, vertex_velocity.reshape(capacity, 3, vertices))


def solution(mesh):
    placed = (
        P(None, ("parts", "slab"), "cross", "sub"),
        P(("parts", "slab", "cross", "sub"), None, None),
        P(("parts", "slab", "cross", "sub"), None),
        P(("parts", "slab", "cross", "sub")),
    )
    return jax.shard_map(
        on_device,
        mesh=mesh,
        in_specs=placed,
        out_specs=(
            P(None, ("parts", "slab"), "cross", "sub"),
            P(("parts", "slab", "cross", "sub"), None, None),
        ),
        check_vma=False,
    )
```

profile of v0, /device:TPU:0, one launch (start us, length us, event | category | flops | bytes accessed | tf_op | source)
XLA Modules:
  0.0 616.1 jit_solution(1412615913002003247)
XLA Ops:
  30.9 11.9 %fusion.3 = f32[16,36,144]{2,1,0:T(8,128)S(1)} fusion(f32[16,144,642]{2,0,1:T(8,128)S(1)} %bitcast.165, f32[16,36,642]{2,0,1:T(8,128)S(1)} %bitcast.167), kind=kOutput, calls=%fused_computation.8 | convolution fusion | flops 639000576 | bytes 7727616 | tf_op jit(solution)/shard_map/while/body/eval_jaxpr/bjv,bmv->bjm/dot_general | solution.py:124
  47.0 294.2 %while.9 = (s32[]{:T(128)}, f32[3,24,24,140]{3,2,1,0:T(8,128)S(1)}, s32[16,3]{1,0:T(8,128)S(1)}, f32[16,3,12,12,12]{4,3,2,1,0:T(8,128)}, s32[]{:T(128)}, /*index=5*/s32[]{:T(128)}, s32[]{:T(128)}, s32[]{:T(128)}) while((s32[]{:T(128)}, f32[3,24,24,140]{3,2,1,0:T(8,128)S(1)}, s32[16,3]{1,0:T(8,128)S(1)}, f32[16,3,12,12,12]{4,3,2,1,0:T(8,128)}, ...), condition=%wide.region_16.17_spmd, body=%wide.region_15.16_spmd.sunk | while | flops 5195 | bytes 103939 | solution.py:242
  63.7 11.3 %dynamic_update_slice.14 = f32[3,24,24,140]{3,2,1,0:T(8,128)S(1)} dynamic-update-slice(f32[3,24,24,140]{3,2,1,0:T(8,128)S(1)} %get-tuple-element.348, f32[3,12,12,12]{3,2,1,0:T(8,128)S(1)} %bitcast_add_fusion.2, s32[]{:T(128)} %constant.204.clone.1..sunk, s32[]{:T(128)S(6)} %select_n.135, s32[]{:T(128)S(6)} %select_n.136, s32[]{:T(128)S(6)} %select_n.137) | dynamic-update-slice | bytes 41476 | tf_op jit(solution)/shard_map/while/body/eval_jaxpr/dynamic_update_slice | solution.py:240
  82.6 11.3 %dynamic_update_slice.14 = f32[3,24,24,140]{3,2,1,0:T(8,128)S(1)} dynamic-update-slice(f32[3,24,24,140]{3,2,1,0:T(8,128)S(1)} %get-tuple-element.348, f32[3,12,12,12]{3,2,1,0:T(8,128)S(1)} %bitcast_add_fusion.2, s32[]{:T(128)} %constant.204.clone.1..sunk, s32[]{:T(128)S(6)} %select_n.135, s32[]{:T(128)S(6)} %select_n.136, s32[]{:T(128)S(6)} %select_n.137) | dynamic-update-slice | bytes 41476 | tf_op jit(solution)/shard_map/while/body/eval_jaxpr/dynamic_update_slice | solution.py:240
  101.5 11.4 %dynamic_update_slice.14 = f32[3,24,24,140]{3,2,1,0:T(8,128)S(1)} dynamic-update-slice(f32[3,24,24,140]{3,2,1,0:T(8,128)S(1)} %get-tuple-element.348, f32[3,12,12,12]{3,2,1,0:T(8,128)S(1)} %bitcast_add_fusion.2, s32[]{:T(128)} %constant.204.clone.1..sunk, s32[]{:T(128)S(6)} %select_n.135, s32[]{:T(128)S(6)} %select_n.136, s32[]{:T(128)S(6)} %select_n.137) | dynamic-update-slice | bytes 41476 | tf_op jit(solution)/shard_map/while/body/eval_jaxpr/dynamic_update_slice | solution.py:240
  120.6 11.4 %dynamic_update_slice.14 = f32[3,24,24,140]{3,2,1,0:T(8,128)S(1)} dynamic-update-slice(f32[3,24,24,140]{3,2,1,0:T(8,128)S(1)} %get-tuple-element.348, f32[3,12,12,12]{3,2,1,0:T(8,128)S(1)} %bitcast_add_fusion.2, s32[]{:T(128)} %constant.204.clone.1..sunk, s32[]{:T(128)S(6)} %select_n.135, s32[]{:T(128)S(6)} %select_n.136, s32[]{:T(128)S(6)} %select_n.137) | dynamic-update-slice | bytes 41476 | tf_op jit(solution)/shard_map/while/body/eval_jaxpr/dynamic_update_slice | solution.py:240
  139.6 11.4 %dynamic_update_slice.14 = f32[3,24,24,140]{3,2,1,0:T(8,128)S(1)} dynamic-update-slice(f32[3,24,24,140]{3,2,1,0:T(8,128)S(1)} %get-tuple-element.348, f32[3,12,12,12]{3,2,1,0:T(8,128)S(1)} %bitcast_add_fusion.2, s32[]{:T(128)} %constant.204.clone.1..sunk, s32[]{:T(128)S(6)} %select_n.135, s32[]{:T(128)S(6)} %select_n.136, s32[]{:T(128)S(6)} %select_n.137) | dynamic-update-slice | bytes 41476 | tf_op jit(solution)/shard_map/while/body/eval_jaxpr/dynamic_update_slice | solution.py:240
  158.7 11.4 %dynamic_update_slice.14 = f32[3,24,24,140]{3,2,1,0:T(8,128)S(1)} dynamic-update-slice(f32[3,24,24,140]{3,2,1,0:T(8,128)S(1)} %get-tuple-element.348, f32[3,12,12,12]{3,2,1,0:T(8,128)S(1)} %bitcast_add_fusion.2, s32[]{:T(128)} %constant.204.clone.1..sunk, s32[]{:T(128)S(6)} %select_n.135, s32[]{:T(128)S(6)} %select_n.136, s32[]{:T(128)S(6)} %select_n.137) | dynamic-update-slice | bytes 41476 | tf_op jit(solution)/shard_map/while/body/eval_jaxpr/dynamic_update_slice | solution.py:240
  177.8 11.3 %dynamic_update_slice.14 = f32[3,24,24,140]{3,2,1,0:T(8,128)S(1)} dynamic-update-slice(f32[3,24,24,140]{3,2,1,0:T(8,128)S(1)} %get-tuple-element.348, f32[3,12,12,12]{3,2,1,0:T(8,128)S(1)} %bitcast_add_fusion.2, s32[]{:T(128)} %constant.204.clone.1..sunk, s32[]{:T(128)S(6)} %select_n.135, s32[]{:T(128)S(6)} %select_n.136, s32[]{:T(128)S(6)} %select_n.137) | dynamic-update-slice | bytes 41476 | tf_op jit(solution)/shard_map/while/body/eval_jaxpr/dynamic_update_slice | solution.py:240
  196.7 11.3 %dynamic_update_slice.14 = f32[3,24,24,140]{3,2,1,0:T(8,128)S(1)} dynamic-update-slice(f32[3,24,24,140]{3,2,1,0:T(8,128)S(1)} %get-tuple-element.348, f32[3,12,12,12]{3,2,1,0:T(8,128)S(1)} %bitcast_add_fusion.2, s32[]{:T(128)} %constant.204.clone.1..sunk, s32[]{:T(128)S(6)} %select_n.135, s32[]{:T(128)S(6)} %select_n.136, s32[]{:T(128)S(6)} %select_n.137) | dynamic-update-slice | bytes 41476 | tf_op jit(solution)/shard_map/while/body/eval_jaxpr/dynamic_update_slice | solution.py:240
  215.6 11.4 %dynamic_update_slice.14 = f32[3,24,24,140]{3,2,1,0:T(8,128)S(1)} dynamic-update-slice(f32[3,24,24,140]{3,2,1,0:T(8,128)S(1)} %get-tuple-element.348, f32[3,12,12,12]{3,2,1,0:T(8,128)S(1)} %bitcast_add_fusion.2, s32[]{:T(128)} %constant.204.clone.1..sunk, s32[]{:T(128)S(6)} %select_n.135, s32[]{:T(128)S(6)} %select_n.136, s32[]{:T(128)S(6)} %select_n.137) | dynamic-update-slice | bytes 41476 | tf_op jit(solution)/shard_map/while/body/eval_jaxpr/dynamic_update_slice | solution.py:240
  234.7 11.4 %dynamic_update_slice.14 = f32[3,24,24,140]{3,2,1,0:T(8,128)S(1)} dynamic-update-slice(f32[3,24,24,140]{3,2,1,0:T(8,128)S(1)} %get-tuple-element.348, f32[3,12,12,12]{3,2,1,0:T(8,128)S(1)} %bitcast_add_fusion.2, s32[]{:T(128)} %constant.204.clone.1..sunk, s32[]{:T(128)S(6)} %select_n.135, s32[]{:T(128)S(6)} %select_n.136, s32[]{:T(128)S(6)} %select_n.137) | dynamic-update-slice | bytes 41476 | tf_op jit(solution)/shard_map/while/body/eval_jaxpr/dynamic_update_slice | solution.py:240
  253.7 11.4 %dynamic_update_slice.14 = f32[3,24,24,140]{3,2,1,0:T(8,128)S(1)} dynamic-update-slice(f32[3,24,24,140]{3,2,1,0:T(8,128)S(1)} %get-tuple-element.348, f32[3,12,12,12]{3,2,1,0:T(8,128)S(1)} %bitcast_add_fusion.2, s32[]{:T(128)} %constant.204.clone.1..sunk, s32[]{:T(128)S(6)} %select_n.135, s32[]{:T(128)S(6)} %select_n.136, s32[]{:T(128)S(6)} %select_n.137) | dynamic-update-slice | bytes 41476 | tf_op jit(solution)/shard_map/while/body/eval_jaxpr/dynamic_update_slice | solution.py:240
  272.8 11.4 %dynamic_update_slice.14 = f32[3,24,24,140]{3,2,1,0:T(8,128)S(1)} dynamic-update-slice(f32[3,24,24,140]{3,2,1,0:T(8,128)S(1)} %get-tuple-element.348, f32[3,12,12,12]{3,2,1,0:T(8,128)S(1)} %bitcast_add_fusion.2, s32[]{:T(128)} %constant.204.clone.1..sunk, s32[]{:T(128)S(6)} %select_n.135, s32[]{:T(128)S(6)} %select_n.136, s32[]{:T(128)S(6)} %select_n.137) | dynamic-update-slice | bytes 41476 | tf_op jit(solution)/shard_map/while/body/eval_jaxpr/dynamic_update_slice | solution.py:240
  291.9 11.3 %dynamic_update_slice.14 = f32[3,24,24,140]{3,2,1,0:T(8,128)S(1)} dynamic-update-slice(f32[3,24,24,140]{3,2,1,0:T(8,128)S(1)} %get-tuple-element.348, f32[3,12,12,12]{3,2,1,0:T(8,128)S(1)} %bitcast_add_fusion.2, s32[]{:T(128)} %constant.204.clone.1..sunk, s32[]{:T(128)S(6)} %select_n.135, s32[]{:T(128)S(6)} %select_n.136, s32[]{:T(128)S(6)} %select_n.137) | dynamic-update-slice | bytes 41476 | tf_op jit(solution)/shard_map/while/body/eval_jaxpr/dynamic_update_slice | solution.py:240
  310.8 11.4 %dynamic_update_slice.14 = f32[3,24,24,140]{3,2,1,0:T(8,128)S(1)} dynamic-update-slice(f32[3,24,24,140]{3,2,1,0:T(8,128)S(1)} %get-tuple-element.348, f32[3,12,12,12]{3,2,1,0:T(8,128)S(1)} %bitcast_add_fusion.2, s32[]{:T(128)} %constant.204.clone.1..sunk, s32[]{:T(128)S(6)} %select_n.135, s32[]{:T(128)S(6)} %select_n.136, s32[]{:T(128)S(6)} %select_n.137) | dynamic-update-slice | bytes 41476 | tf_op jit(solution)/shard_map/while/body/eval_jaxpr/dynamic_update_slice | solution.py:240
  329.8 11.3 %dynamic_update_slice.14 = f32[3,24,24,140]{3,2,1,0:T(8,128)S(1)} dynamic-update-slice(f32[3,24,24,140]{3,2,1,0:T(8,128)S(1)} %get-tuple-element.348, f32[3,12,12,12]{3,2,1,0:T(8,128)S(1)} %bitcast_add_fusion.2, s32[]{:T(128)} %constant.204.clone.1..sunk, s32[]{:T(128)S(6)} %select_n.135, s32[]{:T(128)S(6)} %select_n.136, s32[]{:T(128)S(6)} %select_n.137) | dynamic-update-slice | bytes 41476 | tf_op jit(solution)/shard_map/while/body/eval_jaxpr/dynamic_update_slice | solution.py:240
  341.2 8.1 %collective-permute-start.2 = (f32[3,6,24,140]{3,2,1,0:T(8,128)S(1)}, f32[3,6,24,140]{3,2,1,0:T(8,128)S(1)}, u32[]{:S(2)}, u32[]{:S(2)}) collective-permute-start(f32[3,6,24,140]{3,2,1,0:T(8,128)S(1)} %get-tuple-element.229), channel_id=1, source_target_pairs={{0,4},{4,8},{8,12},{12,0},{1,5},{5,9},{9,13},{13,1},{2,6},{6,10},{... | collective-permute-start | bytes 725768 | tf_op jit(solution)/shard_map/ppermute | solution.py:59
  351.1 9.4 %collective-permute-done.2 = f32[3,6,24,140]{3,2,1,0:T(8,128)S(1)} collective-permute-done((f32[3,6,24,140]{3,2,1,0:T(8,128)S(1)}, f32[3,6,24,140]{3,2,1,0:T(8,128)S(1)}, u32[]{:S(2)}, u32[]{:S(2)}) %collective-permute-start.2) | collective-permute-done | bytes 241952 | tf_op jit(solution)/shard_map/ppermute | solution.py:59
  374.7 17.1 %collective-permute-done.4 = f32[3,36,6,140]{3,1,2,0:T(8,128)S(1)} collective-permute-done((f32[3,36,6,140]{3,1,2,0:T(8,128)S(1)}, f32[3,36,6,140]{3,1,2,0:T(8,128)S(1)}, u32[]{:S(2)}, u32[]{:S(2)}) %collective-permute-start.4) | collective-permute-done | bytes 362912 | tf_op jit(solution)/shard_map/ppermute | solution.py:59
  392.2 14.3 %collective-permute-done.5 = f32[3,36,6,140]{3,1,2,0:T(8,128)S(1)} collective-permute-done((f32[3,36,6,140]{3,1,2,0:T(8,128)S(1)}, f32[3,36,6,140]{3,1,2,0:T(8,128)S(1)}, u32[]{:S(2)}, u32[]{:S(2)}) %collective-permute-start.5) | collective-permute-done | bytes 362912 | tf_op jit(solution)/shard_map/ppermute | solution.py:61
  431.8 8.2 %pad_maximum_fusion.1 = f32[3,36,36,152]{3,0,2,1:T(4,128)S(1)} fusion(f32[3,36,36,6]{3,0,2,1:T(4,128)} %copy.164, f32[3,36,6,140]{3,0,2,1:T(4,128)} %copy-done.9, f32[3,36,24,140]{3,0,2,1:T(4,128)S(1)} %copy_dynamic-update-slice_fusion.1, f32[3,36,6,140]{3,0,2,1:T(4,128)} %copy-done.7, f32[3,36,36,6]{3,0,2,1:T(4,128)} %copy.163), kind=kLoop, calls=%fused_computation.11 | loop fusion | flops 2363904 | bytes 4727808 | tf_op jit(solution)/shard_map/concatenate | solution.py:57
  543.8 57.6 %while.10 = (s32[]{:T(128)}, f32[3,24,24,140]{3,0,2,1:T(4,128)S(1)}, s32[16,4]{0,1:T(4,128)S(1)}, f32[16,3,12,12,12]{4,3,2,1,0:T(8,128)}, s32[]{:T(128)}) while((s32[]{:T(128)}, f32[3,24,24,140]{3,0,2,1:T(4,128)S(1)}, s32[16,4]{0,1:T(4,128)S(1)}, f32[16,3,12,12,12]{4,3,2,1,0:T(8,128)}, s32[]{:T(128)}) %tuple.128), condition=%wide.while_cond, body=%wide.while_body.sunk | while | flops 2 | bytes 357765 | solution.py:253
  605.1 8.9 %fusion.1 = f32[16,36,642]{2,1,0:T(8,128)S(1)} fusion(f32[16,36,144]{2,1,0:T(8,128)S(1)} %reshape.591, f32[16,144,642]{2,0,1:T(8,128)} %bitcast.166), kind=kOutput, calls=%fused_computation.6 | convolution fusion | flops 639000576 | bytes 7727616 | tf_op jit(solution)/shard_map/while/body/eval_jaxpr/bjm,bmv->bjv/dot_general | solution.py:129
  (365 shorter events, 272.1 us)
Async XLA Ops:
  4.0 6.8 %collective-permute-start.1 = (f32[4,1930]{1,0:T(4,128)S(1)}, f32[4,1930]{1,0:T(4,128)S(1)}, u32[]{:S(2)}, u32[]{:S(2)}) collective-permute-start(f32[4,1930]{1,0:T(4,128)S(1)} %fusion.43), channel_id=1, source_target_pairs={{4,0},{8,4},{12,8},{0,12},{5,1},{9,5},{13,9},{1,13},{6,2},{10,6},{... | collective-permute-start | bytes 92648 | tf_op jit(solution)/shard_map/ppermute | solution.py:49
  9.6 5.8 collective-permute-start
  341.1 9.9 %copy-start.6 = (f32[3,24,24,140]{3,2,1,0:T(8,128)}, f32[3,24,24,140]{3,2,1,0:T(8,128)S(1)}, u32[]{:S(2)}) copy-start(f32[3,24,24,140]{3,2,1,0:T(8,128)S(1)} %get-tuple-element.105) | copy-start | bytes 2903044
  341.2 19.3 %collective-permute-start.2 = (f32[3,6,24,140]{3,2,1,0:T(8,128)S(1)}, f32[3,6,24,140]{3,2,1,0:T(8,128)S(1)}, u32[]{:S(2)}, u32[]{:S(2)}) collective-permute-start(f32[3,6,24,140]{3,2,1,0:T(8,128)S(1)} %get-tuple-element.229), channel_id=1, source_target_pairs={{0,4},{4,8},{8,12},{12,0},{1,5},{5,9},{9,13},{13,1},{2,6},{6,10},{... | collective-permute-start | bytes 725768 | tf_op jit(solution)/shard_map/ppermute | solution.py:59
  349.3 22.1 %collective-permute-start.3 = (f32[3,6,24,140]{3,2,1,0:T(8,128)S(1)}, f32[3,6,24,140]{3,2,1,0:T(8,128)S(1)}, u32[]{:S(2)}, u32[]{:S(2)}) collective-permute-start(f32[3,6,24,140]{3,2,1,0:T(8,128)S(1)} %get-tuple-element.228), channel_id=1, source_target_pairs={{4,0},{8,4},{12,8},{0,12},{5,1},{9,5},{13,9},{1,13},{6,2},{10,6},{... | collective-permute-start | bytes 725768 | tf_op jit(solution)/shard_map/ppermute | solution.py:61
  372.3 19.4 %collective-permute-start.4 = (f32[3,36,6,140]{3,1,2,0:T(8,128)S(1)}, f32[3,36,6,140]{3,1,2,0:T(8,128)S(1)}, u32[]{:S(2)}, u32[]{:S(2)}) collective-permute-start(f32[3,36,6,140]{3,1,2,0:T(8,128)S(1)} %copy.157), channel_id=1, source_target_pairs={{0,2},{2,0},{1,3},{3,1},{4,6},{6,4},{5,7},{7,5},{8,10},{10,8},{9,1... | collective-permute-start | bytes 1088648 | tf_op jit(solution)/shard_map/ppermute | solution.py:59
  373.8 32.7 %collective-permute-start.5 = (f32[3,36,6,140]{3,1,2,0:T(8,128)S(1)}, f32[3,36,6,140]{3,1,2,0:T(8,128)S(1)}, u32[]{:S(2)}, u32[]{:S(2)}) collective-permute-start(f32[3,36,6,140]{3,1,2,0:T(8,128)S(1)} %copy.158), channel_id=1, source_target_pairs={{2,0},{0,2},{3,1},{1,3},{6,4},{4,6},{7,5},{5,7},{10,8},{8,10},{11,... | collective-permute-start | bytes 1088648 | tf_op jit(solution)/shard_map/ppermute | solution.py:61
  392.2 14.8 %copy-start.7 = (f32[3,36,6,140]{3,0,2,1:T(4,128)}, f32[3,36,6,140]{3,0,2,1:T(4,128)S(1)}, u32[]{:S(2)}) copy-start(f32[3,36,6,140]{3,0,2,1:T(4,128)S(1)} %copy.159) | copy-start | bytes 1088644
  417.4 6.8 %collective-permute-start.6 = (f32[3,36,36,6]{2,1,3,0:T(8,128)}, f32[3,36,36,6]{2,1,3,0:T(8,128)}, u32[]{:S(2)}, u32[]{:S(2)}) collective-permute-start(f32[3,36,36,6]{2,1,3,0:T(8,128)} %copy.161), channel_id=1, source_target_pairs={{0,1},{1,0},{2,3},{3,2},{4,5},{5,4},{6,7},{7,6},{8,9},{9,8},{10,11... | collective-permute-start | bytes 279944 | tf_op jit(solution)/shard_map/ppermute | solution.py:59
  421.2 6.8 %collective-permute-start.7 = (f32[3,36,36,6]{2,1,3,0:T(8,128)}, f32[3,36,36,6]{2,1,3,0:T(8,128)}, u32[]{:S(2)}, u32[]{:S(2)}) collective-permute-start(f32[3,36,36,6]{2,1,3,0:T(8,128)} %copy.162), channel_id=1, source_target_pairs={{1,0},{0,1},{3,2},{2,3},{5,4},{4,5},{7,6},{6,7},{9,8},{8,9},{11,10... | collective-permute-start | bytes 279944 | tf_op jit(solution)/shard_map/ppermute | solution.py:61
  453.9 17.7 %copy-start.1 = (f32[19,12,12,128]{3,0,2,1:T(8,128)}, f32[19,12,12,128]{3,0,2,1:T(8,128)S(1)}, u32[]{:S(2)}) copy-start(f32[19,12,12,128]{3,0,2,1:T(8,128)S(1)} %fusion.17) | copy-start | bytes 4202500
  453.9 8.6 %collective-permute-start.8 = (f32[19,1,12,128]{3,0,2,1:T(8,128)S(1)}, f32[19,1,12,128]{3,0,2,1:T(8,128)S(1)}, u32[]{:S(2)}, u32[]{:S(2)}) collective-permute-start(f32[19,1,12,128]{3,0,2,1:T(8,128)S(1)} %get-tuple-element.224), channel_id=1, source_target_pairs={{0,4},{4,8},{8,12},{12,0},{1,5},{5,9},{9,13},{13,1},{2,6},{6,10},{... | collective-permute-start | bytes 350216 | tf_op jit(solution)/shard_map/ppermute | solution.py:59
  454.0 9.0 %collective-permute-start.9 = (f32[19,1,12,128]{3,0,2,1:T(8,128)S(1)}, f32[19,1,12,128]{3,0,2,1:T(8,128)S(1)}, u32[]{:S(2)}, u32[]{:S(2)}) collective-permute-start(f32[19,1,12,128]{3,0,2,1:T(8,128)S(1)} %get-tuple-element.225), channel_id=1, source_target_pairs={{4,0},{8,4},{12,8},{0,12},{5,1},{9,5},{13,9},{1,13},{6,2},{10,6},{... | collective-permute-start | bytes 350216 | tf_op jit(solution)/shard_map/ppermute | solution.py:61
  463.0 6.8 %collective-permute-start.10 = (f32[19,14,1,128]{3,0,2,1:T(8,128)S(1)}, f32[19,14,1,128]{3,0,2,1:T(8,128)S(1)}, u32[]{:S(2)}, u32[]{:S(2)}) collective-permute-start(f32[19,14,1,128]{3,0,2,1:T(8,128)S(1)} %get-tuple-element.222), channel_id=1, source_target_pairs={{0,2},{2,0},{1,3},{3,1},{4,6},{6,4},{5,7},{7,5},{8,10},{10,8},{9,1... | collective-permute-start | bytes 408584 | tf_op jit(solution)/shard_map/ppermute | solution.py:59
  464.4 7.2 %collective-permute-start.11 = (f32[19,14,1,128]{3,0,2,1:T(8,128)S(1)}, f32[19,14,1,128]{3,0,2,1:T(8,128)S(1)}, u32[]{:S(2)}, u32[]{:S(2)}) collective-permute-start(f32[19,14,1,128]{3,0,2,1:T(8,128)S(1)} %get-tuple-element.223), channel_id=1, source_target_pairs={{2,0},{0,2},{3,1},{1,3},{6,4},{4,6},{7,5},{5,7},{10,8},{8,10},{11,... | collective-permute-start | bytes 408584 | tf_op jit(solution)/shard_map/ppermute | solution.py:61
  476.7 2.7 collective-permute-start.12
  478.9 2.7 collective-permute-start.13
  503.6 11.7 %copy-start.11 = (f32[19,12,12,128]{3,0,2,1:T(8,128)}, f32[19,12,12,128]{3,0,2,1:T(8,128)S(1)}, u32[]{:S(2)}) copy-start(f32[19,12,12,128]{3,0,2,1:T(8,128)S(1)} %copy.201) | copy-start | bytes 4202500
  504.8 8.6 %collective-permute-start.14 = (f32[3,6,12,128]{3,0,2,1:T(4,128)S(1)}, f32[3,6,12,128]{3,0,2,1:T(4,128)S(1)}, u32[]{:S(2)}, u32[]{:S(2)}) collective-permute-start(f32[3,6,12,128]{3,0,2,1:T(4,128)S(1)} %get-tuple-element.239), channel_id=1, source_target_pairs={{0,4},{4,8},{8,12},{12,0},{1,5},{5,9},{9,13},{13,1},{2,6},{6,10},{... | collective-permute-start | bytes 331784 | tf_op jit(solution)/shard_map/ppermute | solution.py:59
  506.4 8.8 %collective-permute-start.15 = (f32[3,6,12,128]{3,0,2,1:T(4,128)S(1)}, f32[3,6,12,128]{3,0,2,1:T(4,128)S(1)}, u32[]{:S(2)}, u32[]{:S(2)}) collective-permute-start(f32[3,6,12,128]{3,0,2,1:T(4,128)S(1)} %get-tuple-element.240), channel_id=1, source_target_pairs={{4,0},{8,4},{12,8},{0,12},{5,1},{9,5},{13,9},{1,13},{6,2},{10,6},{... | collective-permute-start | bytes 331784 | tf_op jit(solution)/shard_map/ppermute | solution.py:61
  515.4 10.0 %collective-permute-start.16 = (f32[3,24,6,128]{3,0,2,1:T(4,128)S(1)}, f32[3,24,6,128]{3,0,2,1:T(4,128)S(1)}, u32[]{:S(2)}, u32[]{:S(2)}) collective-permute-start(f32[3,24,6,128]{3,0,2,1:T(4,128)S(1)} %get-tuple-element.235), channel_id=1, source_target_pairs={{0,2},{2,0},{1,3},{3,1},{4,6},{6,4},{5,7},{7,5},{8,10},{10,8},{9,1... | collective-permute-start | bytes 663560 | tf_op jit(solution)/shard_map/ppermute | solution.py:59
  517.0 13.4 %collective-permute-start.17 = (f32[3,24,6,128]{3,0,2,1:T(4,128)S(1)}, f32[3,24,6,128]{3,0,2,1:T(4,128)S(1)}, u32[]{:S(2)}, u32[]{:S(2)}) collective-permute-start(f32[3,24,6,128]{3,0,2,1:T(4,128)S(1)} %get-tuple-element.236), channel_id=1, source_target_pairs={{2,0},{0,2},{3,1},{1,3},{6,4},{4,6},{7,5},{5,7},{10,8},{8,10},{11,... | collective-permute-start | bytes 663560 | tf_op jit(solution)/shard_map/ppermute | solution.py:61
  532.7 1.9 collective-permute-start.18
  533.3 2.8 collective-permute-start.19
  (21 other events, 64.1 us)
where the time goes:
time: 628 us; the launch traced here: 616 us
  local copies, waits for them, and re-layouts  304 us (48%)
  loops' own time  94 us (15%)
  waiting for transfers between devices  83.5 us (13%)
  other arithmetic  72.9 us (12%)
  starting transfers between devices  30.7 us (5%)
  matrix products  28.8 us (5%)
    dynamic_update_slice x16, local copies, waits for them, and re-layouts, place(): lax.dynamic_update_slice(total, current + patches[position], start_at)  172 us
    another operation x1, loops' own time, on_device(): padded = lax.fori_loop(0, capacity, place, padded)  93.9 us
    gather x64, local copies, waits for them, and re-layouts  57.5 us
    ppermute x9, waiting for transfers between devices, padded_2(): lax.ppermute(tail, axis, [(i, (i + 1) % count) for i in range(count)])  47.7 us
    ppermute x9, waiting for transfers between devices, padded_2(): lax.ppermute(head, axis, [((i + 1) % count, i) for i in range(count)])  31.1 us
    concatenate x7, other arithmetic, padded_2(): jnp.concatenate([lax.ppermute(tail, axis, [(i, (i + 1) % count) for i in...  20 us
    add x16, other arithmetic, place(): current + patches[position]  18 us
    slice x11, local copies, waits for them, and re-layouts, padded_2(): lax.slice_in_dim(cells, cells.shape[dim] - width, cells.shape[dim], axis=...  15.6 us
  transfers between devices with their start and end apart: 20, of which 13 were waited for; matrix products, arithmetic and copies ran while one was open for 4% of the time, Pallas kernels for 0%

commit v1 on v0

v1 whole, which is shorter than its diff:
```python
import functools
import math

import jax
import jax.numpy as jnp
import numpy as np
from jax import lax
from jax.experimental import pallas as pl
from jax.experimental.pallas import tpu as pltpu
from jax.sharding import PartitionSpec as P

REACH = 6
MIG = 4
STRIDES = (21, 34, 55)
DIRS = (
    (0, 0, 0),
    (1, 0, 0), (-1, 0, 0), (0, 1, 0), (0, -1, 0), (0, 0, 1), (0, 0, -1),
    (1, 1, 0), (-1, -1, 0), (1, -1, 0), (-1, 1, 0),
    (1, 0, 1), (-1, 0, -1), (1, 0, -1), (-1, 0, 1),
    (0, 1, 1), (0, -1, -1), (0, 1, -1), (0, -1, 1),
)
RISING = (5, 11, 14, 15, 18)
FALLING = (6, 12, 13, 16, 17)
WEIGHTS = (1.0 / 3.0,) + (1.0 / 18.0,) * 6 + (1.0 / 36.0,) * 12
FAR = 100.0
F32 = jnp.float32
VMEM = pl.BlockSpec(memory_space=pltpu.VMEM)
SMEM = pl.BlockSpec(memory_space=pltpu.SMEM)


def params(limit=40):
    return pltpu.CompilerParams(vmem_limit_bytes=limit * 1024 * 1024)


def chain_table(vertices, width):
    v = np.arange(vertices)
    h = 1.0 - (2.0 * v + 1.0) / vertices
    t = 2.0 * math.pi / 2584.0 * (v * 1597 % 2584)
    across = np.sqrt(1.0 - h * h)
    rest = 3.0 * np.stack([across * np.cos(t), across * np.sin(t), h])
    table = np.zeros((16, width))
    for n, s in enumerate(STRIDES):
        gap = rest[:, s:] - rest[:, :-s]
        table[5 * n : 5 * n + 3, : vertices - s] = gap
        table[5 * n + 3, : vertices - s] = 0.05 / np.sum(gap * gap, axis=0)
        table[5 * n + 4, : vertices - s] = 1.0
    return jnp.asarray(table, F32)


def pack_kernel(capacity, slabs, plane, here, targets, anchors, membrane, up, down, up_info, down_info):
    for r in range(MIG):
        up_info[r, 0] = -1
        down_info[r, 0] = -1

    def step(c, counts):
        target = targets[c]
        owner = target // capacity
        peer = owner // plane
        slot = target - owner * capacity
        slab = here[0]
        leaving = owner != here[3]
        rises = jnp.logical_and(leaving, peer == lax.rem(slab + 1, slabs))
        falls = jnp.logical_and(leaving, peer == lax.rem(slab + slabs - 1, slabs))

        @pl.when(rises)
        def _():
            n = counts[0]
            up[n] = membrane[c]
            up_info[n, 0] = slot
            for d in range(3):
                up_info[n, 1 + d] = anchors[c, d]

        @pl.when(falls)
        def _():
            n = counts[1]
            down[n] = membrane[c]
            down_info[n, 0] = slot
            for d in range(3):
                down_info[n, 1 + d] = anchors[c, d]

        return (
            jnp.minimum(counts[0] + rises.astype(jnp.int32), MIG - 1 + 1),
            jnp.minimum(counts[1] + falls.astype(jnp.int32), MIG - 1 + 1),
        )

    lax.fori_loop(0, capacity, step, (jnp.int32(0), jnp.int32(0)))


def assemble_kernel(
    capacity, vertices, extent, here, targets, anchors, below_info, above_info, membrane, below, above, pos, corner
):
    pos[...] = jnp.full(pos.shape, FAR, F32)
    roots = [here[d] * extent[d] for d in range(3)]

    def put(slot, source, n, known):
        for a in range(3):
            pos[a, pl.ds(slot, 1), 0:vertices] = source(a)
        for d in range(3):
            corner[slot, d] = known(d) - roots[d]

    def step(c, carry):
        target = targets[c]
        owner = target // capacity
        slot = target - owner * capacity

        @pl.when(owner == here[3])
        def _():
            put(slot, lambda a: membrane[a, pl.ds(c, 1), :], c, lambda d: anchors[c, d])

        return carry

    lax.fori_loop(0, capacity, step, jnp.int32(0))
    for cells, info in ((below, below_info), (above, above_info)):
        for r in range(MIG):
            slot = info[r, 0]

            @pl.when(slot >= 0)
            def _():
                put(slot, lambda a: cells[r, a : a + 1, :], r, lambda d: info[r, 1 + d])


def wide(tile, width):
    return jnp.concatenate([tile] * (width // 128), axis=1)


def waves(x):
    h = (x - 4.0 * jnp.floor(0.25 * x + 0.5)) * (math.pi / 4.0)
    q = h * h
    sine = h * (1.0 + q * (-1 / 6 + q * (1 / 120 + q * (-1 / 5040 + q * (1 / 362880 - q * (1 / 39916800))))))
    cosine = 1.0 + q * (
        -1 / 2 + q * (1 / 24 + q * (-1 / 720 + q * (1 / 40320 + q * (-1 / 3628800 + q * (1 / 479001600)))))
    )
    return 0.25 - 0.5 * sine * sine, 0.5 * sine * cosine


def fill_waves(pos, wave):
    for a in range(3):
        wave[2 * a], wave[2 * a + 1] = waves(pos[a])


def fill_force(pos, table, force):
    cells, width = pos.shape[1:]
    for h in range(cells // 8):
        rows = slice(8 * h, 8 * h + 8)
        x = [pos[a, rows, :] for a in range(3)]
        lap = [jnp.zeros((8, width), F32) for _ in range(3)]
        pulls = []
        for n, s in enumerate(STRIDES):
            gap = [table[5 * n + a : 5 * n + a + 1, :] for a in range(3)]
            scale = table[5 * n + 3 : 5 * n + 4, :]
            mask = table[5 * n + 4 : 5 * n + 5, :]
            d = [pltpu.roll(x[a], width - s, 1) - x[a] for a in range(3)]
            square = d[0] * d[0] + d[1] * d[1] + d[2] * d[2]
            strain = square * scale - 0.05 * mask
            pulls.append([strain * d[a] for a in range(3)])
            for a in range(3):
                bend = mask * d[a] - gap[a]
                lap[a] = lap[a] + bend - pltpu.roll(bend, s, 1)
        for a in range(3):
            total = jnp.zeros((8, width), F32)
            for n, s in enumerate(STRIDES):
                mask = table[5 * n + 4 : 5 * n + 5, :]
                t = pulls[n][a] - 0.002 * (mask * (pltpu.roll(lap[a], width - s, 1) - lap[a]))
                total = total + t - pltpu.roll(t, s, 1)
            force[a, rows, :] = total


def split(x):
    high = x.astype(jnp.bfloat16)
    return high, (x - high.astype(F32)).astype(jnp.bfloat16)


def row_of(ref, i, c):
    return jnp.broadcast_to(ref[i, pl.ds(c, 1), :], (8, ref.shape[2]))


def fill_planar(pos, wave, c, high, low):
    width = pos.shape[2]
    row = lax.broadcasted_iota(jnp.int32, (8, 128), 0)
    rowf = wide((row - REACH).astype(F32), width)
    odd = wide((row & 1), width) == 1
    flip = wide((row & 2), width) == 0
    z, cz, sz = row_of(pos, 2, c), row_of(wave, 4, c), row_of(wave, 5, c)
    base = jnp.where(odd, sz, cz)
    pattern = 0.25 + jnp.where(flip, -base, base)
    wz = jnp.concatenate(
        [
            jnp.where(jnp.abs(rowf - z) < 2.0, pattern, 0.0),
            jnp.where(jnp.abs(rowf + 8.0 - z) < 2.0, pattern, 0.0),
        ],
        axis=0,
    )
    x, cx, sx = row_of(pos, 0, c), row_of(wave, 0, c), row_of(wave, 1, c)
    quarter = (0.25 - cx, 0.25 - sx, 0.25 + cx, 0.25 + sx)
    for kx in range(2 * REACH):
        wx = jnp.where(jnp.abs(x - float(kx - REACH)) < 2.0, quarter[kx % 4], 0.0)
        high[16 * kx : 16 * kx + 16, :], low[16 * kx : 16 * kx + 16, :] = split(
            jnp.concatenate([wx, wx], axis=0) * wz
        )


def rows_weight(pos, wave, c, anchor, images):
    width = pos.shape[2]
    n = lax.broadcasted_iota(jnp.int32, (8, 128), 0) - 1 - anchor
    nf = wide(n.astype(F32), width)
    odd = wide(n & 1, width) == 1
    flip = wide(n & 2, width) == 2
    y, cy, sy = row_of(pos, 1, c), row_of(wave, 2, c), row_of(wave, 3, c)
    base = jnp.where(odd, sy, cy)
    pattern = 0.25 + jnp.where(flip, -base, base)
    halves = []
    for h in range(2):
        gap = nf + 8.0 * h - y
        near = jnp.abs(gap - float(images[0])) < 2.0
        for image in images[1:]:
            near = jnp.logical_or(near, jnp.abs(gap - float(image)) < 2.0)
        halves.append(jnp.where(near, pattern, 0.0))
    return jnp.concatenate(halves, axis=0)


def nt_dot(a, b):
    return lax.dot_general(a, b, (((1,), (1,)), ((), ())), preferred_element_type=F32)


def spread_kernel(images, first, corner, pos, table, *refs):
    if first:
        acc, far, wave, force, high, low, patch = refs
        acc[...] = jnp.zeros(acc.shape, F32)
        far[...] = jnp.zeros(far.shape, F32)
    else:
        acc_in, far_in, acc, far, wave, force, high, low, patch = refs
        acc[...] = acc_in[...]
        far[...] = far_in[...]
    cells = pos.shape[1]
    fill_waves(pos, wave)
    fill_force(pos, table, force)

    def weigh(c, b):
        fill_planar(pos, wave, c, high.at[b], low.at[b])
        wy = rows_weight(pos, wave, c, corner[c, 1], images)
        lifted = []
        for a in range(3):
            f = row_of(force, a, c)
            lifted.append(jnp.concatenate([f, f], axis=0) * wy)
        lhigh, llow = split(jnp.concatenate(lifted, axis=0))
        both = nt_dot(jnp.concatenate([lhigh, llow], axis=0), high[b])
        total = both[:48] + both[48:] + nt_dot(lhigh, low[b])
        patch[c, :, 0:192] = total

    def weigh_two(i, carry):
        weigh(2 * i, 0)
        weigh(2 * i + 1, 1)
        return carry

    lax.fori_loop(0, cells // 2, weigh_two, 0)
    lane = lax.broadcasted_iota(jnp.int32, (48, 128), 1)

    def rolled(c, kx, z0):
        t = kx // 8
        return pltpu.roll(
            patch[c, :, 128 * t : 128 * t + 128], (z0 + 256 - 16 * (kx % 8)) & 127, 1
        )

    def place(c, carry):
        z0 = corner[c, 2] - REACH
        x0 = corner[c, 0]
        inside = jnp.logical_and(lane >= z0, lane < z0 + 16)
        for kx in range(2 * REACH):
            acc[x0 + kx] += jnp.where(inside, rolled(c, kx, z0), 0.0)
        return carry

    lax.fori_loop(0, cells, place, 0)

    def place_far(c, carry):
        z0 = corner[c, 2] - REACH
        x0 = corner[c, 0]

        @pl.when(jnp.logical_or(z0 < 0, z0 + 12 > 128))
        def _():
            outside = jnp.logical_or(lane >= z0 + 128, lane < z0 - 112)
            for kx in range(2 * REACH):
                far[x0 + kx] += jnp.where(outside, rolled(c, kx, z0), 0.0)

        return carry

    lax.fori_loop(0, cells, place_far, 0)


def spread(images, corner, pos, table, sums=None):
    cells, width = pos.shape[1:]
    shape = jax.ShapeDtypeStruct((24, 48, 128), F32)
    first = sums is None
    return pl.pallas_call(
        functools.partial(spread_kernel, images, first),
        out_shape=(shape, shape),
        in_specs=[SMEM, VMEM, VMEM] + ([] if first else [VMEM, VMEM]),
        out_specs=(VMEM, VMEM),
        scratch_shapes=[
            pltpu.VMEM((6, cells, width), F32),
            pltpu.VMEM((3, cells, width), F32),
            pltpu.VMEM((2, 192, width), jnp.bfloat16),
            pltpu.VMEM((2, 192, width), jnp.bfloat16),
            pltpu.VMEM((cells, 48, 256), F32),
        ],
        compiler_params=params(),
        name="spread",
        cost_estimate=pl.CostEstimate(flops=int(2e9), bytes_accessed=4_000_000, transcendentals=0),
    )(corner, pos, table, *(() if first else sums))


def sample_kernel(images, corner, pos, low_side, own, high_side, low_far, own_far, high_far, out, flow, far, wave, high, low):
    cells, width = pos.shape[1:]
    at = 0
    for part, part_far in ((low_side, low_far), (own, own_far), (high_side, high_far)):
        size = part.shape[0]
        flow[at : at + size] = part[...]
        far[at : at + size] = part_far[...]
        at += size
    fill_waves(pos, wave)
    lane = lax.broadcasted_iota(jnp.int32, (48, 128), 1)
    group = lane // 16

    def sample(c, b):
        fill_planar(pos, wave, c, high.at[b], low.at[b])
        z0 = corner[c, 2] - REACH
        x0 = corner[c, 0]
        outside = jnp.logical_or(lane >= z0 + 128, lane < z0 - 112)
        tiles = [jnp.zeros((48, 128), F32), jnp.zeros((48, 128), F32)]
        for kx in range(2 * REACH):
            g = kx % 8
            source = jnp.where(outside, far[x0 + kx], flow[x0 + kx])
            turned = pltpu.roll(source, (16 * g + 256 - z0) & 127, 1)
            tiles[kx // 8] = jnp.where(group == g, turned, tiles[kx // 8])
        whole = jnp.concatenate([tiles[0], tiles[1][:, 0:64]], axis=1)
        qhigh, qlow = split(whole)
        both = jnp.dot(jnp.concatenate([qhigh, qlow], axis=0), high[b], preferred_element_type=F32)
        mixed = both[:48] + both[48:] + jnp.dot(qhigh, low[b], preferred_element_type=F32)
        wy = rows_weight(pos, wave, c, corner[c, 1], images)
        for a in range(3):
            out[a, pl.ds(c, 1), :] = jnp.sum(mixed[16 * a : 16 * a + 16] * wy, axis=0, keepdims=True)

    def sample_two(i, carry):
        sample(2 * i, 0)
        sample(2 * i + 1, 1)
        return carry

    lax.fori_loop(0, cells // 2, sample_two, 0)


def sampled(images, corner, pos, parts):
    cells, width = pos.shape[1:]
    return pl.pallas_call(
        functools.partial(sample_kernel, images),
        out_shape=jax.ShapeDtypeStruct((3, cells, width), F32),
        in_specs=[SMEM] + [VMEM] * 7,
        out_specs=VMEM,
        scratch_shapes=[
            pltpu.VMEM((24, 48, 128), F32),
            pltpu.VMEM((24, 48, 128), F32),
            pltpu.VMEM((6, cells, width), F32),
            pltpu.VMEM((2, 192, width), jnp.bfloat16),
            pltpu.VMEM((2, 192, width), jnp.bfloat16),
        ],
        compiler_params=params(),
        name="sample",
        cost_estimate=pl.CostEstimate(flops=int(2e9), bytes_accessed=4_000_000, transcendentals=0),
    )(corner, pos, *parts)


def extend_kernel(pops, x_low, x_high, y_low, y_high, out):
    nx, ny = pops.shape[:2]
    directions = pops.shape[2]
    for x in range(nx + 2):
        middle = x_low[0] if x == 0 else (x_high[0] if x == nx + 1 else pops[x - 1])
        block = jnp.concatenate([y_low[x : x + 1], middle, y_high[x : x + 1], y_low[x : x + 1], y_low[x : x + 1]], axis=0)
        out[:, x] = jnp.transpose(block, (1, 0, 2))


def collide_kernel(pops, own, from_low, from_high, post, force, edge):
    planes = pops.shape[1]
    n_low, n_high = from_low.shape[0], from_high.shape[0]
    for e in range(planes):
        total = own[e]
        if e < n_low:
            total = total + from_low[e]
        if e >= planes - n_high:
            total = total + from_high[e - (planes - n_high)]
        force[e] = total
    lane = lax.broadcasted_iota(jnp.int32, (16, 128), 1)

    def plane(e, carry):
        p = [pops[i, e] for i in range(19)]
        f = [force[e, 16 * a : 16 * a + 16, :] for a in range(3)]
        rho = p[0]
        for i in range(1, 19):
            rho = rho + p[i]
        u = []
        for a in range(3):
            m = 0.5 * f[a]
            for i in range(1, 19):
                if DIRS[i][a] == 1:
                    m = m + p[i]
                elif DIRS[i][a] == -1:
                    m = m - p[i]
            u.append(m / rho)
        kinetic = u[0] * u[0] + u[1] * u[1] + u[2] * u[2]
        power = u[0] * f[0] + u[1] * f[1] + u[2] * f[2]
        level = 1.25 * rho * (1.0 - 1.5 * kinetic) - 1.125 * power
        bow, tilt = 5.625 * rho, 3.75 * rho
        new = [None] * 19
        new[0] = WEIGHTS[0] * level - 0.25 * p[0]
        for i in range(1, 19, 2):
            along = [a for a in range(3) if DIRS[i][a] != 0]
            cu, cf = None, None
            for a in along:
                tu, tf = u[a], f[a]
                if DIRS[i][a] < 0:
                    tu, tf = -tu, -tf
                cu = tu if cu is None else cu + tu
                cf = tf if cf is None else cf + tf
            even = WEIGHTS[i] * (level + cu * (bow * cu + 3.375 * cf))
            odd = WEIGHTS[i] * (tilt * cu + 1.125 * cf)
            new[i] = even + odd - 0.25 * p[i]
            new[i + 1] = even - odd - 0.25 * p[i + 1]
        for i in range(19):
            post[i, e] = new[i]
        for j in range(5):
            edge[j, e] = jnp.where(
                lane == 0, pltpu.roll(new[RISING[j]], 1, 1), pltpu.roll(new[FALLING[j]], 127, 1)
            )
        return carry

    lax.fori_loop(0, planes, plane, 0)


def stream_kernel(post, edge, force, pops, velocity):
    ny = pops.shape[1]
    lane = lax.broadcasted_iota(jnp.int32, (ny, 128), 1)
    velocity[...] = jnp.zeros(velocity.shape, F32)

    def plane(x, carry):
        n = []
        for i in range(19):
            cx, cy, cz = DIRS[i]
            value = post[i, x + 1 - cx, 1 - cy : 1 - cy + ny, :]
            if cz == 1:
                side = edge[RISING.index(i), x + 1 - cx, 1 - cy : 1 - cy + ny, :]
                value = jnp.where(lane == 0, side, pltpu.roll(value, 1, 1))
            elif cz == -1:
                side = edge[FALLING.index(i), x + 1 - cx, 1 - cy : 1 - cy + ny, :]
                value = jnp.where(lane == 127, side, pltpu.roll(value, 127, 1))
            n.append(value)
        rho = n[0]
        for i in range(1, 19):
            rho = rho + n[i]
        for a in range(3):
            m = 0.5 * force[x + 1, 16 * a + 1 : 16 * a + 1 + ny, :]
            for i in range(1, 19):
                if DIRS[i][a] == 1:
                    m = m + n[i]
                elif DIRS[i][a] == -1:
                    m = m - n[i]
            velocity[x, 16 * a + 1 : 16 * a + 1 + ny, :] = m / rho
        pops[x] = jnp.transpose(jnp.stack(n), (1, 0, 2))
        return carry

    lax.fori_loop(0, pops.shape[0], plane, 0)


def shifted(x, axis, distance):
    count = lax.axis_size(axis)
    return lax.ppermute(x, axis, [(i, (i + distance) % count) for i in range(count)])


def on_device(populations, membrane, anchors, targets):
    extent = populations.shape[1:]
    capacity, _, vertices = membrane.shape
    slabs, crosses, subs = (lax.axis_size(a) for a in ("slab", "cross", "sub"))
    assert subs == 2 and extent == (12, 12, 128) and capacity % 8 == 0
    width = -(-vertices // 128) * 128
    place = [lax.axis_index(a) for a in ("slab", "cross", "sub")]
    here = jnp.stack(place + [(place[0] * crosses + place[1]) * subs + place[2]]).astype(jnp.int32)
    table = chain_table(vertices, width)

    cell = jax.ShapeDtypeStruct((MIG, 3, vertices), F32)
    info = jax.ShapeDtypeStruct((MIG, 4), jnp.int32)
    up, down, up_info, down_info = pl.pallas_call(
        functools.partial(pack_kernel, capacity, slabs, crosses * subs),
        out_shape=(cell, cell, info, info),
        in_specs=[SMEM, SMEM, SMEM, VMEM],
        out_specs=(VMEM, VMEM, SMEM, SMEM),
        compiler_params=params(),
        name="pack",
    )(here, targets, anchors, membrane)
    below, above = shifted(up, "slab", 1), shifted(down, "slab", -1)
    below_info, above_info = shifted(up_info, "slab", 1), shifted(down_info, "slab", -1)
    pos, corner = pl.pallas_call(
        functools.partial(assemble_kernel, capacity, vertices, extent),
        out_shape=(
            jax.ShapeDtypeStruct((3, capacity, width), F32),
            jax.ShapeDtypeStruct((capacity, 3), jnp.int32),
        ),
        in_specs=[SMEM] * 5 + [VMEM] * 3,
        out_specs=(VMEM, SMEM),
        compiler_params=params(),
        name="assemble",
    )(here, targets, anchors, below_info, above_info, jnp.transpose(membrane, (1, 0, 2)), below, above)

    pops = jnp.transpose(populations, (1, 2, 0, 3))
    x_low = shifted(pops[extent[0] - 1 :], "slab", 1)
    x_high = shifted(pops[:1], "slab", -1)
    first = jnp.concatenate([x_low[:, 0], pops[:, 0], x_high[:, 0]])
    last = jnp.concatenate([x_low[:, -1], pops[:, -1], x_high[:, -1]])
    if crosses == 2:
        rows = shifted(jnp.stack([last, first]), "cross", 1)
        y_low, y_high = rows[0], rows[1]
    else:
        y_low, y_high = shifted(last, "cross", 1), shifted(first, "cross", -1)
    planes = extent[0] + 2
    extended = pl.pallas_call(
        extend_kernel,
        out_shape=jax.ShapeDtypeStruct((19, planes, 16, 128), F32),
        in_specs=[VMEM] * 5,
        out_specs=VMEM,
        compiler_params=params(),
        name="extend",
    )(pops, x_low, x_high, y_low, y_high)

    if crosses == 2:
        others = [(1, (extent[1], -extent[1]))]
    else:
        others = [(1, (-extent[1],)), (-1, (extent[1],))]
    visitors = [(shifted(corner, "cross", d), shifted(pos, "cross", d), images, d) for d, images in others]
    sums = spread((0,), corner, pos, table)
    for their_corner, their_pos, images, _ in visitors:
        sums = spread(images, their_corner, their_pos, table, sums)
    acc = sums[0] + shifted(sums[1], "sub", 1)
    from_high = shifted(acc[: REACH + 1], "slab", -1)
    from_low = shifted(acc[REACH + extent[0] - 1 : 2 * REACH + extent[0] - 1], "slab", 1)
    own = acc[REACH - 1 : REACH - 1 + planes]

    post, force, edge = pl.pallas_call(
        collide_kernel,
        out_shape=(
            jax.ShapeDtypeStruct((19, planes, 16, 128), F32),
            jax.ShapeDtypeStruct((planes, 48, 128), F32),
            jax.ShapeDtypeStruct((5, planes, 16, 128), F32),
        ),
        in_specs=[VMEM] * 4,
        out_specs=(VMEM,) * 3,
        compiler_params=params(),
        name="collide",
    )(extended, own, from_low, from_high)
    edge = shifted(edge, "sub", 1)
    renewed, velocity = pl.pallas_call(
        stream_kernel,
        out_shape=(
            jax.ShapeDtypeStruct((extent[0], extent[1], 19, 128), F32),
            jax.ShapeDtypeStruct((extent[0], 48, 128), F32),
        ),
        in_specs=[VMEM] * 3,
        out_specs=(VMEM,) * 2,
        compiler_params=params(),
        name="stream",
    )(post, edge, force)

    low_side = shifted(velocity[extent[0] - REACH :], "slab", 1)
    high_side = shifted(velocity[: REACH - 1], "slab", -1)
    parts = (low_side, velocity, high_side)
    parts = parts + tuple(shifted(part, "sub", 1) for part in parts)
    shares = [
        shifted(sampled(images, their_corner, their_pos, parts), "cross", -d)
        for their_corner, their_pos, images, d in visitors
    ]
    total = sampled((0,), corner, pos, parts)
    for share in shares:
        total = total + share
    return (
        jnp.transpose(renewed, (2, 0, 1, 3)),
        jnp.transpose(total[:, :, :vertices], (1, 0, 2)),
    )


def solution(mesh):
    placed = (
        P(None, ("parts", "slab"), "cross", "sub"),
        P(("parts", "slab", "cross", "sub"), None, None),
        P(("parts", "slab", "cross", "sub"), None),
        P(("parts", "slab", "cross", "sub")),
    )
    return jax.shard_map(
        on_device,
        mesh=mesh,
        in_specs=placed,
        out_specs=(
            P(None, ("parts", "slab"), "cross", "sub"),
            P(("parts", "slab", "cross", "sub"), None, None),
        ),
        check_vma=False,
    )
```

time: 628 us -> 84.4 us (0.13); the launches traced: 616 us -> 84.4 us
  local copies, waits for them, and re-layouts: 304 us -> 4.62 us
  loops' own time: 94 us -> 0 us
  other arithmetic: 72.9 us -> 0.88 us
  waiting for transfers between devices: 83.5 us -> 14.7 us
  Pallas kernels: 0 us -> 38.6 us
  matrix products: 28.8 us -> 0 us
    dynamic_update_slice x16 -> x0, local copies, waits for them, and re-layouts: 172 us -> none  [place(): lax.dynamic_update_slice(total, current + patches[position], start_at)]
    another operation x2 -> x0, loops' own time: 94 us -> none  [the longest x1 93.9 us: on_device(): padded = lax.fori_loop(0, capacity, place, padded)]
    ppermute x20 -> x19, waiting for transfers between devices: 83.5 us -> 14.7 us  [shifted(): lax.ppermute(x, axis, [(i, (i + distance) % count) for i in range(count)])]
    gather x64 -> x0, local copies, waits for them, and re-layouts: 57.5 us -> none
    pallas_call x0 -> x9, Pallas kernels: none -> 38.6 us  [the longest x2 19.4 us: spread(): pl.pallas_call(functools.partial(spread_kernel, images, first), out_shape...]
    slice x46 -> x6, local copies, waits for them, and re-layouts: 34.8 us -> 1.07 us  [the longest x1 1 us: on_device(): x_high = shifted(pops[:1], 'slab', -1)]
    dot_general x10 -> x0, matrix products: 28.8 us -> none  [the longest x1 11.9 us: spread_group(): jnp.einsum('bjv,bmv->bjm', lifted, planar(weights), precision=highest)]
    add x20 -> x1, other arithmetic: 25.4 us -> 0.07 us  [on_device(): acc = sums[0] + shifted(sums[1], 'sub', 1)]
  transfers between devices with their start and end apart: 20 -> 19, of which waited for: 13 -> 7; matrix products, arithmetic and copies ran while one was open for 4% -> 3% of each run, Pallas kernels for 0% -> 32%
where the time goes in v1:
time: 84.4 us
  Pallas kernels  38.6 us (46%)
  starting transfers between devices  24.7 us (29%)
  waiting for transfers between devices  14.7 us (17%)
  local copies, waits for them, and re-layouts  4.62 us (5%)
  between operations  0.92 us (1%)
  other arithmetic  0.88 us (1%)
    ppermute x19, starting transfers between devices, shifted(): lax.ppermute(x, axis, [(i, (i + distance) % count) for i in range(count)])  24.7 us
    pallas_call x2, Pallas kernels, spread(): pl.pallas_call(functools.partial(spread_kernel, images, first), out_shape...  19.4 us
    ppermute x19, waiting for transfers between devices, shifted(): lax.ppermute(x, axis, [(i, (i + distance) % count) for i in range(count)])  14.7 us
    pallas_call x2, Pallas kernels, sampled(): pl.pallas_call(functools.partial(sample_kernel, images), out_shape=jax.Sh...  10.3 us
    unnamed x12, local copies, waits for them, and re-layouts  2.52 us
    pallas_call x1, Pallas kernels, on_device(): pl.pallas_call(stream_kernel, out_shape=(jax.ShapeDtypeStruct((extent[0],...  2.46 us
    pallas_call x1, Pallas kernels, on_device(): pl.pallas_call(collide_kernel, out_shape=(jax.ShapeDtypeStruct((19, plane...  2.22 us
    pallas_call x1, Pallas kernels, on_device(): pl.pallas_call(functools.partial(assemble_kernel, capacity, vertices, ext...  1.93 us
  transfers between devices with their start and end apart: 19, of which 7 were waited for; matrix products, arithmetic and copies ran while one was open for 3% of the time, Pallas kernels for 32%

profile of v1, /device:TPU:0, one launch (start us, length us, event | category | flops | bytes accessed | tf_op | source)
XLA Modules:
  0.0 84.4 jit_solution(14137833482712038480)
XLA Ops:
  1.5 1.0 %copy.8.membrane = f32[16,3,642]{2,1,0:T(4,128)S(1)} copy(f32[16,3,642]{2,0,1:T(8,128)} %param.6) | data formatting | bytes 246528 | tf_op args[1]
  3.3 1.9 %pack.1 = (f32[4,3,642]{2,1,0:T(4,128)S(1)}, f32[4,3,642]{2,1,0:T(4,128)S(1)}, s32[4,4]{1,0:T(4,128)S(1)}, s32[4,4]{1,0:T(4,128)S(1)}) custom-call(s32[4]{0:T(128)S(1)} %pad_add_fusion.here, s32[16]{0:T(128)S(1)} %copy-done.2, s32[16,3]{1,0:T(8,128)S(1)} %copy.9.anchors, f32[16,3,642]{2,1,0:T(4,128)S(1)} %copy.8.membrane), custom_call_target="tpu_custom_call" | custom-call | tf_op jit(solution)/shard_map/pack/pallas_call | solution.py:487
  5.2 3.1 %collective-permute-start.3 = (s32[4,4]{1,0:T(4,128)S(1)}, s32[4,4]{1,0:T(4,128)S(1)}, u32[]{:S(2)}, u32[]{:S(2)}) collective-permute-start(s32[4,4]{1,0:T(4,128)S(1)} %get-tuple-element.17), channel_id=1, source_target_pairs={{0,4},{4,8},{8,12},{12,0},{1,5},{5,9},{9,13},{13,1},{2,6},{6,10},{... | collective-permute-start | bytes 200 | tf_op jit(solution)/shard_map/ppermute | solution.py:472
  8.2 2.1 %collective-permute-start.4 = (s32[4,4]{1,0:T(4,128)S(1)}, s32[4,4]{1,0:T(4,128)S(1)}, u32[]{:S(2)}, u32[]{:S(2)}) collective-permute-start(s32[4,4]{1,0:T(4,128)S(1)} %get-tuple-element.18), channel_id=1, source_target_pairs={{0,12},{4,0},{8,4},{12,8},{1,13},{5,1},{9,5},{13,9},{2,14},{6,2},{... | collective-permute-start | bytes 200 | tf_op jit(solution)/shard_map/ppermute | solution.py:472
  10.3 3.8 %collective-permute-start.6 = (f32[4,3,642]{2,1,0:T(4,128)S(1)}, f32[4,3,642]{2,1,0:T(4,128)S(1)}, u32[]{:S(2)}, u32[]{:S(2)}) collective-permute-start(f32[4,3,642]{2,1,0:T(4,128)S(1)} %get-tuple-element.20), channel_id=1, source_target_pairs={{0,12},{4,0},{8,4},{12,8},{1,13},{5,1},{9,5},{13,9},{2,14},{6,2},{... | collective-permute-start | bytes 92456 | tf_op jit(solution)/shard_map/ppermute | solution.py:472
  15.4 1.0 %slice_bitcast_fusion.3 = (f32[12,19,128]{2,1,0:T(8,128)S(1)}, f32[12,19,128]{2,1,0:T(8,128)S(1)}) fusion(f32[12,12,19,128]{3,2,1,0:T(8,128)} %bitcast.30), kind=kLoop, calls=%fused_computation.8 | loop fusion | bytes 466944 | tf_op jit(solution)/shard_map/squeeze | solution.py:513
  16.4 1.9 %collective-permute-start = (f32[1,12,19,128]{3,2,1,0:T(8,128)S(1)}, f32[1,12,19,128]{3,2,1,0:T(8,128)S(1)}, u32[]{:S(2)}, u32[]{:S(2)}) collective-permute-start(f32[1,12,19,128]{3,2,1,0:T(8,128)S(1)} %get-tuple-element.35), channel_id=1, source_target_pairs={{0,4},{4,8},{8,12},{12,0},{1,5},{5,9},{9,13},{13,1},{2,6},{6,10},{... | collective-permute-start | bytes 350216 | tf_op jit(solution)/shard_map/ppermute | solution.py:472
  18.3 1.9 %assemble.1 = (f32[3,16,768]{2,1,0:T(8,128)S(1)}, s32[16,3]{1,0:T(8,128)S(1)}) custom-call(s32[4]{0:T(128)S(1)} %pad_add_fusion.here, s32[16]{0:T(128)S(1)} %copy-done.3, s32[16,3]{1,0:T(8,128)S(1)} %copy.9.anchors, s32[4,4]{1,0:T(4,128)S(1)} %collective-permute-done.3.below_info, s32[4,4]{1,0:T(4,128)S(1)} %collective-permute-done.4.above_info, ...), custom_call_target="tpu_custom_call" | custom-call | tf_op jit(solution)/shard_map/assemble/pallas_call | solution.py:497
  20.3 1.7 %collective-permute-start.7 = (s32[16,3]{1,0:T(8,128)S(1)}, s32[16,3]{1,0:T(8,128)S(1)}, u32[]{:S(2)}, u32[]{:S(2)}) collective-permute-start(s32[16,3]{1,0:T(8,128)S(1)} %get-tuple-element.21.corner), channel_id=1, source_target_pairs={{0,2},{2,0},{1,3},{3,1},{4,6},{6,4},{5,7},{7,5},{8,10},{10,8},{9,1... | collective-permute-start | bytes 584 | tf_op jit(solution)/shard_map/ppermute | solution.py:472
  22.4 10.0 %spread.2 = (f32[24,48,128]{2,1,0:T(8,128)S(1)}, f32[24,48,128]{2,1,0:T(8,128)S(1)}) custom-call(s32[16,3]{1,0:T(8,128)S(1)} %get-tuple-element.21.corner, f32[3,16,768]{2,1,0:T(8,128)S(1)} %get-tuple-element.22.pos, f32[16,768]{1,0:T(8,128)S(1)} %copy-done.4), custom_call_target="tpu_custom_call" | custom-call | flops 2000000000 | bytes 4000000 | tf_op jit(solution)/shard_map/spread/pallas_call | solution.py:293
  32.4 9.4 %spread.3 = (f32[24,48,128]{2,1,0:T(8,128)S(1)}, f32[24,48,128]{2,1,0:T(8,128)S(1)}) custom-call(s32[16,3]{1,0:T(8,128)S(1)} %collective-permute-done.7.corner, f32[3,16,768]{2,1,0:T(8,128)S(1)} %collective-permute-done.8.pos, f32[16,768]{1,0:T(8,128)S(1)} %copy-done.4, f32[24,48,128]{2,1,0:T(8,128)S(1)} %get-tuple-element.23.refs_0_, ...), custom_call_target="tpu_custom_call" | custom-call | flops 2000000000 | bytes 4000000 | tf_op jit(solution)/shard_map/spread/pallas_call | solution.py:293
  42.0 1.7 %collective-permute-start.2 = (f32[2,14,19,128]{3,2,1,0:T(8,128)S(1)}, f32[2,14,19,128]{3,2,1,0:T(8,128)S(1)}, u32[]{:S(2)}, u32[]{:S(2)}) collective-permute-start(f32[2,14,19,128]{3,2,1,0:T(8,128)S(1)} %pad_maximum_fusion), channel_id=1, source_target_pairs={{0,2},{2,0},{1,3},{3,1},{4,6},{6,4},{5,7},{7,5},{8,10},{10,8},{9,1... | collective-permute-start | bytes 817160 | tf_op jit(solution)/shard_map/ppermute | solution.py:472
  44.2 3.7 %collective-permute-start.11 = (f32[7,48,128]{2,1,0:T(8,128)S(1)}, f32[7,48,128]{2,1,0:T(8,128)S(1)}, u32[]{:S(2)}, u32[]{:S(2)}) collective-permute-start(f32[7,48,128]{2,1,0:T(8,128)S(1)} %slice.76), channel_id=1, source_target_pairs={{0,12},{4,0},{8,4},{12,8},{1,13},{5,1},{9,5},{13,9},{2,14},{6,2},{... | collective-permute-start | bytes 516104 | tf_op jit(solution)/shard_map/ppermute | solution.py:472
  47.9 4.6 %collective-permute-done.2 = f32[2,14,19,128]{3,2,1,0:T(8,128)S(1)} collective-permute-done((f32[2,14,19,128]{3,2,1,0:T(8,128)S(1)}, f32[2,14,19,128]{3,2,1,0:T(8,128)S(1)}, u32[]{:S(2)}, u32[]{:S(2)}) %collective-permute-start.2) | collective-permute-done | bytes 272416 | tf_op jit(solution)/shard_map/ppermute | solution.py:472
  53.7 2.2 %collide.1 = (f32[19,14,16,128]{3,2,1,0:T(8,128)S(1)}, f32[14,48,128]{2,1,0:T(8,128)S(1)}, f32[5,14,16,128]{3,2,1,0:T(8,128)S(1)}) custom-call(f32[19,14,16,128]{3,2,1,0:T(8,128)S(1)} %extend.1.pops, f32[14,48,128]{2,1,0:T(8,128)S(1)} %slice.74.own, f32[6,48,128]{2,1,0:T(8,128)S(1)} %collective-permute-done.10.from_low, ...), custom_call_target="tpu_custom_call" | custom-call | tf_op jit(solution)/shard_map/collide/pallas_call | solution.py:542
  56.0 2.0 %collective-permute-done.12.edge = f32[5,14,16,128]{3,2,1,0:T(8,128)S(1)} collective-permute-done((f32[5,14,16,128]{3,2,1,0:T(8,128)S(1)}, f32[5,14,16,128]{3,2,1,0:T(8,128)S(1)}, u32[]{:S(2)}, u32[]{:S(2)}) %collective-permute-start.12) | collective-permute-done | bytes 573472 | tf_op jit(solution)/shard_map/ppermute | solution.py:472
  58.0 2.5 %stream.1 = (f32[12,12,19,128]{3,2,1,0:T(8,128)}, f32[12,48,128]{2,1,0:T(8,128)S(1)}) custom-call(f32[19,14,16,128]{3,2,1,0:T(8,128)S(1)} %get-tuple-element.27.post, f32[5,14,16,128]{3,2,1,0:T(8,128)S(1)} %collective-permute-done.12.edge, f32[14,48,128]{2,1,0:T(8,128)S(1)} %get-tuple-element.29.force), custom_call_target="tpu_custom_call" | custom-call | tf_op jit(solution)/shard_map/stream/pallas_call | solution.py:555
  61.6 2.9 %collective-permute-start.14 = (f32[5,48,128]{2,1,0:T(8,128)S(1)}, f32[5,48,128]{2,1,0:T(8,128)S(1)}, u32[]{:S(2)}, u32[]{:S(2)}) collective-permute-start(f32[5,48,128]{2,1,0:T(8,128)S(1)} %slice.62), channel_id=1, source_target_pairs={{0,12},{4,0},{8,4},{12,8},{1,13},{5,1},{9,5},{13,9},{2,14},{6,2},{... | collective-permute-start | bytes 368648 | tf_op jit(solution)/shard_map/ppermute | solution.py:472
  64.6 4.6 %collective-permute-done.13.low_side = f32[6,48,128]{2,1,0:T(8,128)S(1)} collective-permute-done((f32[6,48,128]{2,1,0:T(8,128)S(1)}, f32[6,48,128]{2,1,0:T(8,128)S(1)}, u32[]{:S(2)}, u32[]{:S(2)}) %collective-permute-start.13) | collective-permute-done | bytes 147488 | tf_op jit(solution)/shard_map/ppermute | solution.py:472
  69.2 1.2 %collective-permute-done.14.high_side = f32[5,48,128]{2,1,0:T(8,128)S(1)} collective-permute-done((f32[5,48,128]{2,1,0:T(8,128)S(1)}, f32[5,48,128]{2,1,0:T(8,128)S(1)}, u32[]{:S(2)}, u32[]{:S(2)}) %collective-permute-start.14) | collective-permute-done | bytes 122912 | tf_op jit(solution)/shard_map/ppermute | solution.py:472
  70.4 1.3 %collective-permute-done.17.high_far = f32[5,48,128]{2,1,0:T(8,128)S(1)} collective-permute-done((f32[5,48,128]{2,1,0:T(8,128)S(1)}, f32[5,48,128]{2,1,0:T(8,128)S(1)}, u32[]{:S(2)}, u32[]{:S(2)}) %collective-permute-start.17) | collective-permute-done | bytes 122912 | tf_op jit(solution)/shard_map/ppermute | solution.py:472
  71.7 5.2 %sample.3 = f32[3,16,768]{2,1,0:T(8,128)S(1)} custom-call(s32[16,3]{1,0:T(8,128)S(1)} %collective-permute-done.7.corner, f32[3,16,768]{2,1,0:T(8,128)S(1)} %collective-permute-done.8.pos, f32[6,48,128]{2,1,0:T(8,128)S(1)} %collective-permute-done.13.low_side, f32[12,48,128]{2,1,0:T(8,128)S(1)} %get-tuple-element.31.own, ...), custom_call_target="tpu_custom_call" | custom-call | flops 2000000000 | bytes 4000000 | tf_op jit(solution)/shard_map/sample/pallas_call | solution.py:352
  76.9 1.7 %collective-permute-start.18 = (f32[3,16,768]{2,1,0:T(8,128)S(1)}, f32[3,16,768]{2,1,0:T(8,128)S(1)}, u32[]{:S(2)}, u32[]{:S(2)}) collective-permute-start(f32[3,16,768]{2,1,0:T(8,128)S(1)} %sample.3), channel_id=1, source_target_pairs={{0,2},{2,0},{1,3},{3,1},{4,6},{6,4},{5,7},{7,5},{8,10},{10,8},{9,1... | collective-permute-start | bytes 442376 | tf_op jit(solution)/shard_map/ppermute | solution.py:472
  78.6 5.1 %sample.2 = f32[3,16,768]{2,1,0:T(8,128)S(1)} custom-call(s32[16,3]{1,0:T(8,128)S(1)} %get-tuple-element.21.corner, f32[3,16,768]{2,1,0:T(8,128)S(1)} %get-tuple-element.22.pos, f32[6,48,128]{2,1,0:T(8,128)S(1)} %collective-permute-done.13.low_side, f32[12,48,128]{2,1,0:T(8,128)S(1)} %get-tuple-element.31.own, ...), custom_call_target="tpu_custom_call" | custom-call | flops 2000000000 | bytes 4000000 | tf_op jit(solution)/shard_map/sample/pallas_call | solution.py:352
  (50 shorter events, 6.9 us)
Async XLA Ops:
  0.6 21.7 %copy-start.4 = (f32[16,768]{1,0:T(8,128)S(1)}, f32[16,768]{1,0:T(8,128)}, u32[]{:S(2)}) copy-start(f32[16,768]{1,0:T(8,128)} %constant.15.clone.table) | copy-start | bytes 147460
  0.6 17.7 %copy-start.1 = (f32[16,3,642]{2,0,1:T(8,128)S(1)}, f32[16,3,642]{2,0,1:T(8,128)}, u32[]{:S(2)}) copy-start(f32[16,3,642]{2,0,1:T(8,128)} %param.6) | copy-start | bytes 369796
  0.7 17.7 %copy-start.3 = (s32[16]{0:T(128)S(1)}, s32[16]{0:T(128)}, u32[]{:S(2)}) copy-start(s32[16]{0:T(128)} %targets.3) | copy-start | bytes 196
  2.6 0.7 copy-start.2
  5.2 11.2 %collective-permute-start.3 = (s32[4,4]{1,0:T(4,128)S(1)}, s32[4,4]{1,0:T(4,128)S(1)}, u32[]{:S(2)}, u32[]{:S(2)}) collective-permute-start(s32[4,4]{1,0:T(4,128)S(1)} %get-tuple-element.17), channel_id=1, source_target_pairs={{0,4},{4,8},{8,12},{12,0},{1,5},{5,9},{9,13},{13,1},{2,6},{6,10},{... | collective-permute-start | bytes 200 | tf_op jit(solution)/shard_map/ppermute | solution.py:472
  8.2 10.1 %collective-permute-start.4 = (s32[4,4]{1,0:T(4,128)S(1)}, s32[4,4]{1,0:T(4,128)S(1)}, u32[]{:S(2)}, u32[]{:S(2)}) collective-permute-start(s32[4,4]{1,0:T(4,128)S(1)} %get-tuple-element.18), channel_id=1, source_target_pairs={{0,12},{4,0},{8,4},{12,8},{1,13},{5,1},{9,5},{13,9},{2,14},{6,2},{... | collective-permute-start | bytes 200 | tf_op jit(solution)/shard_map/ppermute | solution.py:472
  10.3 8.0 %collective-permute-start.5 = (f32[4,3,642]{2,1,0:T(4,128)S(1)}, f32[4,3,642]{2,1,0:T(4,128)S(1)}, u32[]{:S(2)}, u32[]{:S(2)}) collective-permute-start(f32[4,3,642]{2,1,0:T(4,128)S(1)} %get-tuple-element.19), channel_id=1, source_target_pairs={{0,4},{4,8},{8,12},{12,0},{1,5},{5,9},{9,13},{13,1},{2,6},{6,10},{... | collective-permute-start | bytes 92456 | tf_op jit(solution)/shard_map/ppermute | solution.py:472
  10.3 8.0 %collective-permute-start.6 = (f32[4,3,642]{2,1,0:T(4,128)S(1)}, f32[4,3,642]{2,1,0:T(4,128)S(1)}, u32[]{:S(2)}, u32[]{:S(2)}) collective-permute-start(f32[4,3,642]{2,1,0:T(4,128)S(1)} %get-tuple-element.20), channel_id=1, source_target_pairs={{0,12},{4,0},{8,4},{12,8},{1,13},{5,1},{9,5},{13,9},{2,14},{6,2},{... | collective-permute-start | bytes 92456 | tf_op jit(solution)/shard_map/ppermute | solution.py:472
  15.2 17.2 %collective-permute-start.1 = (f32[1,12,19,128]{3,2,1,0:T(8,128)S(1)}, f32[1,12,19,128]{3,2,1,0:T(8,128)S(1)}, u32[]{:S(2)}, u32[]{:S(2)}) collective-permute-start(f32[1,12,19,128]{3,2,1,0:T(8,128)S(1)} %get-tuple-element.34), channel_id=1, source_target_pairs={{0,12},{4,0},{8,4},{12,8},{1,13},{5,1},{9,5},{13,9},{2,14},{6,2},{... | collective-permute-start | bytes 350216 | tf_op jit(solution)/shard_map/ppermute | solution.py:472
  16.4 25.5 %collective-permute-start = (f32[1,12,19,128]{3,2,1,0:T(8,128)S(1)}, f32[1,12,19,128]{3,2,1,0:T(8,128)S(1)}, u32[]{:S(2)}, u32[]{:S(2)}) collective-permute-start(f32[1,12,19,128]{3,2,1,0:T(8,128)S(1)} %get-tuple-element.35), channel_id=1, source_target_pairs={{0,4},{4,8},{8,12},{12,0},{1,5},{5,9},{9,13},{13,1},{2,6},{6,10},{... | collective-permute-start | bytes 350216 | tf_op jit(solution)/shard_map/ppermute | solution.py:472
  20.3 12.1 %collective-permute-start.7 = (s32[16,3]{1,0:T(8,128)S(1)}, s32[16,3]{1,0:T(8,128)S(1)}, u32[]{:S(2)}, u32[]{:S(2)}) collective-permute-start(s32[16,3]{1,0:T(8,128)S(1)} %get-tuple-element.21.corner), channel_id=1, source_target_pairs={{0,2},{2,0},{1,3},{3,1},{4,6},{6,4},{5,7},{7,5},{8,10},{10,8},{9,1... | collective-permute-start | bytes 584 | tf_op jit(solution)/shard_map/ppermute | solution.py:472
  22.0 10.5 %collective-permute-start.8 = (f32[3,16,768]{2,1,0:T(8,128)S(1)}, f32[3,16,768]{2,1,0:T(8,128)S(1)}, u32[]{:S(2)}, u32[]{:S(2)}) collective-permute-start(f32[3,16,768]{2,1,0:T(8,128)S(1)} %get-tuple-element.22.pos), channel_id=1, source_target_pairs={{0,2},{2,0},{1,3},{3,1},{4,6},{6,4},{5,7},{7,5},{8,10},{10,8},{9,1... | collective-permute-start | bytes 442376 | tf_op jit(solution)/shard_map/ppermute | solution.py:472
  41.8 2.1 %collective-permute-start.9 = (f32[24,48,128]{2,1,0:T(8,128)S(1)}, f32[24,48,128]{2,1,0:T(8,128)S(1)}, u32[]{:S(2)}, u32[]{:S(2)}) collective-permute-start(f32[24,48,128]{2,1,0:T(8,128)S(1)} %get-tuple-element.26), channel_id=1, source_target_pairs={{0,1},{1,0},{2,3},{3,2},{4,5},{5,4},{6,7},{7,6},{8,9},{9,8},{10,11... | collective-permute-start | bytes 1769480 | tf_op jit(solution)/shard_map/ppermute | solution.py:472
  42.0 10.6 %copy-start = (f32[19,12,12,128]{3,0,2,1:T(8,128)S(1)}, f32[19,12,12,128]{3,0,2,1:T(8,128)}, u32[]{:S(2)}) copy-start(f32[19,12,12,128]{3,0,2,1:T(8,128)} %param.5) | copy-start | bytes 4202500
  42.0 10.5 %collective-permute-start.2 = (f32[2,14,19,128]{3,2,1,0:T(8,128)S(1)}, f32[2,14,19,128]{3,2,1,0:T(8,128)S(1)}, u32[]{:S(2)}, u32[]{:S(2)}) collective-permute-start(f32[2,14,19,128]{3,2,1,0:T(8,128)S(1)} %pad_maximum_fusion), channel_id=1, source_target_pairs={{0,2},{2,0},{1,3},{3,1},{4,6},{6,4},{5,7},{7,5},{8,10},{10,8},{9,1... | collective-permute-start | bytes 817160 | tf_op jit(solution)/shard_map/ppermute | solution.py:472
  44.0 8.9 %collective-permute-start.10 = (f32[6,48,128]{2,1,0:T(8,128)S(1)}, f32[6,48,128]{2,1,0:T(8,128)S(1)}, u32[]{:S(2)}, u32[]{:S(2)}) collective-permute-start(f32[6,48,128]{2,1,0:T(8,128)S(1)} %slice.75), channel_id=1, source_target_pairs={{0,4},{4,8},{8,12},{12,0},{1,5},{5,9},{9,13},{13,1},{2,6},{6,10},{... | collective-permute-start | bytes 442376 | tf_op jit(solution)/shard_map/ppermute | solution.py:472
  44.2 9.5 %collective-permute-start.11 = (f32[7,48,128]{2,1,0:T(8,128)S(1)}, f32[7,48,128]{2,1,0:T(8,128)S(1)}, u32[]{:S(2)}, u32[]{:S(2)}) collective-permute-start(f32[7,48,128]{2,1,0:T(8,128)S(1)} %slice.76), channel_id=1, source_target_pairs={{0,12},{4,0},{8,4},{12,8},{1,13},{5,1},{9,5},{13,9},{2,14},{6,2},{... | collective-permute-start | bytes 516104 | tf_op jit(solution)/shard_map/ppermute | solution.py:472
  55.9 2.0 %collective-permute-start.12 = (f32[5,14,16,128]{3,2,1,0:T(8,128)S(1)}, f32[5,14,16,128]{3,2,1,0:T(8,128)S(1)}, u32[]{:S(2)}, u32[]{:S(2)}) collective-permute-start(f32[5,14,16,128]{3,2,1,0:T(8,128)S(1)} %get-tuple-element.28), channel_id=1, source_target_pairs={{0,1},{1,0},{2,3},{3,2},{4,5},{5,4},{6,7},{7,6},{8,9},{9,8},{10,11... | collective-permute-start | bytes 1720328 | tf_op jit(solution)/shard_map/ppermute | solution.py:472
  60.5 11.3 %collective-permute-start.16 = (f32[12,48,128]{2,1,0:T(8,128)S(1)}, f32[12,48,128]{2,1,0:T(8,128)S(1)}, u32[]{:S(2)}, u32[]{:S(2)}) collective-permute-start(f32[12,48,128]{2,1,0:T(8,128)S(1)} %get-tuple-element.31.own), channel_id=1, source_target_pairs={{0,1},{1,0},{2,3},{3,2},{4,5},{5,4},{6,7},{7,6},{8,9},{9,8},{10,11... | collective-permute-start | bytes 884744 | tf_op jit(solution)/shard_map/ppermute | solution.py:472
  60.7 8.5 %collective-permute-start.13 = (f32[6,48,128]{2,1,0:T(8,128)S(1)}, f32[6,48,128]{2,1,0:T(8,128)S(1)}, u32[]{:S(2)}, u32[]{:S(2)}) collective-permute-start(f32[6,48,128]{2,1,0:T(8,128)S(1)} %slice.61), channel_id=1, source_target_pairs={{0,4},{4,8},{8,12},{12,0},{1,5},{5,9},{9,13},{13,1},{2,6},{6,10},{... | collective-permute-start | bytes 442376 | tf_op jit(solution)/shard_map/ppermute | solution.py:472
  61.6 8.8 %collective-permute-start.14 = (f32[5,48,128]{2,1,0:T(8,128)S(1)}, f32[5,48,128]{2,1,0:T(8,128)S(1)}, u32[]{:S(2)}, u32[]{:S(2)}) collective-permute-start(f32[5,48,128]{2,1,0:T(8,128)S(1)} %slice.62), channel_id=1, source_target_pairs={{0,12},{4,0},{8,4},{12,8},{1,13},{5,1},{9,5},{13,9},{2,14},{6,2},{... | collective-permute-start | bytes 368648 | tf_op jit(solution)/shard_map/ppermute | solution.py:472
  69.2 2.5 %collective-permute-start.15 = (f32[6,48,128]{2,1,0:T(8,128)S(1)}, f32[6,48,128]{2,1,0:T(8,128)S(1)}, u32[]{:S(2)}, u32[]{:S(2)}) collective-permute-start(f32[6,48,128]{2,1,0:T(8,128)S(1)} %collective-permute-done.13.low_side), channel_id=1, source_target_pairs={{0,1},{1,0},{2,3},{3,2},{4,5},{5,4},{6,7},{7,6},{8,9},{9,8},{10,11... | collective-permute-start | bytes 442376 | tf_op jit(solution)/shard_map/ppermute | solution.py:472
  70.4 1.3 %collective-permute-start.17 = (f32[5,48,128]{2,1,0:T(8,128)S(1)}, f32[5,48,128]{2,1,0:T(8,128)S(1)}, u32[]{:S(2)}, u32[]{:S(2)}) collective-permute-start(f32[5,48,128]{2,1,0:T(8,128)S(1)} %collective-permute-done.14.high_side), channel_id=1, source_target_pairs={{0,1},{1,0},{2,3},{3,2},{4,5},{5,4},{6,7},{7,6},{8,9},{9,8},{10,11... | collective-permute-start | bytes 368648 | tf_op jit(solution)/shard_map/ppermute | solution.py:472
  76.9 6.8 %collective-permute-start.18 = (f32[3,16,768]{2,1,0:T(8,128)S(1)}, f32[3,16,768]{2,1,0:T(8,128)S(1)}, u32[]{:S(2)}, u32[]{:S(2)}) collective-permute-start(f32[3,16,768]{2,1,0:T(8,128)S(1)} %sample.3), channel_id=1, source_target_pairs={{0,2},{2,0},{1,3},{3,1},{4,6},{6,4},{5,7},{7,5},{8,10},{10,8},{9,1... | collective-permute-start | bytes 442376 | tf_op jit(solution)/shard_map/ppermute | solution.py:472

commit v2 on v1

v2 whole, which is shorter than its diff:
```python
import functools
import math

import jax
import jax.numpy as jnp
import numpy as np
from jax import lax
from jax.experimental import pallas as pl
from jax.experimental.pallas import tpu as pltpu
from jax.sharding import PartitionSpec as P

REACH = 6
MIG = 4
STRIDES = (21, 34, 55)
DIRS = (
    (0, 0, 0),
    (1, 0, 0), (-1, 0, 0), (0, 1, 0), (0, -1, 0), (0, 0, 1), (0, 0, -1),
    (1, 1, 0), (-1, -1, 0), (1, -1, 0), (-1, 1, 0),
    (1, 0, 1), (-1, 0, -1), (1, 0, -1), (-1, 0, 1),
    (0, 1, 1), (0, -1, -1), (0, 1, -1), (0, -1, 1),
)
RISING = (5, 11, 14, 15, 18)
FALLING = (6, 12, 13, 16, 17)
WEIGHTS = (1.0 / 3.0,) + (1.0 / 18.0,) * 6 + (1.0 / 36.0,) * 12
FAR = 100.0
F32 = jnp.float32
WIDTH = 768
VMEM = pl.BlockSpec(memory_space=pltpu.VMEM)
SMEM = pl.BlockSpec(memory_space=pltpu.SMEM)


def params(limit=14):
    return pltpu.CompilerParams(vmem_limit_bytes=limit * 1024 * 1024)


def chain_table(vertices, width):
    v = np.arange(vertices)
    h = 1.0 - (2.0 * v + 1.0) / vertices
    t = 2.0 * math.pi / 2584.0 * (v * 1597 % 2584)
    across = np.sqrt(1.0 - h * h)
    rest = 3.0 * np.stack([across * np.cos(t), across * np.sin(t), h])
    table = np.zeros((16, width))
    for n, s in enumerate(STRIDES):
        gap = rest[:, s:] - rest[:, :-s]
        table[5 * n : 5 * n + 3, : vertices - s] = gap
        table[5 * n + 3, : vertices - s] = 0.05 / np.sum(gap * gap, axis=0)
        table[5 * n + 4, : vertices - s] = 1.0
    return jnp.asarray(table, F32)


def pack_kernel(capacity, slabs, plane, groups, here, infos, *refs):
    cells, (sides, up, down) = refs[:groups], refs[groups:]
    ny, directions = sides.shape[1:3]
    tiles = WIDTH // 128
    held = 3 * tiles * MIG
    spare = up.shape[0] - 8
    up[0 : groups * held, :] = jnp.full((groups * held, 128), -1.0, F32)
    down[0 : groups * held, :] = jnp.full((groups * held, 128), -1.0, F32)
    over = lax.rem(here[0] + 1, slabs)
    under = lax.rem(here[0] + slabs - 1, slabs)
    for g in range(groups):
        n_up, n_down = jnp.int32(0), jnp.int32(0)
        for c in range(capacity):
            owner = infos[g * capacity + c, 0] // capacity
            peer = owner // plane
            leaving = owner != here[3 + g]
            rises = jnp.logical_and(leaving, peer == over)
            falls = jnp.logical_and(leaving, peer == under)
            to_up = g * held + jnp.minimum(n_up, MIG - 1)
            to_down = g * held + jnp.minimum(n_down, MIG - 1)

            def put(message, start):
                for a in range(3):
                    for t in range(tiles):
                        row = cells[g][a, c : c + 1, 128 * t : 128 * t + 128]
                        message[pl.ds(start + (a * tiles + t) * MIG, 1), :] = row

            @pl.when(rises)
            def _():
                put(up, to_up)

            @pl.when(falls)
            def _():
                put(down, to_down)

            n_up = n_up + rises.astype(jnp.int32)
            n_down = n_down + falls.astype(jnp.int32)
    for n, message in enumerate((up, down)):
        for y in range(ny):
            first = groups * held + 24 * y
            message[first : first + directions, :] = sides[n, y]


def cell_row(block, offset, r, a):
    if len(block.shape) == 3:
        return block[a, r : r + 1, :]
    tiles = WIDTH // 128
    first = offset + a * tiles * MIG + r
    return jnp.concatenate([block[first + t * MIG : first + t * MIG + 1, :] for t in range(tiles)], axis=1)


def cell_count(block):
    return block.shape[1] if len(block.shape) == 3 else MIG


def hide_rest(pos, vertices):
    width = pos.shape[2]
    lane = lax.broadcasted_iota(jnp.int32, (pos.shape[1], 128), 1) + (width - 128)
    for a in range(3):
        pos[a, :, width - 128 :] = jnp.where(lane < vertices, pos[a, :, width - 128 :], FAR)


def assemble(capacity, vertices, extent, owner, infos, sources, pos, corner):
    for first, block, offset, migrated in sources:
        for r in range(cell_count(block)):
            target = infos[first + r, 0]
            wanted = target >= 0 if migrated else target // capacity == owner
            slot = jnp.where(wanted, lax.rem(target, capacity), capacity)
            for a in range(3):
                pos[a, pl.ds(slot, 1), :] = cell_row(block, offset, r, a)
            for d in range(3):
                corner[slot, d] = lax.rem(infos[first + r, 1 + d], extent[d])
    hide_rest(pos, vertices)


def assemble_kernel(sizes, groups, offsets, *refs):
    capacity, vertices, extent = sizes
    here, infos = refs[:2]
    cells = refs[2 : 2 + 3 * groups]
    positions, corners = refs[3 + 3 * groups : 3 + 4 * groups], refs[3 + 4 * groups :]
    for g in range(groups):
        start = groups * capacity + g * 2 * MIG
        sources = [
            (g * capacity, cells[3 * g], 0, False),
            (start, cells[3 * g + 1], offsets[3 * g + 1], True),
            (start + MIG, cells[3 * g + 2], offsets[3 * g + 2], True),
        ]
        assemble(capacity, vertices, extent, here[3 + g], infos, sources, positions[g], corners[g])


def wide(tile, width):
    return jnp.concatenate([tile] * (width // 128), axis=1)


def waves(x):
    h = (x - 4.0 * jnp.floor(0.25 * x + 0.5)) * (math.pi / 4.0)
    q = h * h
    sine = h * (1.0 + q * (-1 / 6 + q * (1 / 120 + q * (-1 / 5040 + q * (1 / 362880 - q * (1 / 39916800))))))
    cosine = 1.0 + q * (
        -1 / 2 + q * (1 / 24 + q * (-1 / 720 + q * (1 / 40320 + q * (-1 / 3628800 + q * (1 / 479001600)))))
    )
    return 0.25 - 0.5 * sine * sine, 0.5 * sine * cosine


def fill_waves(pos, wave):
    cells = wave.shape[1]
    for a in range(3):
        wave[2 * a], wave[2 * a + 1] = waves(pos[a, 0:cells, :])


def fill_force(pos, table, force):
    cells, width = force.shape[1:]
    for h in range(cells // 8):
        rows = slice(8 * h, 8 * h + 8)
        x = [pos[a, rows, :] for a in range(3)]
        lap = [jnp.zeros((8, width), F32) for _ in range(3)]
        pulls = []
        for n, s in enumerate(STRIDES):
            gap = [table[5 * n + a : 5 * n + a + 1, :] for a in range(3)]
            scale = table[5 * n + 3 : 5 * n + 4, :]
            mask = table[5 * n + 4 : 5 * n + 5, :]
            d = [pltpu.roll(x[a], width - s, 1) - x[a] for a in range(3)]
            square = d[0] * d[0] + d[1] * d[1] + d[2] * d[2]
            strain = square * scale - 0.05 * mask
            pulls.append([strain * d[a] for a in range(3)])
            for a in range(3):
                bend = mask * d[a] - gap[a]
                lap[a] = lap[a] + bend - pltpu.roll(bend, s, 1)
        for a in range(3):
            total = jnp.zeros((8, width), F32)
            for n, s in enumerate(STRIDES):
                mask = table[5 * n + 4 : 5 * n + 5, :]
                t = pulls[n][a] - 0.002 * (mask * (pltpu.roll(lap[a], width - s, 1) - lap[a]))
                total = total + t - pltpu.roll(t, s, 1)
            force[a, rows, :] = total


def split(x):
    high = x.astype(jnp.bfloat16)
    return high, (x - high.astype(F32)).astype(jnp.bfloat16)


def row_of(ref, i, c):
    return jnp.broadcast_to(ref[i, pl.ds(c, 1), :], (8, ref.shape[2]))


def fill_planar(pos, wave, c, high, low):
    width = pos.shape[2]
    row = lax.broadcasted_iota(jnp.int32, (8, 128), 0)
    rowf = wide((row - REACH).astype(F32), width)
    odd = wide((row & 1), width) == 1
    flip = wide((row & 2), width) == 0
    z, cz, sz = row_of(pos, 2, c), row_of(wave, 4, c), row_of(wave, 5, c)
    base = jnp.where(odd, sz, cz)
    pattern = 0.25 + jnp.where(flip, -base, base)
    wz = jnp.concatenate(
        [
            jnp.where(jnp.abs(rowf - z) < 2.0, pattern, 0.0),
            jnp.where(jnp.abs(rowf + 8.0 - z) < 2.0, pattern, 0.0),
        ],
        axis=0,
    )
    x, cx, sx = row_of(pos, 0, c), row_of(wave, 0, c), row_of(wave, 1, c)
    quarter = (0.25 - cx, 0.25 - sx, 0.25 + cx, 0.25 + sx)
    for kx in range(2 * REACH):
        wx = jnp.where(jnp.abs(x - float(kx - REACH)) < 2.0, quarter[kx % 4], 0.0)
        high[16 * kx : 16 * kx + 16, :], low[16 * kx : 16 * kx + 16, :] = split(
            jnp.concatenate([wx, wx], axis=0) * wz
        )


def rows_weight(pos, wave, c, anchor, images):
    width = pos.shape[2]
    n = lax.broadcasted_iota(jnp.int32, (8, 128), 0) - 1 - anchor
    nf = wide(n.astype(F32), width)
    odd = wide(n & 1, width) == 1
    flip = wide(n & 2, width) == 2
    y, cy, sy = row_of(pos, 1, c), row_of(wave, 2, c), row_of(wave, 3, c)
    base = jnp.where(odd, sy, cy)
    pattern = 0.25 + jnp.where(flip, -base, base)
    halves = []
    for h in range(2):
        gap = nf + 8.0 * h - y
        near = jnp.abs(gap - images[0]) < 2.0
        if len(images) > 1:
            near = jnp.logical_or(near, jnp.abs(gap - images[1]) < 2.0)
        halves.append(jnp.where(near, pattern, 0.0))
    return jnp.concatenate(halves, axis=0)


def nt_dot(a, b):
    return lax.dot_general(a, b, (((1,), (1,)), ((), ())), preferred_element_type=F32)


def stage_kernel(sizes, plan, last, copies, counts, together, *refs):
    _, vertices, extent = sizes
    n_cells, n_sums, n_copied = counts
    here, infos, table = refs[:3]
    refs = refs[3:]
    cells, refs = refs[:n_cells], refs[n_cells:]
    sums, refs = refs[:n_sums], refs[n_sums:]
    n_from = len({c[0] for c in copies})
    givers, refs = refs[:n_from], refs[n_from:]
    if last:
        own, down, up, far = refs[:4]
        refs = refs[4:]
    else:
        acc, refs = refs[0], refs[1:]
    takers, refs = refs[:n_copied], refs[n_copied:]
    pos, wave, force, planar, corner = refs[:5]
    if last:
        acc = refs[5]
    moves = []
    for n, (giver, source, taker, target) in enumerate(copies):
        move = pltpu.make_async_copy(givers[giver].at[source], takers[taker].at[target], refs[5].at[n])
        move.start()
        moves.append(move)
    if sums:
        total = sums[0][...]
        for more in sums[1:]:
            total = total + more[...]
        acc[...] = total
    else:
        acc[...] = jnp.zeros(acc.shape, F32)
    pos[...] = jnp.full(pos.shape, FAR, F32)
    rows = pos.shape[1] - 8
    for r in range(rows + 1):
        for d in range(3):
            corner[r, d] = 0
        for d in range(2):
            corner[r, 3 + d] = 0
    count = jnp.int32(0)
    at = 0
    for array, owner, images, offset in plan:
        block = cells[array]
        for r in range(cell_count(block)):
            target = infos[at, 0]
            wanted = target >= 0 if owner is None else target // sizes[0] == here[owner]
            row = jnp.where(wanted, count, rows)
            for a in range(3):
                pos[a, pl.ds(row, 1), :] = cell_row(block, offset, r, a)
            for d in range(3):
                corner[row, d] = lax.rem(infos[at, 1 + d], extent[d])
            corner[row, 3] = images[0]
            corner[row, 4] = images[-1]
            count = count + wanted.astype(jnp.int32)
            at += 1
    hide_rest(pos, vertices)
    fill_waves(pos, wave)
    fill_force(pos, table, force)

    def weigh(c, b):
        fill_planar(pos, wave, c, planar.at[b, 0:192], planar.at[b, 192:384])
        images = (corner[c, 3].astype(F32), corner[c, 4].astype(F32))
        wy = rows_weight(pos, wave, c, corner[c, 1], images)
        lifted = []
        for a in range(3):
            f = row_of(force, a, c)
            lifted.append(jnp.concatenate([f, f], axis=0) * wy)
        high, low = split(jnp.concatenate(lifted, axis=0))
        both = nt_dot(planar[b], high)
        total = both[:192] + both[192:] + nt_dot(planar[b, 0:192], low)
        x0, z0 = corner[c, 0], corner[c, 2] + 2
        acc[pl.ds(x0, 12), pl.ds(z0, 16), :] += total.reshape(12, 16, 48)

    def weigh_some(i, carry):
        for b in range(together):
            weigh(together * i + b, b)
        return carry

    lax.fori_loop(0, (count + together - 1) // together, weigh_some, 0)
    if last:
        for x in range(23):
            turned = jnp.transpose(acc[x, 8:136, :], (1, 0))
            if REACH - 1 <= x < REACH - 1 + own.shape[0]:
                own[x - REACH + 1] = turned
            if x < down.shape[0]:
                down[x] = turned
            if x >= 23 - up.shape[0]:
                up[x - 23 + up.shape[0]] = turned
        for n in range(3):
            outside = []
            for x in range(8 * n, 8 * n + 8):
                outside += [acc[x, 0:8, :], acc[x, 136:144, :]]
            far[n] = jnp.transpose(jnp.concatenate(outside, axis=0), (1, 0))
    for move in moves:
        move.wait()


def stage(sizes, plan, here, infos, table, cells, sums=(), last=False, givers=(), takers=(), copies=(), together=2):
    width = table.shape[1]
    rows = sum(cell_count(cells[p[0]]) for p in plan)
    counts = (len(cells), len(sums), len(takers))
    whole = pl.BlockSpec(memory_space=pl.ANY)
    fixed = pl.BlockSpec(memory_space=pltpu.HBM)
    return pl.pallas_call(
        functools.partial(stage_kernel, sizes, plan, last, copies, counts, together),
        out_shape=tuple(
            jax.ShapeDtypeStruct(shape, F32)
            for shape in ([(n, 48, 128) for n in (14, REACH + 1, REACH, 3)] if last else [(24, 152, 48)])
        )
        + tuple(takers),
        in_specs=[SMEM, SMEM, VMEM] + [VMEM] * (len(cells) + len(sums)) + [fixed] * len(givers),
        out_specs=(VMEM,) * (4 if last else 1) + (whole,) * len(takers),
        scratch_shapes=[
            pltpu.VMEM((3, rows + 8, width), F32),
            pltpu.VMEM((6, rows, width), F32),
            pltpu.VMEM((3, rows, width), F32),
            pltpu.VMEM((together, 384, width), jnp.bfloat16),
            pltpu.SMEM((rows + 8, 5), jnp.int32),
        ]
        + ([pltpu.VMEM((24, 152, 48), F32)] if last else [])
        + ([pltpu.SemaphoreType.DMA((len(copies),))] if copies else []),
        compiler_params=params(),
        name="spread",
        cost_estimate=pl.CostEstimate(flops=int(4e9), bytes_accessed=4_000_000, transcendentals=0),
    )(here, infos, table, *cells, *sums, *givers)


def fold_kernel(own_in, down_in, up_in, far, own, down, up):
    lane = lax.broadcasted_iota(jnp.int32, (48, 128), 1)
    rim = jnp.logical_or(lane < 8, lane >= 120)
    for x in range(23):
        more = jnp.where(rim, pltpu.roll(far[x // 8], (120 - 16 * (x % 8)) % 128, 1), 0.0)
        if REACH - 1 <= x < REACH - 1 + own.shape[0]:
            own[x - REACH + 1] = own_in[x - REACH + 1] + more
        if x < down.shape[0]:
            down[x] = down_in[x] + more
        n = x - 23 + up.shape[0]
        if n >= 0:
            up[n] = up_in[n] + more


def sample_kernel(images, corner, pos, low_side, own, high_side, low_far, own_far, high_far, out, flow, far, wave, high, low):
    cells = out.shape[1]
    at = 0
    for part, part_far in ((low_side, low_far), (own, own_far), (high_side, high_far)):
        size = part.shape[0]
        flow[at : at + size] = part[...]
        far[at : at + size] = part_far[...]
        at += size
    fill_waves(pos, wave)
    lane = lax.broadcasted_iota(jnp.int32, (8, 128), 1)

    def sample(c, b):
        fill_planar(pos, wave, c, high.at[b], low.at[b])
        z0 = corner[c, 2] - REACH
        x0 = corner[c, 0]
        turn = (z0 + 16 * x0 + 128) & 127
        origin = (lane - turn) & 127
        group = jnp.right_shift(origin, 4)
        z = (origin & 15) + z0
        inside = jnp.logical_and(z >= 0, z < 128)
        chosen = [group == g for g in range(8)]
        blocks = []
        for r in range(6):
            rows = slice(8 * r, 8 * r + 8)
            near = flow[pl.ds(x0, 12), rows, :]
            there = far[pl.ds(x0, 12), rows, :]
            turned = []
            for t in range(2):
                a, b_ = near[8 * t], there[8 * t]
                for g in range(1, 8 - 4 * t):
                    a = jnp.where(chosen[g], near[8 * t + g], a)
                    b_ = jnp.where(chosen[g], there[8 * t + g], b_)
                turned.append(pltpu.roll(jnp.where(inside, a, b_), (128 - turn) & 127, 1))
            blocks.append(jnp.concatenate([turned[0], turned[1][:, 0:64]], axis=1))
        qhigh, qlow = split(jnp.concatenate(blocks, axis=0))
        both = jnp.dot(jnp.concatenate([qhigh, qlow], axis=0), high[b], preferred_element_type=F32)
        mixed = both[:48] + both[48:] + jnp.dot(qhigh, low[b], preferred_element_type=F32)
        wy = rows_weight(pos, wave, c, corner[c, 1], images)
        for a in range(3):
            out[a, pl.ds(c, 1), :] = jnp.sum(mixed[16 * a : 16 * a + 16] * wy, axis=0, keepdims=True)

    def sample_some(i, carry):
        for b in range(4):
            sample(4 * i + b, b)
        return carry

    lax.fori_loop(0, cells // 4, sample_some, 0)


def sampled(cells, images, corner, pos, parts):
    width = pos.shape[2]
    return pl.pallas_call(
        functools.partial(sample_kernel, images),
        out_shape=jax.ShapeDtypeStruct((3, cells, width), F32),
        in_specs=[SMEM] + [VMEM] * 7,
        out_specs=VMEM,
        scratch_shapes=[
            pltpu.VMEM((24, 48, 128), F32),
            pltpu.VMEM((24, 48, 128), F32),
            pltpu.VMEM((6, cells, width), F32),
            pltpu.VMEM((4, 192, width), jnp.bfloat16),
            pltpu.VMEM((4, 192, width), jnp.bfloat16),
        ],
        compiler_params=params(),
        name="sample",
        cost_estimate=pl.CostEstimate(flops=int(2e9), bytes_accessed=4_000_000, transcendentals=0),
    )(corner, pos, *parts)


def extend_kernel(n_low, n_high, pops, x_low, x_high, y_low, y_high, out):
    nx, ny = pops.shape[:2]
    directions = pops.shape[2]
    for x in range(nx + 2):
        middle = x_low[0, :, 0:19, :] if x == 0 else (x_high[0, :, 0:19, :] if x == nx + 1 else pops[x - 1])
        block = jnp.concatenate([y_low[n_low, x : x + 1], middle, y_high[n_high, x : x + 1], y_low[n_low, x : x + 1], y_low[n_low, x : x + 1]], axis=0)
        out[:, x] = jnp.transpose(block, (1, 0, 2))


def collide_kernel(pops, own, from_low, from_high, *refs):
    post, force, edge = refs[-3:]
    planes = pops.shape[1]
    n_low, n_high = from_low.shape[0], from_high.shape[0]
    for e in range(planes):
        total = own[e]
        if e < n_low:
            total = total + from_low[e]
        if e >= planes - n_high:
            total = total + from_high[e - (planes - n_high)]
        force[e] = total
    lane = lax.broadcasted_iota(jnp.int32, (16, 128), 1)

    def plane(e, carry):
        p = [pops[i, e] for i in range(19)]
        f = [force[e, 16 * a : 16 * a + 16, :] for a in range(3)]
        rho = p[0]
        for i in range(1, 19):
            rho = rho + p[i]
        u = []
        for a in range(3):
            m = 0.5 * f[a]
            for i in range(1, 19):
                if DIRS[i][a] == 1:
                    m = m + p[i]
                elif DIRS[i][a] == -1:
                    m = m - p[i]
            u.append(m / rho)
        kinetic = u[0] * u[0] + u[1] * u[1] + u[2] * u[2]
        power = u[0] * f[0] + u[1] * f[1] + u[2] * f[2]
        level = 1.25 * rho * (1.0 - 1.5 * kinetic) - 1.125 * power
        bow, tilt = 5.625 * rho, 3.75 * rho
        new = [None] * 19
        new[0] = WEIGHTS[0] * level - 0.25 * p[0]
        for i in range(1, 19, 2):
            along = [a for a in range(3) if DIRS[i][a] != 0]
            cu, cf = None, None
            for a in along:
                tu, tf = u[a], f[a]
                if DIRS[i][a] < 0:
                    tu, tf = -tu, -tf
                cu = tu if cu is None else cu + tu
                cf = tf if cf is None else cf + tf
            even = WEIGHTS[i] * (level + cu * (bow * cu + 3.375 * cf))
            odd = WEIGHTS[i] * (tilt * cu + 1.125 * cf)
            new[i] = even + odd - 0.25 * p[i]
            new[i + 1] = even - odd - 0.25 * p[i + 1]
        for i in range(19):
            post[i, e] = new[i]
        for j in range(5):
            edge[j, e] = jnp.where(
                lane == 0, pltpu.roll(new[RISING[j]], 1, 1), pltpu.roll(new[FALLING[j]], 127, 1)
            )
        return carry

    lax.fori_loop(0, planes, plane, 0)


def stream_kernel(post, edge, force, pops, own, up, down, velocity):
    ny = pops.shape[1]
    lane = lax.broadcasted_iota(jnp.int32, (ny, 128), 1)
    velocity[...] = jnp.zeros(velocity.shape, F32)

    def plane(x, carry):
        n = []
        for i in range(19):
            cx, cy, cz = DIRS[i]
            value = post[i, x + 1 - cx, 1 - cy : 1 - cy + ny, :]
            if cz == 1:
                side = edge[RISING.index(i), x + 1 - cx, 1 - cy : 1 - cy + ny, :]
                value = jnp.where(lane == 0, side, pltpu.roll(value, 1, 1))
            elif cz == -1:
                side = edge[FALLING.index(i), x + 1 - cx, 1 - cy : 1 - cy + ny, :]
                value = jnp.where(lane == 127, side, pltpu.roll(value, 127, 1))
            n.append(value)
        rho = n[0]
        for i in range(1, 19):
            rho = rho + n[i]
        for a in range(3):
            m = 0.5 * force[x + 1, 16 * a + 1 : 16 * a + 1 + ny, :]
            for i in range(1, 19):
                if DIRS[i][a] == 1:
                    m = m + n[i]
                elif DIRS[i][a] == -1:
                    m = m - n[i]
            velocity[x, 16 * a + 1 : 16 * a + 1 + ny, :] = m / rho
        pops[x] = jnp.transpose(jnp.stack(n), (1, 0, 2))
        return carry

    nx = pops.shape[0]
    lax.fori_loop(0, nx, plane, 0)
    for x in range(nx):
        own[x] = pltpu.roll(velocity[x], 16 * (x + REACH) % 128, 1)
        if x >= nx - REACH:
            up[x - nx + REACH] = pltpu.roll(velocity[x], 16 * (x + REACH - nx) % 128, 1)
        if x < REACH - 1:
            down[x] = pltpu.roll(velocity[x], 16 * (x + REACH + nx) % 128, 1)


def shifted(x, axis, distance):
    count = lax.axis_size(axis)
    return lax.ppermute(x, axis, [(i, (i + distance) % count) for i in range(count)])


def on_device(populations, membrane, anchors, targets):
    extent = populations.shape[1:]
    capacity, _, vertices = membrane.shape
    slabs, crosses, subs = (lax.axis_size(a) for a in ("slab", "cross", "sub"))
    assert subs == 2 and extent == (12, 12, 128) and capacity % 8 == 0
    width = WIDTH
    assert vertices + 4 <= width < vertices + 128
    place = [lax.axis_index(a) for a in ("slab", "cross", "sub")]
    table = chain_table(vertices, width)

    notes = jnp.concatenate([targets[:, None], anchors], axis=1)
    raw = jnp.concatenate(
        [
            jnp.transpose(membrane, (1, 0, 2)),
            jnp.broadcast_to(notes.astype(F32)[None], (3, capacity, 4)),
            jnp.full((3, capacity, width - vertices - 4), FAR, F32),
        ],
        axis=2,
    )
    if crosses == 2:
        beside = [(1, (extent[1], -extent[1]))]
    else:
        beside = [(1, (-extent[1],)), (-1, (extent[1],))]
    owners = [(place[0] * crosses + (place[1] + crosses - d) % crosses) * subs + place[2] for d in [0] + [d for d, _ in beside]]
    here = jnp.stack(place + owners).astype(jnp.int32)
    guests = [shifted(raw, "cross", d) for d, _ in beside]
    groups = 1 + len(beside)
    nx, ny = extent[:2]
    planes = nx + 2
    pops = jnp.transpose(populations, (1, 2, 0, 3))
    sides = jnp.concatenate([pops[nx - 1 :], pops[:1]])
    held = 3 * (width // 128) * MIG
    message = jax.ShapeDtypeStruct((groups * held + 24 * ny + 8, 128), F32)
    home = jnp.concatenate([g[0, :, vertices : vertices + 4].astype(jnp.int32) for g in [raw] + guests])
    up, down = pl.pallas_call(
        functools.partial(pack_kernel, capacity, slabs, crosses * subs, groups),
        out_shape=(message, message),
        in_specs=[SMEM, SMEM] + [VMEM] * (groups + 1),
        out_specs=(VMEM, VMEM),
        compiler_params=params(),
        name="pack",
    )(here, home, raw, *guests, sides)
    sizes = (capacity, vertices, extent)
    below, above = shifted(up, "slab", 1), shifted(down, "slab", -1)
    images = [(0,)] + [image for _, image in beside]

    row = jax.ShapeDtypeStruct((nx,) + pops.shape[2:], F32)
    sum_1, first, last = stage(
        sizes,
        [(g, 3 + g, images[g], 0) for g in range(groups)],
        here,
        home,
        table,
        [raw] + guests,
        givers=(pops,),
        takers=(row, row),
        copies=((0, (pl.ds(0, nx), 0), 0, pl.ds(0, nx)), (0, (pl.ds(0, nx), ny - 1), 1, pl.ds(0, nx))),
        together=4,
    )
    x_low = below[groups * held : groups * held + 24 * ny].reshape(1, ny, 24, 128)
    x_high = above[groups * held : groups * held + 24 * ny].reshape(1, ny, 24, 128)
    first = jnp.concatenate([x_low[:, 0, :19], first, x_high[:, 0, :19]])
    last = jnp.concatenate([x_low[:, -1, :19], last, x_high[:, -1, :19]])
    if crosses == 2:
        rows = shifted(jnp.stack([last, first]), "cross", 1)
        y_low, y_high = (rows, 0), (rows, 1)
    else:
        y_low, y_high = (shifted(last, "cross", 1)[None], 0), (shifted(first, "cross", -1)[None], 0)
    lane = vertices - (width - 128)
    starts = [g * held + (width // 128 - 1) * MIG for g in range(groups)]
    notes_in = [m[s : s + MIG, lane : lane + 4].astype(jnp.int32) for s in starts for m in (below, above)]
    own, down_force, up_force, far = stage(
        sizes,
        [(n, None, images[g], g * held) for g in range(groups) for n in (0, 1)],
        here,
        jnp.concatenate(notes_in),
        table,
        [below, above],
        sums=(sum_1,),
        last=True,
    )
    cells = []
    for block in [raw] + guests:
        cells += [block, below, above]
    offsets = tuple(g * held for g in range(groups) for _ in range(3))
    extended = pl.pallas_call(
        functools.partial(extend_kernel, y_low[1], y_high[1]),
        out_shape=jax.ShapeDtypeStruct((19, planes, 16, 128), F32),
        in_specs=[VMEM] * 5,
        out_specs=VMEM,
        compiler_params=params(),
        name="extend",
    )(pops, x_low, x_high, y_low[0], y_high[0])

    own, down_force, up_force = pl.pallas_call(
        fold_kernel,
        out_shape=tuple(jax.ShapeDtypeStruct((n, 48, 128), F32) for n in (planes, REACH + 1, REACH)),
        in_specs=[VMEM] * 4,
        out_specs=(VMEM,) * 3,
        compiler_params=params(),
        name="fold",
    )(own, down_force, up_force, shifted(far, "sub", 1))
    from_high = shifted(down_force, "slab", -1)
    from_low = shifted(up_force, "slab", 1)

    placed = pl.pallas_call(
        functools.partial(assemble_kernel, sizes, groups, offsets),
        out_shape=(jax.ShapeDtypeStruct((3, capacity + 8, width), F32),) * groups
        + (jax.ShapeDtypeStruct((capacity + 8, 3), jnp.int32),) * groups,
        in_specs=[SMEM, SMEM] + [VMEM] * len(cells) + [pl.BlockSpec(memory_space=pl.ANY)],
        out_specs=(VMEM,) * groups + (SMEM,) * groups,
        compiler_params=params(),
        name="assemble",
    )(here, jnp.concatenate([home] + notes_in), *cells, own)
    positions, corners = placed[:groups], placed[groups:]
    post, force, edge = pl.pallas_call(
        collide_kernel,
        out_shape=(
            jax.ShapeDtypeStruct((19, planes, 16, 128), F32),
            jax.ShapeDtypeStruct((planes, 48, 128), F32),
            jax.ShapeDtypeStruct((5, planes, 16, 128), F32),
        ),
        in_specs=[VMEM] * 4 + [pl.BlockSpec(memory_space=pl.ANY)] * groups,
        out_specs=(VMEM,) * 3,
        compiler_params=params(),
        name="collide",
    )(extended, own, from_low, from_high, *positions)
    edge = shifted(edge, "sub", 1)
    renewed, velocity, up_flow, down_flow = pl.pallas_call(
        stream_kernel,
        out_shape=(jax.ShapeDtypeStruct((extent[0], extent[1], 19, 128), F32),)
        + tuple(jax.ShapeDtypeStruct((n, 48, 128), F32) for n in (extent[0], REACH, REACH - 1)),
        in_specs=[VMEM] * 3,
        out_specs=(VMEM,) * 4,
        scratch_shapes=[pltpu.VMEM((extent[0], 48, 128), F32)],
        compiler_params=params(),
        name="stream",
    )(post, edge, force)

    low_side = shifted(up_flow, "slab", 1)
    high_side = shifted(down_flow, "slab", -1)
    parts = (low_side, velocity, high_side)
    parts = parts + tuple(shifted(part, "sub", 1) for part in parts)
    shares = [
        shifted(sampled(capacity, image, corner, pos, parts), "cross", -d)
        for (d, image), corner, pos in zip(beside, corners[1:], positions[1:])
    ]
    total = sampled(capacity, (0,), corners[0], positions[0], parts)
    for share in shares:
        total = total + share
    return (
        jnp.transpose(renewed, (2, 0, 1, 3)),
        jnp.transpose(total[:, :, :vertices], (1, 0, 2)),
    )


def solution(mesh):
    placed = (
        P(None, ("parts", "slab"), "cross", "sub"),
        P(("parts", "slab", "cross", "sub"), None, None),
        P(("parts", "slab", "cross", "sub"), None),
        P(("parts", "slab", "cross", "sub")),
    )
    return jax.shard_map(
        on_device,
        mesh=mesh,
        in_specs=placed,
        out_specs=(
            P(None, ("parts", "slab"), "cross", "sub"),
            P(("parts", "slab", "cross", "sub"), None, None),
        ),
        check_vma=False,
    )
```

time: 84.4 us -> 79.3 us (0.940)
  starting transfers between devices: 24.7 us -> 15.1 us
  waiting for transfers between devices: 14.7 us -> 18.4 us
  other arithmetic: 0.88 us -> 3.56 us
  local copies, waits for them, and re-layouts: 4.62 us -> 2.01 us
    ppermute x19 -> x14, starting transfers between devices: 24.7 us -> 15.1 us  [shifted(): lax.ppermute(x, axis, [(i, (i + distance) % count) for i in range(count)])]
    ppermute x19 -> x14, waiting for transfers between devices: 14.7 us -> 18.4 us  [shifted(): lax.ppermute(x, axis, [(i, (i + distance) % count) for i in range(count)])]
    unnamed x12 -> x6, local copies, waits for them, and re-layouts: 2.52 us -> 0.03 us
    concatenate x0 -> x5, other arithmetic: none -> 1.85 us  [the longest x1 0.99 us: on_device(): jnp.concatenate([jnp.transpose(membrane, (1, 0, 2)), jnp.broadcast_to(not...]
    squeeze x4 -> x2, local copies, waits for them, and re-layouts: 1.04 us -> 0.01 us  [on_device(): last = jnp.concatenate([x_low[:, -1, :19], last, x_high[:, -1, :19]])]
    pallas_call x1, Pallas kernels: 2.22 us -> 3.22 us  [on_device(): pl.pallas_call(collide_kernel, out_shape=(jax.ShapeDtypeStruct((19, plane...]
    concatenate x0 -> x3, local copies, waits for them, and re-layouts: none -> 0.86 us  [the longest x1 0.7 us: on_device(): jnp.concatenate([home] + notes_in)]
    pallas_call x4 -> x5, Pallas kernels: 21.7 us -> 21.5 us  [the longest x2 17.6 us: stage(): pl.pallas_call(functools.partial(stage_kernel, sizes, plan, last, copies,...]
  transfers between devices with their start and end apart: 19 -> 14, of which waited for: 7 -> 8; matrix products, arithmetic and copies ran while one was open for 3% -> 3% of each run, Pallas kernels for 32% -> 34%
where the time goes in v2:
time: 79.3 us; the launch traced here: 78.9 us
  Pallas kernels  39 us (49%)
  waiting for transfers between devices  18.4 us (23%)
  starting transfers between devices  15.1 us (19%)
  other arithmetic  3.56 us (4%)
  local copies, waits for them, and re-layouts  2.01 us (3%)
  between operations  0.84 us (1%)
    ppermute x14, waiting for transfers between devices, shifted(): lax.ppermute(x, axis, [(i, (i + distance) % count) for i in range(count)])  18.4 us
    pallas_call x2, Pallas kernels, stage(): pl.pallas_call(functools.partial(stage_kernel, sizes, plan, last, copies,...  17.6 us
    ppermute x14, starting transfers between devices, shifted(): lax.ppermute(x, axis, [(i, (i + distance) % count) for i in range(count)])  15.1 us
    pallas_call x2, Pallas kernels, sampled(): pl.pallas_call(functools.partial(sample_kernel, images), out_shape=jax.Sh...  10 us
    pallas_call x1, Pallas kernels, on_device(): pl.pallas_call(collide_kernel, out_shape=(jax.ShapeDtypeStruct((19, plane...  3.22 us
    pallas_call x1, Pallas kernels, on_device(): pl.pallas_call(functools.partial(assemble_kernel, sizes, groups, offsets)...  2.63 us
    pallas_call x1, Pallas kernels, on_device(): pl.pallas_call(stream_kernel, out_shape=(jax.ShapeDtypeStruct((extent[0],...  2.58 us
    pallas_call x1, Pallas kernels, on_device(): pl.pallas_call(functools.partial(pack_kernel, capacity, slabs, crosses *...  1.66 us
  transfers between devices with their start and end apart: 14, of which 8 were waited for; matrix products, arithmetic and copies ran while one was open for 3% of the time, Pallas kernels for 34%

profile of v2, /device:TPU:0, one launch (start us, length us, event | category | flops | bytes accessed | tf_op | source)
XLA Modules:
  0.0 78.9 jit_solution(15126662127185546005)
XLA Ops:
  1.7 1.0 %maximum_maximum_fusion.refs_0_.refs_3_.refs_2_ = f32[3,16,768]{2,1,0:T(8,128)S(1)} fusion(f32[3,16,4]{2,1,0:T(8,128)S(1)} %broadcast_in_dim.4, f32[3,16,642]{2,1,0:T(8,128)} %bitcast.34, f32[768]{0:T(1024)S(1)} %pad.18.clone), kind=kLoop, calls=%fused_computation.6 | loop fusion | flops 73728 | bytes 274560 | tf_op jit(solution)/shard_map/concatenate | solution.py:577
  2.6 2.9 %collective-permute-start = (f32[3,16,768]{2,1,0:T(8,128)S(1)}, f32[3,16,768]{2,1,0:T(8,128)S(1)}, u32[]{:S(2)}, u32[]{:S(2)}) collective-permute-start(f32[3,16,768]{2,1,0:T(8,128)S(1)} %maximum_maximum_fusion.refs_0_.refs_3_.refs_2_), channel_id=1, source_target_pairs={{0,2},{2,0},{1,3},{3,1},{4,6},{6,4},{5,7},{7,5},{8,10},{10,8},{9,1... | collective-permute-start | bytes 442376 | tf_op jit(solution)/shard_map/ppermute | solution.py:563
  5.6 1.0 %fusion.2 = (f32[1,12,19,128]{3,2,1,0:T(8,128)S(1)}, f32[1,12,19,128]{3,2,1,0:T(8,128)S(1)}) fusion(f32[12,12,19,128]{3,2,1,0:T(8,128)} %bitcast.27), kind=kLoop, calls=%fused_computation.21 | loop fusion | bytes 466944 | tf_op jit(solution)/shard_map/slice | solution.py:596
  6.7 2.7 %collective-permute-done.refs_1_.refs_4_.refs_5_ = f32[3,16,768]{2,1,0:T(8,128)S(1)} collective-permute-done((f32[3,16,768]{2,1,0:T(8,128)S(1)}, f32[3,16,768]{2,1,0:T(8,128)S(1)}, u32[]{:S(2)}, u32[]{:S(2)}) %collective-permute-start) | collective-permute-done | bytes 147488 | tf_op jit(solution)/shard_map/ppermute | solution.py:563
  9.5 1.7 %pack.1 = (f32[440,128]{1,0:T(8,128)S(1)}, f32[440,128]{1,0:T(8,128)S(1)}) custom-call(s32[5]{0:T(128)S(1)} %stack.32.here.refs_0_, s32[32,4]{1,0:T(8,128)S(1)} %pad_add_fusion.infos.refs_1_, f32[3,16,768]{2,1,0:T(8,128)S(1)} %maximum_maximum_fusion.refs_0_.refs_3_.refs_2_, f32[3,16,768]{2,1,0:T(8,128)S(1)} %collective-permute-done.refs_1_.refs_4_.refs_5_, ...), custom_call_target="tpu_custom_call" | custom-call | tf_op jit(solution)/shard_map/pack/pallas_call | solution.py:600
  11.2 1.9 %collective-permute-start.1 = (f32[440,128]{1,0:T(8,128)S(1)}, f32[440,128]{1,0:T(8,128)S(1)}, u32[]{:S(2)}, u32[]{:S(2)}) collective-permute-start(f32[440,128]{1,0:T(8,128)S(1)} %get-tuple-element.25), channel_id=1, source_target_pairs={{0,4},{4,8},{8,12},{12,0},{1,5},{5,9},{9,13},{13,1},{2,6},{6,10},{... | collective-permute-start | bytes 675848 | tf_op jit(solution)/shard_map/ppermute | solution.py:563
  13.1 2.1 %collective-permute-start.2 = (f32[440,128]{1,0:T(8,128)S(1)}, f32[440,128]{1,0:T(8,128)S(1)}, u32[]{:S(2)}, u32[]{:S(2)}) collective-permute-start(f32[440,128]{1,0:T(8,128)S(1)} %get-tuple-element.26), channel_id=1, source_target_pairs={{0,12},{4,0},{8,4},{12,8},{1,13},{5,1},{9,5},{13,9},{2,14},{6,2},{... | collective-permute-start | bytes 675848 | tf_op jit(solution)/shard_map/ppermute | solution.py:563
  15.2 11.7 %spread.2 = (f32[24,152,48]{2,1,0:T(8,128)S(1)}, f32[12,19,128]{2,1,0:T(8,128)S(1)}, f32[12,19,128]{2,1,0:T(8,128)S(1)}) custom-call(s32[5]{0:T(128)S(1)} %stack.32.here.refs_0_, s32[32,4]{1,0:T(8,128)S(1)} %pad_add_fusion.infos.refs_1_, f32[16,768]{1,0:T(8,128)S(1)} %copy-done.1, f32[3,16,768]{2,1,0:T(8,128)S(1)} %maximum_maximum_fusion.refs_0_.refs_3_.refs_2_, ...), custom_call_target="tpu_custom_call" | custom-call | flops 4000000000 | bytes 4000000 | tf_op jit(solution)/shard_map/spread/pallas_call | solution.py:346
  27.8 1.7 %collective-permute-start.3 = (f32[2,14,19,128]{3,2,1,0:T(8,128)}, f32[2,14,19,128]{3,2,1,0:T(8,128)S(1)}, u32[]{:S(2)}, u32[]{:S(2)}) collective-permute-start(f32[2,14,19,128]{3,2,1,0:T(8,128)} %pad_maximum_fusion), channel_id=1, source_target_pairs={{0,2},{2,0},{1,3},{3,1},{4,6},{6,4},{5,7},{7,5},{8,10},{10,8},{9,1... | collective-permute-start | bytes 817160 | tf_op jit(solution)/shard_map/ppermute | solution.py:563
  29.6 5.9 %spread.3 = (f32[14,48,128]{2,1,0:T(8,128)S(1)}, f32[7,48,128]{2,1,0:T(8,128)S(1)}, f32[6,48,128]{2,1,0:T(8,128)S(1)}, f32[3,48,128]{2,1,0:T(8,128)S(1)}) custom-call(s32[5]{0:T(128)S(1)} %stack.32.here.refs_0_, s32[16,4]{1,0:T(8,128)S(1)} %pad_add_fusion.1.refs_1_, f32[16,768]{1,0:T(8,128)S(1)} %copy-done.1, ...), custom_call_target="tpu_custom_call" | custom-call | flops 4000000000 | bytes 4000000 | tf_op jit(solution)/shard_map/spread/pallas_call | solution.py:346
  35.6 1.3 %collective-permute-done.4.far = f32[3,48,128]{2,1,0:T(8,128)S(1)} collective-permute-done((f32[3,48,128]{2,1,0:T(8,128)S(1)}, f32[3,48,128]{2,1,0:T(8,128)S(1)}, u32[]{:S(2)}, u32[]{:S(2)}) %collective-permute-start.4) | collective-permute-done | bytes 73760 | tf_op jit(solution)/shard_map/ppermute | solution.py:563
  37.8 1.6 %collective-permute-start.6 = (f32[7,48,128]{2,1,0:T(8,128)}, f32[7,48,128]{2,1,0:T(8,128)}, u32[]{:S(2)}, u32[]{:S(2)}) collective-permute-start(f32[7,48,128]{2,1,0:T(8,128)} %get-tuple-element.36), channel_id=1, source_target_pairs={{0,12},{4,0},{8,4},{12,8},{1,13},{5,1},{9,5},{13,9},{2,14},{6,2},{... | collective-permute-start | bytes 516104 | tf_op jit(solution)/shard_map/ppermute | solution.py:563
  40.5 2.6 %assemble.1 = (f32[3,24,768]{2,1,0:T(8,128)S(1)}, f32[3,24,768]{2,1,0:T(8,128)S(1)}, s32[24,3]{1,0:T(8,128)S(1)}, s32[24,3]{1,0:T(8,128)S(1)}) custom-call(s32[5]{0:T(128)S(1)} %stack.32.here.refs_0_, s32[48,4]{1,0:T(8,128)S(1)} %concatenate.39.refs_1_, f32[3,16,768]{2,1,0:T(8,128)S(1)} %maximum_maximum_fusion.refs_0_.refs_3_.refs_2_, ...), custom_call_target="tpu_custom_call" | custom-call | tf_op jit(solution)/shard_map/assemble/pallas_call | solution.py:671
  43.5 4.1 %collective-permute-done.5.from_low = f32[6,48,128]{2,1,0:T(8,128)} collective-permute-done((f32[6,48,128]{2,1,0:T(8,128)}, f32[6,48,128]{2,1,0:T(8,128)}, u32[]{:S(2)}, u32[]{:S(2)}) %collective-permute-start.5) | collective-permute-done | bytes 147488 | tf_op jit(solution)/shard_map/ppermute | solution.py:563
  47.7 3.2 %collide.1 = (f32[19,14,16,128]{3,2,1,0:T(8,128)S(1)}, f32[14,48,128]{2,1,0:T(8,128)S(1)}, f32[5,14,16,128]{3,2,1,0:T(8,128)S(1)}) custom-call(f32[19,14,16,128]{3,2,1,0:T(8,128)S(1)} %extend.1.pops, f32[14,48,128]{2,1,0:T(8,128)S(1)} %get-tuple-element.34.refs_8_.own, f32[6,48,128]{2,1,0:T(8,128)} %collective-permute-done.5.from_low, ...), custom_call_target="tpu_custom_call" | custom-call | tf_op jit(solution)/shard_map/collide/pallas_call | solution.py:681
  51.0 2.0 %collective-permute-done.7.edge = f32[5,14,16,128]{3,2,1,0:T(8,128)S(1)} collective-permute-done((f32[5,14,16,128]{3,2,1,0:T(8,128)S(1)}, f32[5,14,16,128]{3,2,1,0:T(8,128)S(1)}, u32[]{:S(2)}, u32[]{:S(2)}) %collective-permute-start.7) | collective-permute-done | bytes 573472 | tf_op jit(solution)/shard_map/ppermute | solution.py:563
  52.9 2.6 %stream.1 = (f32[12,12,19,128]{3,2,1,0:T(8,128)}, f32[12,48,128]{2,1,0:T(8,128)S(1)}, f32[6,48,128]{2,1,0:T(8,128)S(1)}, f32[5,48,128]{2,1,0:T(8,128)S(1)}) custom-call(f32[19,14,16,128]{3,2,1,0:T(8,128)S(1)} %get-tuple-element.39.post, f32[5,14,16,128]{3,2,1,0:T(8,128)S(1)} %collective-permute-done.7.edge, f32[14,48,128]{2,1,0:T(8,128)S(1)} %get-tuple-element.41.force), custom_call_target="tpu_custom_call" | custom-call | tf_op jit(solution)/shard_map/stream/pallas_call | solution.py:694
  55.5 1.7 %collective-permute-start.8 = (f32[6,48,128]{2,1,0:T(8,128)S(1)}, f32[6,48,128]{2,1,0:T(8,128)S(1)}, u32[]{:S(2)}, u32[]{:S(2)}) collective-permute-start(f32[6,48,128]{2,1,0:T(8,128)S(1)} %get-tuple-element.44), channel_id=1, source_target_pairs={{0,4},{4,8},{8,12},{12,0},{1,5},{5,9},{9,13},{13,1},{2,6},{6,10},{... | collective-permute-start | bytes 442376 | tf_op jit(solution)/shard_map/ppermute | solution.py:563
  57.2 2.1 %collective-permute-start.9 = (f32[5,48,128]{2,1,0:T(8,128)S(1)}, f32[5,48,128]{2,1,0:T(8,128)S(1)}, u32[]{:S(2)}, u32[]{:S(2)}) collective-permute-start(f32[5,48,128]{2,1,0:T(8,128)S(1)} %get-tuple-element.46), channel_id=1, source_target_pairs={{0,12},{4,0},{8,4},{12,8},{1,13},{5,1},{9,5},{13,9},{2,14},{6,2},{... | collective-permute-start | bytes 368648 | tf_op jit(solution)/shard_map/ppermute | solution.py:563
  59.3 4.7 %collective-permute-done.8.low_side = f32[6,48,128]{2,1,0:T(8,128)S(1)} collective-permute-done((f32[6,48,128]{2,1,0:T(8,128)S(1)}, f32[6,48,128]{2,1,0:T(8,128)S(1)}, u32[]{:S(2)}, u32[]{:S(2)}) %collective-permute-start.8) | collective-permute-done | bytes 147488 | tf_op jit(solution)/shard_map/ppermute | solution.py:563
  64.1 1.8 %collective-permute-done.9.high_side = f32[5,48,128]{2,1,0:T(8,128)S(1)} collective-permute-done((f32[5,48,128]{2,1,0:T(8,128)S(1)}, f32[5,48,128]{2,1,0:T(8,128)S(1)}, u32[]{:S(2)}, u32[]{:S(2)}) %collective-permute-start.9) | collective-permute-done | bytes 122912 | tf_op jit(solution)/shard_map/ppermute | solution.py:563
  65.9 1.3 %collective-permute-done.12.high_far = f32[5,48,128]{2,1,0:T(8,128)S(1)} collective-permute-done((f32[5,48,128]{2,1,0:T(8,128)S(1)}, f32[5,48,128]{2,1,0:T(8,128)S(1)}, u32[]{:S(2)}, u32[]{:S(2)}) %collective-permute-start.12) | collective-permute-done | bytes 122912 | tf_op jit(solution)/shard_map/ppermute | solution.py:563
  67.2 5.0 %sample.3 = f32[3,16,768]{2,1,0:T(8,128)S(1)} custom-call(s32[24,3]{1,0:T(8,128)S(1)} %get-tuple-element.47.corner, f32[3,24,768]{2,1,0:T(8,128)S(1)} %get-tuple-element.38.refs_1_.pos, f32[6,48,128]{2,1,0:T(8,128)S(1)} %collective-permute-done.8.low_side, f32[12,48,128]{2,1,0:T(8,128)S(1)} %get-tuple-element.45.own, ...), custom_call_target="tpu_custom_call" | custom-call | flops 2000000000 | bytes 4000000 | tf_op jit(solution)/shard_map/sample/pallas_call | solution.py:435
  72.7 5.0 %sample.2 = f32[3,16,768]{2,1,0:T(8,128)S(1)} custom-call(s32[24,3]{1,0:T(8,128)S(1)} %get-tuple-element.43.corner, f32[3,24,768]{2,1,0:T(8,128)S(1)} %get-tuple-element.37.refs_0_.pos, f32[6,48,128]{2,1,0:T(8,128)S(1)} %collective-permute-done.8.low_side, f32[12,48,128]{2,1,0:T(8,128)S(1)} %get-tuple-element.45.own, ...), custom_call_target="tpu_custom_call" | custom-call | flops 2000000000 | bytes 4000000 | tf_op jit(solution)/shard_map/sample/pallas_call | solution.py:435
  (43 shorter events, 6.5 us)
Async XLA Ops:
  0.6 14.5 %copy-start.1 = (f32[16,768]{1,0:T(8,128)S(1)}, f32[16,768]{1,0:T(8,128)}, u32[]{:S(2)}) copy-start(f32[16,768]{1,0:T(8,128)} %constant.35.clone.refs_2_) | copy-start | bytes 147460
  0.6 14.5 %copy-start = (f32[19,12,12,128]{3,0,2,1:T(8,128)S(1)}, f32[19,12,12,128]{3,0,2,1:T(8,128)}, u32[]{:S(2)}) copy-start(f32[19,12,12,128]{3,0,2,1:T(8,128)} %param.5) | copy-start | bytes 4202500
  2.6 6.8 %collective-permute-start = (f32[3,16,768]{2,1,0:T(8,128)S(1)}, f32[3,16,768]{2,1,0:T(8,128)S(1)}, u32[]{:S(2)}, u32[]{:S(2)}) collective-permute-start(f32[3,16,768]{2,1,0:T(8,128)S(1)} %maximum_maximum_fusion.refs_0_.refs_3_.refs_2_), channel_id=1, source_target_pairs={{0,2},{2,0},{1,3},{3,1},{4,6},{6,4},{5,7},{7,5},{8,10},{10,8},{9,1... | collective-permute-start | bytes 442376 | tf_op jit(solution)/shard_map/ppermute | solution.py:563
  11.2 15.7 %collective-permute-start.1 = (f32[440,128]{1,0:T(8,128)S(1)}, f32[440,128]{1,0:T(8,128)S(1)}, u32[]{:S(2)}, u32[]{:S(2)}) collective-permute-start(f32[440,128]{1,0:T(8,128)S(1)} %get-tuple-element.25), channel_id=1, source_target_pairs={{0,4},{4,8},{8,12},{12,0},{1,5},{5,9},{9,13},{13,1},{2,6},{6,10},{... | collective-permute-start | bytes 675848 | tf_op jit(solution)/shard_map/ppermute | solution.py:563
  13.1 13.9 %collective-permute-start.2 = (f32[440,128]{1,0:T(8,128)S(1)}, f32[440,128]{1,0:T(8,128)S(1)}, u32[]{:S(2)}, u32[]{:S(2)}) collective-permute-start(f32[440,128]{1,0:T(8,128)S(1)} %get-tuple-element.26), channel_id=1, source_target_pairs={{0,12},{4,0},{8,4},{12,8},{1,13},{5,1},{9,5},{13,9},{2,14},{6,2},{... | collective-permute-start | bytes 675848 | tf_op jit(solution)/shard_map/ppermute | solution.py:563
  27.8 15.3 %collective-permute-start.3 = (f32[2,14,19,128]{3,2,1,0:T(8,128)}, f32[2,14,19,128]{3,2,1,0:T(8,128)S(1)}, u32[]{:S(2)}, u32[]{:S(2)}) collective-permute-start(f32[2,14,19,128]{3,2,1,0:T(8,128)} %pad_maximum_fusion), channel_id=1, source_target_pairs={{0,2},{2,0},{1,3},{3,1},{4,6},{6,4},{5,7},{7,5},{8,10},{10,8},{9,1... | collective-permute-start | bytes 817160 | tf_op jit(solution)/shard_map/ppermute | solution.py:563
  29.6 5.9 %copy-start.2 = (s32[4,4]{1,0:T(4,128)}, s32[4,4]{1,0:T(4,128)S(1)}, u32[]{:S(2)}) copy-start(s32[4,4]{1,0:T(4,128)S(1)} %get-tuple-element.53) | copy-start | bytes 196
  35.5 1.3 %collective-permute-start.4 = (f32[3,48,128]{2,1,0:T(8,128)S(1)}, f32[3,48,128]{2,1,0:T(8,128)S(1)}, u32[]{:S(2)}, u32[]{:S(2)}) collective-permute-start(f32[3,48,128]{2,1,0:T(8,128)S(1)} %get-tuple-element.33), channel_id=1, source_target_pairs={{0,1},{1,0},{2,3},{3,2},{4,5},{5,4},{6,7},{7,6},{8,9},{9,8},{10,11... | collective-permute-start | bytes 221192 | tf_op jit(solution)/shard_map/ppermute | solution.py:563
  37.8 9.9 %collective-permute-start.6 = (f32[7,48,128]{2,1,0:T(8,128)}, f32[7,48,128]{2,1,0:T(8,128)}, u32[]{:S(2)}, u32[]{:S(2)}) collective-permute-start(f32[7,48,128]{2,1,0:T(8,128)} %get-tuple-element.36), channel_id=1, source_target_pairs={{0,12},{4,0},{8,4},{12,8},{1,13},{5,1},{9,5},{13,9},{2,14},{6,2},{... | collective-permute-start | bytes 516104 | tf_op jit(solution)/shard_map/ppermute | solution.py:563
  39.4 8.2 %collective-permute-start.5 = (f32[6,48,128]{2,1,0:T(8,128)}, f32[6,48,128]{2,1,0:T(8,128)}, u32[]{:S(2)}, u32[]{:S(2)}) collective-permute-start(f32[6,48,128]{2,1,0:T(8,128)} %get-tuple-element.35), channel_id=1, source_target_pairs={{0,4},{4,8},{8,12},{12,0},{1,5},{5,9},{9,13},{13,1},{2,6},{6,10},{... | collective-permute-start | bytes 442376 | tf_op jit(solution)/shard_map/ppermute | solution.py:563
  50.9 2.0 %collective-permute-start.7 = (f32[5,14,16,128]{3,2,1,0:T(8,128)S(1)}, f32[5,14,16,128]{3,2,1,0:T(8,128)S(1)}, u32[]{:S(2)}, u32[]{:S(2)}) collective-permute-start(f32[5,14,16,128]{3,2,1,0:T(8,128)S(1)} %get-tuple-element.40), channel_id=1, source_target_pairs={{0,1},{1,0},{2,3},{3,2},{4,5},{5,4},{6,7},{7,6},{8,9},{9,8},{10,11... | collective-permute-start | bytes 1720328 | tf_op jit(solution)/shard_map/ppermute | solution.py:563
  55.5 8.5 %collective-permute-start.8 = (f32[6,48,128]{2,1,0:T(8,128)S(1)}, f32[6,48,128]{2,1,0:T(8,128)S(1)}, u32[]{:S(2)}, u32[]{:S(2)}) collective-permute-start(f32[6,48,128]{2,1,0:T(8,128)S(1)} %get-tuple-element.44), channel_id=1, source_target_pairs={{0,4},{4,8},{8,12},{12,0},{1,5},{5,9},{9,13},{13,1},{2,6},{6,10},{... | collective-permute-start | bytes 442376 | tf_op jit(solution)/shard_map/ppermute | solution.py:563
  57.2 10.0 %collective-permute-start.11 = (f32[12,48,128]{2,1,0:T(8,128)S(1)}, f32[12,48,128]{2,1,0:T(8,128)S(1)}, u32[]{:S(2)}, u32[]{:S(2)}) collective-permute-start(f32[12,48,128]{2,1,0:T(8,128)S(1)} %get-tuple-element.45.own), channel_id=1, source_target_pairs={{0,1},{1,0},{2,3},{3,2},{4,5},{5,4},{6,7},{7,6},{8,9},{9,8},{10,11... | collective-permute-start | bytes 884744 | tf_op jit(solution)/shard_map/ppermute | solution.py:563
  57.2 8.6 %collective-permute-start.9 = (f32[5,48,128]{2,1,0:T(8,128)S(1)}, f32[5,48,128]{2,1,0:T(8,128)S(1)}, u32[]{:S(2)}, u32[]{:S(2)}) collective-permute-start(f32[5,48,128]{2,1,0:T(8,128)S(1)} %get-tuple-element.46), channel_id=1, source_target_pairs={{0,12},{4,0},{8,4},{12,8},{1,13},{5,1},{9,5},{13,9},{2,14},{6,2},{... | collective-permute-start | bytes 368648 | tf_op jit(solution)/shard_map/ppermute | solution.py:563
  64.0 3.1 %collective-permute-start.10 = (f32[6,48,128]{2,1,0:T(8,128)S(1)}, f32[6,48,128]{2,1,0:T(8,128)S(1)}, u32[]{:S(2)}, u32[]{:S(2)}) collective-permute-start(f32[6,48,128]{2,1,0:T(8,128)S(1)} %collective-permute-done.8.low_side), channel_id=1, source_target_pairs={{0,1},{1,0},{2,3},{3,2},{4,5},{5,4},{6,7},{7,6},{8,9},{9,8},{10,11... | collective-permute-start | bytes 442376 | tf_op jit(solution)/shard_map/ppermute | solution.py:563
  65.8 1.3 %collective-permute-start.12 = (f32[5,48,128]{2,1,0:T(8,128)S(1)}, f32[5,48,128]{2,1,0:T(8,128)S(1)}, u32[]{:S(2)}, u32[]{:S(2)}) collective-permute-start(f32[5,48,128]{2,1,0:T(8,128)S(1)} %collective-permute-done.9.high_side), channel_id=1, source_target_pairs={{0,1},{1,0},{2,3},{3,2},{4,5},{5,4},{6,7},{7,6},{8,9},{9,8},{10,11... | collective-permute-start | bytes 368648 | tf_op jit(solution)/shard_map/ppermute | solution.py:563
  72.2 6.0 %collective-permute-start.13 = (f32[3,16,768]{2,1,0:T(8,128)S(1)}, f32[3,16,768]{2,1,0:T(8,128)S(1)}, u32[]{:S(2)}, u32[]{:S(2)}) collective-permute-start(f32[3,16,768]{2,1,0:T(8,128)S(1)} %sample.3), channel_id=1, source_target_pairs={{0,2},{2,0},{1,3},{3,1},{4,6},{6,4},{5,7},{7,5},{8,10},{10,8},{9,1... | collective-permute-start | bytes 442376 | tf_op jit(solution)/shard_map/ppermute | solution.py:563

commit v3 on v2

--- a/solution.py
+++ b/solution.py
@@ -197,26 +197,29 @@
 def fill_planar(pos, wave, c, high, low):
     width = pos.shape[2]
     row = lax.broadcasted_iota(jnp.int32, (8, 128), 0)
-    rowf = wide((row - REACH).astype(F32), width)
+    rowf = (row - REACH).astype(F32)
+    joint = wide(jnp.where(row < 4, rowf + 8.0, rowf - 4.0), width)
+    rowf = wide(rowf, width)
+    upper = wide(row, width) < 4
     odd = wide((row & 1), width) == 1
     flip = wide((row & 2), width) == 0
     z, cz, sz = row_of(pos, 2, c), row_of(wave, 4, c), row_of(wave, 5, c)
     base = jnp.where(odd, sz, cz)
     pattern = 0.25 + jnp.where(flip, -base, base)
-    wz = jnp.concatenate(
-        [
-            jnp.where(jnp.abs(rowf - z) < 2.0, pattern, 0.0),
-            jnp.where(jnp.abs(rowf + 8.0 - z) < 2.0, pattern, 0.0),
-        ],
-        axis=0,
-    )
+    wz = [
+        jnp.where(jnp.abs(rows - z) < 2.0, pattern, 0.0) for rows in (rowf, joint, rowf + 4.0)
+    ]
     x, cx, sx = row_of(pos, 0, c), row_of(wave, 0, c), row_of(wave, 1, c)
     quarter = (0.25 - cx, 0.25 - sx, 0.25 + cx, 0.25 + sx)
-    for kx in range(2 * REACH):
-        wx = jnp.where(jnp.abs(x - float(kx - REACH)) < 2.0, quarter[kx % 4], 0.0)
-        high[16 * kx : 16 * kx + 16, :], low[16 * kx : 16 * kx + 16, :] = split(
-            jnp.concatenate([wx, wx], axis=0) * wz
-        )
+    for four in range(3):
+        tiles = []
+        for kx in (4 * four, 4 * four + 2):
+            wx = [
+                jnp.where(jnp.abs(x - float(k - REACH)) < 2.0, quarter[k % 4], 0.0) for k in (kx, kx + 1)
+            ]
+            tiles += [wx[0] * wz[0], jnp.where(upper, wx[0], wx[1]) * wz[1], wx[1] * wz[2]]
+        rows = slice(48 * four, 48 * four + 48)
+        high[rows, :], low[rows, :] = split(jnp.concatenate(tiles, axis=0))
 
 
 def rows_weight(pos, wave, c, anchor, images):
@@ -257,12 +260,12 @@
     else:
         acc, refs = refs[0], refs[1:]
     takers, refs = refs[:n_copied], refs[n_copied:]
-    pos, wave, force, planar, corner = refs[:5]
+    pos, wave, force, planar, corner, patch = refs[:6]
     if last:
-        acc = refs[5]
+        acc = refs[6]
     moves = []
     for n, (giver, source, taker, target) in enumerate(copies):
-        move = pltpu.make_async_copy(givers[giver].at[source], takers[taker].at[target], refs[5].at[n])
+        move = pltpu.make_async_copy(givers[giver].at[source], takers[taker].at[target], refs[-1].at[n])
         move.start()
         moves.append(move)
     if sums:
@@ -300,7 +303,7 @@
     fill_force(pos, table, force)
 
     def weigh(c, b):
-        fill_planar(pos, wave, c, planar.at[b, 0:192], planar.at[b, 192:384])
+        fill_planar(pos, wave, c, planar.at[b, 0:144], planar.at[b, 144:288])
         images = (corner[c, 3].astype(F32), corner[c, 4].astype(F32))
         wy = rows_weight(pos, wave, c, corner[c, 1], images)
         lifted = []
@@ -309,9 +312,11 @@
             lifted.append(jnp.concatenate([f, f], axis=0) * wy)
         high, low = split(jnp.concatenate(lifted, axis=0))
         both = nt_dot(planar[b], high)
-        total = both[:192] + both[192:] + nt_dot(planar[b, 0:192], low)
+        patch[b] = both[:144] + both[144:] + nt_dot(planar[b, 0:144], low)
         x0, z0 = corner[c, 0], corner[c, 2] + 2
-        acc[pl.ds(x0, 12), pl.ds(z0, 16), :] += total.reshape(12, 16, 48)
+        before = [acc[x0 + kx, pl.ds(z0, 12), :] for kx in range(12)]
+        for kx in range(12):
+            acc[x0 + kx, pl.ds(z0, 12), :] = before[kx] + patch[b, 12 * kx : 12 * kx + 12, :]
 
     def weigh_some(i, carry):
         for b in range(together):
@@ -356,8 +361,9 @@
             pltpu.VMEM((3, rows + 8, width), F32),
             pltpu.VMEM((6, rows, width), F32),
             pltpu.VMEM((3, rows, width), F32),
-            pltpu.VMEM((together, 384, width), jnp.bfloat16),
+            pltpu.VMEM((together, 288, width), jnp.bfloat16),
             pltpu.SMEM((rows + 8, 5), jnp.int32),
+            pltpu.VMEM((together, 144, 48), F32),
         ]
         + ([pltpu.VMEM((24, 152, 48), F32)] if last else [])
         + ([pltpu.SemaphoreType.DMA((len(copies),))] if copies else []),
@@ -396,25 +402,30 @@
         fill_planar(pos, wave, c, high.at[b], low.at[b])
         z0 = corner[c, 2] - REACH
         x0 = corner[c, 0]
-        turn = (z0 + 16 * x0 + 128) & 127
-        origin = (lane - turn) & 127
-        group = jnp.right_shift(origin, 4)
-        z = (origin & 15) + z0
-        inside = jnp.logical_and(z >= 0, z < 128)
-        chosen = [group == g for g in range(8)]
+        turn = (z0 + 12 * x0 + 128) & 127
+        inside, chosen = [], []
+        for t in range(2):
+            origin = (lane - turn - 72 * t) & 127
+            group = jnp.right_shift(origin * 43, 9)
+            z = origin - 12 * group + z0
+            inside.append(jnp.logical_and(z >= 0, z < 128))
+            chosen.append([group == g for g in range(6)])
+        front = lane < 72
         blocks = []
         for r in range(6):
             rows = slice(8 * r, 8 * r + 8)
-            near = flow[pl.ds(x0, 12), rows, :]
-            there = far[pl.ds(x0, 12), rows, :]
+            near = [flow[x0 + kx, rows, :] for kx in range(12)]
+            there = [far[x0 + kx, rows, :] for kx in range(12)]
             turned = []
             for t in range(2):
-                a, b_ = near[8 * t], there[8 * t]
-                for g in range(1, 8 - 4 * t):
-                    a = jnp.where(chosen[g], near[8 * t + g], a)
-                    b_ = jnp.where(chosen[g], there[8 * t + g], b_)
-                turned.append(pltpu.roll(jnp.where(inside, a, b_), (128 - turn) & 127, 1))
-            blocks.append(jnp.concatenate([turned[0], turned[1][:, 0:64]], axis=1))
+                a, b_ = near[6 * t], there[6 * t]
+                for g in range(1, 6):
+                    a = jnp.where(chosen[t][g], near[6 * t + g], a)
+                    b_ = jnp.where(chosen[t][g], there[6 * t + g], b_)
+                turned.append(pltpu.roll(jnp.where(inside[t], a, b_), (128 - turn) & 127, 1))
+            blocks.append(
+                jnp.concatenate([jnp.where(front, turned[0], turned[1]), turned[1][:, 0:16]], axis=1)
+            )
         qhigh, qlow = split(jnp.concatenate(blocks, axis=0))
         both = jnp.dot(jnp.concatenate([qhigh, qlow], axis=0), high[b], preferred_element_type=F32)
         mixed = both[:48] + both[48:] + jnp.dot(qhigh, low[b], preferred_element_type=F32)
@@ -441,8 +452,8 @@
             pltpu.VMEM((24, 48, 128), F32),
             pltpu.VMEM((24, 48, 128), F32),
             pltpu.VMEM((6, cells, width), F32),
-            pltpu.VMEM((4, 192, width), jnp.bfloat16),
-            pltpu.VMEM((4, 192, width), jnp.bfloat16),
+            pltpu.VMEM((4, 144, width), jnp.bfloat16),
+            pltpu.VMEM((4, 144, width), jnp.bfloat16),
         ],
         compiler_params=params(),
         name="sample",
@@ -517,23 +528,28 @@
     lax.fori_loop(0, planes, plane, 0)
 
 
-def stream_kernel(post, edge, force, pops, own, up, down, velocity):
-    ny = pops.shape[1]
+def arriving(post, edge, x, ny):
     lane = lax.broadcasted_iota(jnp.int32, (ny, 128), 1)
+    found = []
+    for i in range(19):
+        cx, cy, cz = DIRS[i]
+        value = post[i, x + 1 - cx, 1 - cy : 1 - cy + ny, :]
+        if cz == 1:
+            side = edge[RISING.index(i), x + 1 - cx, 1 - cy : 1 - cy + ny, :]
+            value = jnp.where(lane == 0, side, pltpu.roll(value, 1, 1))
+        elif cz == -1:
+            side = edge[FALLING.index(i), x + 1 - cx, 1 - cy : 1 - cy + ny, :]
+            value = jnp.where(lane == 127, side, pltpu.roll(value, 127, 1))
+        found.append(value)
+    return found
+
+
+def flow_kernel(ny, post, edge, force, own, up, down, velocity):
+    nx = own.shape[0]
     velocity[...] = jnp.zeros(velocity.shape, F32)
 
     def plane(x, carry):
-        n = []
-        for i in range(19):
-            cx, cy, cz = DIRS[i]
-            value = post[i, x + 1 - cx, 1 - cy : 1 - cy + ny, :]
-            if cz == 1:
-                side = edge[RISING.index(i), x + 1 - cx, 1 - cy : 1 - cy + ny, :]
-                value = jnp.where(lane == 0, side, pltpu.roll(value, 1, 1))
-            elif cz == -1:
-                side = edge[FALLING.index(i), x + 1 - cx, 1 - cy : 1 - cy + ny, :]
-                value = jnp.where(lane == 127, side, pltpu.roll(value, 127, 1))
-            n.append(value)
+        n = arriving(post, edge, x, ny)
         rho = n[0]
         for i in range(1, 19):
             rho = rho + n[i]
@@ -545,17 +561,23 @@
                 elif DIRS[i][a] == -1:
                     m = m - n[i]
             velocity[x, 16 * a + 1 : 16 * a + 1 + ny, :] = m / rho
-        pops[x] = jnp.transpose(jnp.stack(n), (1, 0, 2))
         return carry
 
-    nx = pops.shape[0]
     lax.fori_loop(0, nx, plane, 0)
     for x in range(nx):
-        own[x] = pltpu.roll(velocity[x], 16 * (x + REACH) % 128, 1)
+        own[x] = pltpu.roll(velocity[x], 12 * (x + REACH) % 128, 1)
         if x >= nx - REACH:
-            up[x - nx + REACH] = pltpu.roll(velocity[x], 16 * (x + REACH - nx) % 128, 1)
+            up[x - nx + REACH] = pltpu.roll(velocity[x], 12 * (x + REACH - nx) % 128, 1)
         if x < REACH - 1:
-            down[x] = pltpu.roll(velocity[x], 16 * (x + REACH + nx) % 128, 1)
+            down[x] = pltpu.roll(velocity[x], 12 * (x + REACH + nx) % 128, 1)
+
+
+def renew_kernel(post, edge, after, pops):
+    def plane(x, carry):
+        pops[x] = jnp.transpose(jnp.stack(arriving(post, edge, x, pops.shape[1])), (1, 0, 2))
+        return carry
+
+    lax.fori_loop(0, pops.shape[0], plane, 0)
 
 
 def shifted(x, axis, distance):
@@ -691,19 +713,27 @@
         name="collide",
     )(extended, own, from_low, from_high, *positions)
     edge = shifted(edge, "sub", 1)
-    renewed, velocity, up_flow, down_flow = pl.pallas_call(
-        stream_kernel,
-        out_shape=(jax.ShapeDtypeStruct((extent[0], extent[1], 19, 128), F32),)
-        + tuple(jax.ShapeDtypeStruct((n, 48, 128), F32) for n in (extent[0], REACH, REACH - 1)),
+    velocity, up_flow, down_flow = pl.pallas_call(
+        functools.partial(flow_kernel, ny),
+        out_shape=tuple(jax.ShapeDtypeStruct((n, 48, 128), F32) for n in (nx, REACH, REACH - 1)),
         in_specs=[VMEM] * 3,
-        out_specs=(VMEM,) * 4,
-        scratch_shapes=[pltpu.VMEM((extent[0], 48, 128), F32)],
-        compiler_params=params(),
-        name="stream",
+        out_specs=(VMEM,) * 3,
+        scratch_shapes=[pltpu.VMEM((nx, 48, 128), F32)],
+        compiler_params=params(),
+        name="flow",
     )(post, edge, force)
+    renewed = pl.pallas_call(
+        renew_kernel,
+        out_shape=jax.ShapeDtypeStruct((nx, ny, 19, 128), F32),
+        in_specs=[VMEM] * 2 + [pl.BlockSpec(memory_space=pl.ANY)],
+        out_specs=VMEM,
+        compiler_params=params(),
+        name="renew",
+    )(post, edge, velocity)
 
     low_side = shifted(up_flow, "slab", 1)
     high_side = shifted(down_flow, "slab", -1)
+    low_side, high_side, renewed = lax.optimization_barrier((low_side, high_side, renewed))
     parts = (low_side, velocity, high_side)
     parts = parts + tuple(shifted(part, "sub", 1) for part in parts)
     shares = [

time: 79.3 us -> 77.9 us (0.982)
  waiting for transfers between devices: 18.4 us -> 16.2 us
    ppermute x14, waiting for transfers between devices: 18.4 us -> 16.2 us  [shifted(): lax.ppermute(x, axis, [(i, (i + distance) % count) for i in range(count)])]
    pallas_call x1 -> x2, Pallas kernels: 2.58 us -> 3.76 us  [the longest x1 2.37 us: on_device(): pl.pallas_call(renew_kernel, out_shape=jax.ShapeDtypeStruct((nx, ny, 19,...]
  transfers between devices with their start and end apart: 14 -> 14, of which waited for: 8 -> 7; matrix products, arithmetic and copies ran while one was open for 3% -> 3% of each run, Pallas kernels for 34% -> 36%
where the time goes in v3:
time: 77.9 us; the launch traced here: 77.5 us
  Pallas kernels  39.2 us (50%)
  waiting for transfers between devices  16.2 us (21%)
  starting transfers between devices  15.7 us (20%)
  other arithmetic  3.56 us (5%)
  local copies, waits for them, and re-layouts  2.01 us (3%)
  between operations  0.85 us (1%)
    pallas_call x2, Pallas kernels, stage(): pl.pallas_call(functools.partial(stage_kernel, sizes, plan, last, copies,...  17 us
    ppermute x14, waiting for transfers between devices, shifted(): lax.ppermute(x, axis, [(i, (i + distance) % count) for i in range(count)])  16.2 us
    ppermute x14, starting transfers between devices, shifted(): lax.ppermute(x, axis, [(i, (i + distance) % count) for i in range(count)])  15.7 us
    pallas_call x2, Pallas kernels, sampled(): pl.pallas_call(functools.partial(sample_kernel, images), out_shape=jax.Sh...  9.65 us
    pallas_call x1, Pallas kernels, on_device(): pl.pallas_call(collide_kernel, out_shape=(jax.ShapeDtypeStruct((19, plane...  3.22 us
    pallas_call x1, Pallas kernels, on_device(): pl.pallas_call(functools.partial(assemble_kernel, sizes, groups, offsets)...  2.63 us
    pallas_call x1, Pallas kernels, on_device(): pl.pallas_call(renew_kernel, out_shape=jax.ShapeDtypeStruct((nx, ny, 19,...  2.37 us
    pallas_call x1, Pallas kernels, on_device(): pl.pallas_call(functools.partial(pack_kernel, capacity, slabs, crosses *...  1.66 us
  transfers between devices with their start and end apart: 14, of which 7 were waited for; matrix products, arithmetic and copies ran while one was open for 3% of the time, Pallas kernels for 36%

profile of v3, /device:TPU:0, one launch (start us, length us, event | category | flops | bytes accessed | tf_op | source)
XLA Modules:
  0.0 77.5 jit_solution(8142282620274976280)
XLA Ops:
  1.7 1.0 %maximum_maximum_fusion.refs_0_.refs_3_.refs_2_ = f32[3,16,768]{2,1,0:T(8,128)S(1)} fusion(f32[3,16,4]{2,1,0:T(8,128)S(1)} %broadcast_in_dim.4, f32[3,16,642]{2,1,0:T(8,128)} %bitcast.35, f32[768]{0:T(1024)S(1)} %pad.18.clone), kind=kLoop, calls=%fused_computation.6 | loop fusion | flops 73728 | bytes 274560 | tf_op jit(solution)/shard_map/concatenate | solution.py:599
  2.6 2.9 %collective-permute-start = (f32[3,16,768]{2,1,0:T(8,128)S(1)}, f32[3,16,768]{2,1,0:T(8,128)S(1)}, u32[]{:S(2)}, u32[]{:S(2)}) collective-permute-start(f32[3,16,768]{2,1,0:T(8,128)S(1)} %maximum_maximum_fusion.refs_0_.refs_3_.refs_2_), channel_id=1, source_target_pairs={{0,2},{2,0},{1,3},{3,1},{4,6},{6,4},{5,7},{7,5},{8,10},{10,8},{9,1... | collective-permute-start | bytes 442376 | tf_op jit(solution)/shard_map/ppermute | solution.py:585
  5.6 1.0 %fusion.2 = (f32[1,12,19,128]{3,2,1,0:T(8,128)S(1)}, f32[1,12,19,128]{3,2,1,0:T(8,128)S(1)}) fusion(f32[12,12,19,128]{3,2,1,0:T(8,128)} %bitcast.27), kind=kLoop, calls=%fused_computation.21 | loop fusion | bytes 466944 | tf_op jit(solution)/shard_map/slice | solution.py:618
  6.7 2.7 %collective-permute-done.refs_1_.refs_4_.refs_5_ = f32[3,16,768]{2,1,0:T(8,128)S(1)} collective-permute-done((f32[3,16,768]{2,1,0:T(8,128)S(1)}, f32[3,16,768]{2,1,0:T(8,128)S(1)}, u32[]{:S(2)}, u32[]{:S(2)}) %collective-permute-start) | collective-permute-done | bytes 147488 | tf_op jit(solution)/shard_map/ppermute | solution.py:585
  9.5 1.7 %pack.1 = (f32[440,128]{1,0:T(8,128)S(1)}, f32[440,128]{1,0:T(8,128)S(1)}) custom-call(s32[5]{0:T(128)S(1)} %stack.32.here.refs_0_, s32[32,4]{1,0:T(8,128)S(1)} %pad_add_fusion.infos.refs_1_, f32[3,16,768]{2,1,0:T(8,128)S(1)} %maximum_maximum_fusion.refs_0_.refs_3_.refs_2_, f32[3,16,768]{2,1,0:T(8,128)S(1)} %collective-permute-done.refs_1_.refs_4_.refs_5_, ...), custom_call_target="tpu_custom_call" | custom-call | tf_op jit(solution)/shard_map/pack/pallas_call | solution.py:622
  11.2 1.9 %collective-permute-start.1 = (f32[440,128]{1,0:T(8,128)S(1)}, f32[440,128]{1,0:T(8,128)S(1)}, u32[]{:S(2)}, u32[]{:S(2)}) collective-permute-start(f32[440,128]{1,0:T(8,128)S(1)} %get-tuple-element.27), channel_id=1, source_target_pairs={{0,4},{4,8},{8,12},{12,0},{1,5},{5,9},{9,13},{13,1},{2,6},{6,10},{... | collective-permute-start | bytes 675848 | tf_op jit(solution)/shard_map/ppermute | solution.py:585
  13.1 2.1 %collective-permute-start.2 = (f32[440,128]{1,0:T(8,128)S(1)}, f32[440,128]{1,0:T(8,128)S(1)}, u32[]{:S(2)}, u32[]{:S(2)}) collective-permute-start(f32[440,128]{1,0:T(8,128)S(1)} %get-tuple-element.28), channel_id=1, source_target_pairs={{0,12},{4,0},{8,4},{12,8},{1,13},{5,1},{9,5},{13,9},{2,14},{6,2},{... | collective-permute-start | bytes 675848 | tf_op jit(solution)/shard_map/ppermute | solution.py:585
  15.2 11.2 %spread.2 = (f32[24,152,48]{2,1,0:T(8,128)S(1)}, f32[12,19,128]{2,1,0:T(8,128)S(1)}, f32[12,19,128]{2,1,0:T(8,128)S(1)}) custom-call(s32[5]{0:T(128)S(1)} %stack.32.here.refs_0_, s32[32,4]{1,0:T(8,128)S(1)} %pad_add_fusion.infos.refs_1_, f32[16,768]{1,0:T(8,128)S(1)} %copy-done.1, f32[3,16,768]{2,1,0:T(8,128)S(1)} %maximum_maximum_fusion.refs_0_.refs_3_.refs_2_, ...), custom_call_target="tpu_custom_call" | custom-call | flops 4000000000 | bytes 4000000 | tf_op jit(solution)/shard_map/spread/pallas_call | solution.py:351
  27.2 1.7 %collective-permute-start.3 = (f32[2,14,19,128]{3,2,1,0:T(8,128)}, f32[2,14,19,128]{3,2,1,0:T(8,128)S(1)}, u32[]{:S(2)}, u32[]{:S(2)}) collective-permute-start(f32[2,14,19,128]{3,2,1,0:T(8,128)} %pad_maximum_fusion), channel_id=1, source_target_pairs={{0,2},{2,0},{1,3},{3,1},{4,6},{6,4},{5,7},{7,5},{8,10},{10,8},{9,1... | collective-permute-start | bytes 817160 | tf_op jit(solution)/shard_map/ppermute | solution.py:585
  29.1 5.8 %spread.3 = (f32[14,48,128]{2,1,0:T(8,128)S(1)}, f32[7,48,128]{2,1,0:T(8,128)S(1)}, f32[6,48,128]{2,1,0:T(8,128)S(1)}, f32[3,48,128]{2,1,0:T(8,128)S(1)}) custom-call(s32[5]{0:T(128)S(1)} %stack.32.here.refs_0_, s32[16,4]{1,0:T(8,128)S(1)} %pad_add_fusion.1.refs_1_, f32[16,768]{1,0:T(8,128)S(1)} %copy-done.1, ...), custom_call_target="tpu_custom_call" | custom-call | flops 4000000000 | bytes 4000000 | tf_op jit(solution)/shard_map/spread/pallas_call | solution.py:351
  35.0 1.3 %collective-permute-done.4.far = f32[3,48,128]{2,1,0:T(8,128)S(1)} collective-permute-done((f32[3,48,128]{2,1,0:T(8,128)S(1)}, f32[3,48,128]{2,1,0:T(8,128)S(1)}, u32[]{:S(2)}, u32[]{:S(2)}) %collective-permute-start.4) | collective-permute-done | bytes 73760 | tf_op jit(solution)/shard_map/ppermute | solution.py:585
  37.1 1.6 %collective-permute-start.6 = (f32[7,48,128]{2,1,0:T(8,128)}, f32[7,48,128]{2,1,0:T(8,128)}, u32[]{:S(2)}, u32[]{:S(2)}) collective-permute-start(f32[7,48,128]{2,1,0:T(8,128)} %get-tuple-element.38), channel_id=1, source_target_pairs={{0,12},{4,0},{8,4},{12,8},{1,13},{5,1},{9,5},{13,9},{2,14},{6,2},{... | collective-permute-start | bytes 516104 | tf_op jit(solution)/shard_map/ppermute | solution.py:585
  39.9 2.6 %assemble.1 = (f32[3,24,768]{2,1,0:T(8,128)S(1)}, f32[3,24,768]{2,1,0:T(8,128)S(1)}, s32[24,3]{1,0:T(8,128)S(1)}, s32[24,3]{1,0:T(8,128)S(1)}) custom-call(s32[5]{0:T(128)S(1)} %stack.32.here.refs_0_, s32[48,4]{1,0:T(8,128)S(1)} %concatenate.39.refs_1_, f32[3,16,768]{2,1,0:T(8,128)S(1)} %maximum_maximum_fusion.refs_0_.refs_3_.refs_2_, ...), custom_call_target="tpu_custom_call" | custom-call | tf_op jit(solution)/shard_map/assemble/pallas_call | solution.py:693
  42.9 4.8 %collective-permute-done.5.from_low = f32[6,48,128]{2,1,0:T(8,128)} collective-permute-done((f32[6,48,128]{2,1,0:T(8,128)}, f32[6,48,128]{2,1,0:T(8,128)}, u32[]{:S(2)}, u32[]{:S(2)}) %collective-permute-start.5) | collective-permute-done | bytes 147488 | tf_op jit(solution)/shard_map/ppermute | solution.py:585
  47.7 3.2 %collide.1 = (f32[19,14,16,128]{3,2,1,0:T(8,128)S(1)}, f32[14,48,128]{2,1,0:T(8,128)S(1)}, f32[5,14,16,128]{3,2,1,0:T(8,128)S(1)}) custom-call(f32[19,14,16,128]{3,2,1,0:T(8,128)S(1)} %extend.1.pops, f32[14,48,128]{2,1,0:T(8,128)S(1)} %get-tuple-element.36.refs_8_.own, f32[6,48,128]{2,1,0:T(8,128)} %collective-permute-done.5.from_low, ...), custom_call_target="tpu_custom_call" | custom-call | tf_op jit(solution)/shard_map/collide/pallas_call | solution.py:703
  51.0 2.0 %collective-permute-done.7.edge = f32[5,14,16,128]{3,2,1,0:T(8,128)S(1)} collective-permute-done((f32[5,14,16,128]{3,2,1,0:T(8,128)S(1)}, f32[5,14,16,128]{3,2,1,0:T(8,128)S(1)}, u32[]{:S(2)}, u32[]{:S(2)}) %collective-permute-start.7) | collective-permute-done | bytes 573472 | tf_op jit(solution)/shard_map/ppermute | solution.py:585
  52.9 1.4 %flow.1 = (f32[12,48,128]{2,1,0:T(8,128)S(1)}, f32[6,48,128]{2,1,0:T(8,128)S(1)}, f32[5,48,128]{2,1,0:T(8,128)S(1)}) custom-call(f32[19,14,16,128]{3,2,1,0:T(8,128)S(1)} %get-tuple-element.41.post, f32[5,14,16,128]{3,2,1,0:T(8,128)S(1)} %collective-permute-done.7.edge, f32[14,48,128]{2,1,0:T(8,128)S(1)} %get-tuple-element.43.force), custom_call_target="tpu_custom_call" | custom-call | tf_op jit(solution)/shard_map/flow/pallas_call | solution.py:716
  54.3 1.0 %collective-permute-start.8 = (f32[6,48,128]{2,1,0:T(8,128)S(1)}, f32[6,48,128]{2,1,0:T(8,128)S(1)}, u32[]{:S(2)}, u32[]{:S(2)}) collective-permute-start(f32[6,48,128]{2,1,0:T(8,128)S(1)} %get-tuple-element.44), channel_id=1, source_target_pairs={{0,4},{4,8},{8,12},{12,0},{1,5},{5,9},{9,13},{13,1},{2,6},{6,10},{... | collective-permute-start | bytes 442376 | tf_op jit(solution)/shard_map/ppermute | solution.py:585
  55.4 2.9 %collective-permute-start.9 = (f32[5,48,128]{2,1,0:T(8,128)S(1)}, f32[5,48,128]{2,1,0:T(8,128)S(1)}, u32[]{:S(2)}, u32[]{:S(2)}) collective-permute-start(f32[5,48,128]{2,1,0:T(8,128)S(1)} %get-tuple-element.45), channel_id=1, source_target_pairs={{0,12},{4,0},{8,4},{12,8},{1,13},{5,1},{9,5},{13,9},{2,14},{6,2},{... | collective-permute-start | bytes 368648 | tf_op jit(solution)/shard_map/ppermute | solution.py:585
  58.2 2.4 %renew.1 = f32[12,12,19,128]{3,2,1,0:T(8,128)} custom-call(f32[19,14,16,128]{3,2,1,0:T(8,128)S(1)} %get-tuple-element.41.post, f32[5,14,16,128]{3,2,1,0:T(8,128)S(1)} %collective-permute-done.7.edge, f32[12,48,128]{2,1,0:T(8,128)S(1)} %get-tuple-element.46.after.own), custom_call_target="tpu_custom_call" | custom-call | tf_op jit(solution)/shard_map/renew/pallas_call | solution.py:725
  60.6 3.7 %collective-permute-done.9.high_side = f32[5,48,128]{2,1,0:T(8,128)S(1)} collective-permute-done((f32[5,48,128]{2,1,0:T(8,128)S(1)}, f32[5,48,128]{2,1,0:T(8,128)S(1)}, u32[]{:S(2)}, u32[]{:S(2)}) %collective-permute-start.9) | collective-permute-done | bytes 122912 | tf_op jit(solution)/shard_map/ppermute | solution.py:585
  64.8 1.0 %collective-permute-done.12.high_far = f32[5,48,128]{2,1,0:T(8,128)S(1)} collective-permute-done((f32[5,48,128]{2,1,0:T(8,128)S(1)}, f32[5,48,128]{2,1,0:T(8,128)S(1)}, u32[]{:S(2)}, u32[]{:S(2)}) %collective-permute-start.12) | collective-permute-done | bytes 122912 | tf_op jit(solution)/shard_map/ppermute | solution.py:585
  65.8 4.8 %sample.3 = f32[3,16,768]{2,1,0:T(8,128)S(1)} custom-call(s32[24,3]{1,0:T(8,128)S(1)} %get-tuple-element.51.corner, f32[3,24,768]{2,1,0:T(8,128)S(1)} %get-tuple-element.40.refs_1_.pos, f32[6,48,128]{2,1,0:T(8,128)S(1)} %collective-permute-done.8.low_side, f32[12,48,128]{2,1,0:T(8,128)S(1)} %get-tuple-element.46.after.own, ...), custom_call_target="tpu_custom_call" | custom-call | flops 2000000000 | bytes 4000000 | tf_op jit(solution)/shard_map/sample/pallas_call | solution.py:446
  71.3 4.8 %sample.2 = f32[3,16,768]{2,1,0:T(8,128)S(1)} custom-call(s32[24,3]{1,0:T(8,128)S(1)} %get-tuple-element.48.corner, f32[3,24,768]{2,1,0:T(8,128)S(1)} %get-tuple-element.39.refs_0_.pos, f32[6,48,128]{2,1,0:T(8,128)S(1)} %collective-permute-done.8.low_side, f32[12,48,128]{2,1,0:T(8,128)S(1)} %get-tuple-element.46.after.own, ...), custom_call_target="tpu_custom_call" | custom-call | flops 2000000000 | bytes 4000000 | tf_op jit(solution)/shard_map/sample/pallas_call | solution.py:446
  (44 shorter events, 7.3 us)
Async XLA Ops:
  0.6 14.5 %copy-start.1 = (f32[16,768]{1,0:T(8,128)S(1)}, f32[16,768]{1,0:T(8,128)}, u32[]{:S(2)}) copy-start(f32[16,768]{1,0:T(8,128)} %constant.35.clone.refs_2_) | copy-start | bytes 147460
  0.6 14.5 %copy-start = (f32[19,12,12,128]{3,0,2,1:T(8,128)S(1)}, f32[19,12,12,128]{3,0,2,1:T(8,128)}, u32[]{:S(2)}) copy-start(f32[19,12,12,128]{3,0,2,1:T(8,128)} %param.5) | copy-start | bytes 4202500
  2.6 6.8 %collective-permute-start = (f32[3,16,768]{2,1,0:T(8,128)S(1)}, f32[3,16,768]{2,1,0:T(8,128)S(1)}, u32[]{:S(2)}, u32[]{:S(2)}) collective-permute-start(f32[3,16,768]{2,1,0:T(8,128)S(1)} %maximum_maximum_fusion.refs_0_.refs_3_.refs_2_), channel_id=1, source_target_pairs={{0,2},{2,0},{1,3},{3,1},{4,6},{6,4},{5,7},{7,5},{8,10},{10,8},{9,1... | collective-permute-start | bytes 442376 | tf_op jit(solution)/shard_map/ppermute | solution.py:585
  11.2 15.1 %collective-permute-start.1 = (f32[440,128]{1,0:T(8,128)S(1)}, f32[440,128]{1,0:T(8,128)S(1)}, u32[]{:S(2)}, u32[]{:S(2)}) collective-permute-start(f32[440,128]{1,0:T(8,128)S(1)} %get-tuple-element.27), channel_id=1, source_target_pairs={{0,4},{4,8},{8,12},{12,0},{1,5},{5,9},{9,13},{13,1},{2,6},{6,10},{... | collective-permute-start | bytes 675848 | tf_op jit(solution)/shard_map/ppermute | solution.py:585
  13.1 13.3 %collective-permute-start.2 = (f32[440,128]{1,0:T(8,128)S(1)}, f32[440,128]{1,0:T(8,128)S(1)}, u32[]{:S(2)}, u32[]{:S(2)}) collective-permute-start(f32[440,128]{1,0:T(8,128)S(1)} %get-tuple-element.28), channel_id=1, source_target_pairs={{0,12},{4,0},{8,4},{12,8},{1,13},{5,1},{9,5},{13,9},{2,14},{6,2},{... | collective-permute-start | bytes 675848 | tf_op jit(solution)/shard_map/ppermute | solution.py:585
  27.2 15.3 %collective-permute-start.3 = (f32[2,14,19,128]{3,2,1,0:T(8,128)}, f32[2,14,19,128]{3,2,1,0:T(8,128)S(1)}, u32[]{:S(2)}, u32[]{:S(2)}) collective-permute-start(f32[2,14,19,128]{3,2,1,0:T(8,128)} %pad_maximum_fusion), channel_id=1, source_target_pairs={{0,2},{2,0},{1,3},{3,1},{4,6},{6,4},{5,7},{7,5},{8,10},{10,8},{9,1... | collective-permute-start | bytes 817160 | tf_op jit(solution)/shard_map/ppermute | solution.py:585
  29.0 5.9 %copy-start.2 = (s32[4,4]{1,0:T(4,128)}, s32[4,4]{1,0:T(4,128)S(1)}, u32[]{:S(2)}) copy-start(s32[4,4]{1,0:T(4,128)S(1)} %get-tuple-element.57) | copy-start | bytes 196
  34.9 1.3 %collective-permute-start.4 = (f32[3,48,128]{2,1,0:T(8,128)S(1)}, f32[3,48,128]{2,1,0:T(8,128)S(1)}, u32[]{:S(2)}, u32[]{:S(2)}) collective-permute-start(f32[3,48,128]{2,1,0:T(8,128)S(1)} %get-tuple-element.35), channel_id=1, source_target_pairs={{0,1},{1,0},{2,3},{3,2},{4,5},{5,4},{6,7},{7,6},{8,9},{9,8},{10,11... | collective-permute-start | bytes 221192 | tf_op jit(solution)/shard_map/ppermute | solution.py:585
  37.1 10.5 %collective-permute-start.6 = (f32[7,48,128]{2,1,0:T(8,128)}, f32[7,48,128]{2,1,0:T(8,128)}, u32[]{:S(2)}, u32[]{:S(2)}) collective-permute-start(f32[7,48,128]{2,1,0:T(8,128)} %get-tuple-element.38), channel_id=1, source_target_pairs={{0,12},{4,0},{8,4},{12,8},{1,13},{5,1},{9,5},{13,9},{2,14},{6,2},{... | collective-permute-start | bytes 516104 | tf_op jit(solution)/shard_map/ppermute | solution.py:585
  38.7 9.0 %collective-permute-start.5 = (f32[6,48,128]{2,1,0:T(8,128)}, f32[6,48,128]{2,1,0:T(8,128)}, u32[]{:S(2)}, u32[]{:S(2)}) collective-permute-start(f32[6,48,128]{2,1,0:T(8,128)} %get-tuple-element.37), channel_id=1, source_target_pairs={{0,4},{4,8},{8,12},{12,0},{1,5},{5,9},{9,13},{13,1},{2,6},{6,10},{... | collective-permute-start | bytes 442376 | tf_op jit(solution)/shard_map/ppermute | solution.py:585
  50.9 2.0 %collective-permute-start.7 = (f32[5,14,16,128]{3,2,1,0:T(8,128)S(1)}, f32[5,14,16,128]{3,2,1,0:T(8,128)S(1)}, u32[]{:S(2)}, u32[]{:S(2)}) collective-permute-start(f32[5,14,16,128]{3,2,1,0:T(8,128)S(1)} %get-tuple-element.42), channel_id=1, source_target_pairs={{0,1},{1,0},{2,3},{3,2},{4,5},{5,4},{6,7},{7,6},{8,9},{9,8},{10,11... | collective-permute-start | bytes 1720328 | tf_op jit(solution)/shard_map/ppermute | solution.py:585
  54.3 9.9 %collective-permute-start.8 = (f32[6,48,128]{2,1,0:T(8,128)S(1)}, f32[6,48,128]{2,1,0:T(8,128)S(1)}, u32[]{:S(2)}, u32[]{:S(2)}) collective-permute-start(f32[6,48,128]{2,1,0:T(8,128)S(1)} %get-tuple-element.44), channel_id=1, source_target_pairs={{0,4},{4,8},{8,12},{12,0},{1,5},{5,9},{9,13},{13,1},{2,6},{6,10},{... | collective-permute-start | bytes 442376 | tf_op jit(solution)/shard_map/ppermute | solution.py:585
  55.4 10.5 %collective-permute-start.11 = (f32[12,48,128]{2,1,0:T(8,128)S(1)}, f32[12,48,128]{2,1,0:T(8,128)S(1)}, u32[]{:S(2)}, u32[]{:S(2)}) collective-permute-start(f32[12,48,128]{2,1,0:T(8,128)S(1)} %get-tuple-element.46.after.own), channel_id=1, source_target_pairs={{0,1},{1,0},{2,3},{3,2},{4,5},{5,4},{6,7},{7,6},{8,9},{9,8},{10,11... | collective-permute-start | bytes 884744 | tf_op jit(solution)/shard_map/ppermute | solution.py:585
  55.4 8.9 %collective-permute-start.9 = (f32[5,48,128]{2,1,0:T(8,128)S(1)}, f32[5,48,128]{2,1,0:T(8,128)S(1)}, u32[]{:S(2)}, u32[]{:S(2)}) collective-permute-start(f32[5,48,128]{2,1,0:T(8,128)S(1)} %get-tuple-element.45), channel_id=1, source_target_pairs={{0,12},{4,0},{8,4},{12,8},{1,13},{5,1},{9,5},{13,9},{2,14},{6,2},{... | collective-permute-start | bytes 368648 | tf_op jit(solution)/shard_map/ppermute | solution.py:585
  64.3 1.6 %collective-permute-start.10 = (f32[6,48,128]{2,1,0:T(8,128)S(1)}, f32[6,48,128]{2,1,0:T(8,128)S(1)}, u32[]{:S(2)}, u32[]{:S(2)}) collective-permute-start(f32[6,48,128]{2,1,0:T(8,128)S(1)} %collective-permute-done.8.low_side), channel_id=1, source_target_pairs={{0,1},{1,0},{2,3},{3,2},{4,5},{5,4},{6,7},{7,6},{8,9},{9,8},{10,11... | collective-permute-start | bytes 442376 | tf_op jit(solution)/shard_map/ppermute | solution.py:585
  64.3 1.5 %collective-permute-start.12 = (f32[5,48,128]{2,1,0:T(8,128)S(1)}, f32[5,48,128]{2,1,0:T(8,128)S(1)}, u32[]{:S(2)}, u32[]{:S(2)}) collective-permute-start(f32[5,48,128]{2,1,0:T(8,128)S(1)} %collective-permute-done.9.high_side), channel_id=1, source_target_pairs={{0,1},{1,0},{2,3},{3,2},{4,5},{5,4},{6,7},{7,6},{8,9},{9,8},{10,11... | collective-permute-start | bytes 368648 | tf_op jit(solution)/shard_map/ppermute | solution.py:585
  70.7 6.1 %collective-permute-start.13 = (f32[3,16,768]{2,1,0:T(8,128)S(1)}, f32[3,16,768]{2,1,0:T(8,128)S(1)}, u32[]{:S(2)}, u32[]{:S(2)}) collective-permute-start(f32[3,16,768]{2,1,0:T(8,128)S(1)} %sample.3), channel_id=1, source_target_pairs={{0,2},{2,0},{1,3},{3,1},{4,6},{6,4},{5,7},{7,5},{8,10},{10,8},{9,1... | collective-permute-start | bytes 442376 | tf_op jit(solution)/shard_map/ppermute | solution.py:585

commit v4 on v3

--- a/solution.py
+++ b/solution.py
@@ -48,20 +48,29 @@
     return jnp.asarray(table, F32)
 
 
-def pack_kernel(capacity, slabs, plane, groups, here, infos, *refs):
-    cells, (sides, up, down) = refs[:groups], refs[groups:]
-    ny, directions = sides.shape[1:3]
+def pack_kernel(capacity, slabs, plane, groups, begun, here, infos, *refs):
     tiles = WIDTH // 128
     held = 3 * tiles * MIG
-    spare = up.shape[0] - 8
-    up[0 : groups * held, :] = jnp.full((groups * held, 128), -1.0, F32)
-    down[0 : groups * held, :] = jnp.full((groups * held, 128), -1.0, F32)
     over = lax.rem(here[0] + 1, slabs)
     under = lax.rem(here[0] + slabs - 1, slabs)
-    for g in range(groups):
+    if begun:
+        cells, (up_begun, down_begun, up, down) = refs[: groups - 1], refs[groups - 1 :]
+        up[...] = up_begun[...]
+        down[...] = down_begun[...]
+    else:
+        cells, (sides, up, down) = refs[:1], refs[1:]
+        up[0 : groups * held, :] = jnp.full((groups * held, 128), -1.0, F32)
+        down[0 : groups * held, :] = jnp.full((groups * held, 128), -1.0, F32)
+        ny, directions = sides.shape[1:3]
+        for n, message in enumerate((up, down)):
+            for y in range(ny):
+                first = groups * held + 24 * y
+                message[first : first + directions, :] = sides[n, y]
+    for n, block in enumerate(cells):
+        g = n + begun
         n_up, n_down = jnp.int32(0), jnp.int32(0)
         for c in range(capacity):
-            owner = infos[g * capacity + c, 0] // capacity
+            owner = infos[n * capacity + c, 0] // capacity
             peer = owner // plane
             leaving = owner != here[3 + g]
             rises = jnp.logical_and(leaving, peer == over)
@@ -72,7 +81,7 @@
             def put(message, start):
                 for a in range(3):
                     for t in range(tiles):
-                        row = cells[g][a, c : c + 1, 128 * t : 128 * t + 128]
+                        row = block[a, c : c + 1, 128 * t : 128 * t + 128]
                         message[pl.ds(start + (a * tiles + t) * MIG, 1), :] = row
 
             @pl.when(rises)
@@ -85,10 +94,6 @@
 
             n_up = n_up + rises.astype(jnp.int32)
             n_down = n_down + falls.astype(jnp.int32)
-    for n, message in enumerate((up, down)):
-        for y in range(ny):
-            first = groups * held + 24 * y
-            message[first : first + directions, :] = sides[n, y]
 
 
 def cell_row(block, offset, r, a):
@@ -158,10 +163,13 @@
         wave[2 * a], wave[2 * a + 1] = waves(pos[a, 0:cells, :])
 
 
-def fill_force(pos, table, force):
+def fill_force(pos, table, wave, force, count):
     cells, width = force.shape[1:]
-    for h in range(cells // 8):
+
+    def some(h):
         rows = slice(8 * h, 8 * h + 8)
+        for a in range(3):
+            wave[2 * a, rows, :], wave[2 * a + 1, rows, :] = waves(pos[a, rows, :])
         x = [pos[a, rows, :] for a in range(3)]
         lap = [jnp.zeros((8, width), F32) for _ in range(3)]
         pulls = []
@@ -183,6 +191,9 @@
                 t = pulls[n][a] - 0.002 * (mask * (pltpu.roll(lap[a], width - s, 1) - lap[a]))
                 total = total + t - pltpu.roll(t, s, 1)
             force[a, rows, :] = total
+
+    for h in range(cells // 8):
+        pl.when(8 * h < count)(functools.partial(some, h))
 
 
 def split(x):
@@ -299,8 +310,7 @@
             count = count + wanted.astype(jnp.int32)
             at += 1
     hide_rest(pos, vertices)
-    fill_waves(pos, wave)
-    fill_force(pos, table, force)
+    fill_force(pos, table, wave, force, count)
 
     def weigh(c, b):
         fill_planar(pos, wave, c, planar.at[b, 0:144], planar.at[b, 144:288])
@@ -618,15 +628,24 @@
     sides = jnp.concatenate([pops[nx - 1 :], pops[:1]])
     held = 3 * (width // 128) * MIG
     message = jax.ShapeDtypeStruct((groups * held + 24 * ny + 8, 128), F32)
-    home = jnp.concatenate([g[0, :, vertices : vertices + 4].astype(jnp.int32) for g in [raw] + guests])
+    theirs = [g[0, :, vertices : vertices + 4].astype(jnp.int32) for g in guests]
     up, down = pl.pallas_call(
-        functools.partial(pack_kernel, capacity, slabs, crosses * subs, groups),
+        functools.partial(pack_kernel, capacity, slabs, crosses * subs, groups, 0),
+        out_shape=(message, message),
+        in_specs=[SMEM, SMEM, VMEM, VMEM],
+        out_specs=(VMEM, VMEM),
+        compiler_params=params(),
+        name="pack",
+    )(here, notes, raw, sides)
+    up, down = pl.pallas_call(
+        functools.partial(pack_kernel, capacity, slabs, crosses * subs, groups, 1),
         out_shape=(message, message),
         in_specs=[SMEM, SMEM] + [VMEM] * (groups + 1),
         out_specs=(VMEM, VMEM),
         compiler_params=params(),
         name="pack",
-    )(here, home, raw, *guests, sides)
+    )(here, jnp.concatenate(theirs), *guests, up, down)
+    home = jnp.concatenate([raw[0, :, vertices : vertices + 4].astype(jnp.int32)] + theirs)
     sizes = (capacity, vertices, extent)
     below, above = shifted(up, "slab", 1), shifted(down, "slab", -1)
     images = [(0,)] + [image for _, image in beside]
@@ -648,11 +667,7 @@
     x_high = above[groups * held : groups * held + 24 * ny].reshape(1, ny, 24, 128)
     first = jnp.concatenate([x_low[:, 0, :19], first, x_high[:, 0, :19]])
     last = jnp.concatenate([x_low[:, -1, :19], last, x_high[:, -1, :19]])
-    if crosses == 2:
-        rows = shifted(jnp.stack([last, first]), "cross", 1)
-        y_low, y_high = (rows, 0), (rows, 1)
-    else:
-        y_low, y_high = (shifted(last, "cross", 1)[None], 0), (shifted(first, "cross", -1)[None], 0)
+    y_low, y_high = (shifted(last, "cross", 1)[None], 0), (shifted(first, "cross", -1)[None], 0)
     lane = vertices - (width - 128)
     starts = [g * held + (width // 128 - 1) * MIG for g in range(groups)]
     notes_in = [m[s : s + MIG, lane : lane + 4].astype(jnp.int32) for s in starts for m in (below, above)]

time: 77.9 us -> 74.1 us (0.951)
  waiting for transfers between devices: 16.2 us -> 10.5 us
  starting transfers between devices: 15.7 us -> 18 us
  Pallas kernels: 39.2 us -> 37.9 us
    ppermute x14 -> x15, waiting for transfers between devices: 16.2 us -> 10.5 us  [shifted(): lax.ppermute(x, axis, [(i, (i + distance) % count) for i in range(count)])]
    ppermute x14 -> x15, starting transfers between devices: 15.7 us -> 18 us  [shifted(): lax.ppermute(x, axis, [(i, (i + distance) % count) for i in range(count)])]
    pallas_call x2, Pallas kernels: 17 us -> 15.3 us  [stage(): pl.pallas_call(functools.partial(stage_kernel, sizes, plan, last, copies,...]
    concatenate x1 -> x3, other arithmetic: 0.01 us -> 1.38 us  [the longest x1 0.69 us: on_device(): first = jnp.concatenate([x_low[:, 0, :19], first, x_high[:, 0, :19]])]
    another operation x2 -> x0, other arithmetic: 0.8 us -> none  [on_device(): rows = shifted(jnp.stack([last, first]), 'cross', 1)]
    pallas_call x1 -> x2, Pallas kernels: 1.66 us -> 2.19 us  [on_device(): pl.pallas_call(functools.partial(pack_kernel, capacity, slabs, crosses *...]
  transfers between devices with their start and end apart: 14 -> 15, of which waited for: 7 -> 6; matrix products, arithmetic and copies ran while one was open for 3% -> 4% of each run, Pallas kernels for 36% -> 31%
where the time goes in v4:
time: 74.1 us; the launch traced here: 73.5 us
  Pallas kernels  37.9 us (51%)
  starting transfers between devices  18 us (24%)
  waiting for transfers between devices  10.5 us (14%)
  other arithmetic  4.13 us (6%)
  local copies, waits for them, and re-layouts  2 us (3%)
  between operations  0.85 us (1%)
    ppermute x15, starting transfers between devices, shifted(): lax.ppermute(x, axis, [(i, (i + distance) % count) for i in range(count)])  18 us
    pallas_call x2, Pallas kernels, stage(): pl.pallas_call(functools.partial(stage_kernel, sizes, plan, last, copies,...  15.3 us
    ppermute x15, waiting for transfers between devices, shifted(): lax.ppermute(x, axis, [(i, (i + distance) % count) for i in range(count)])  10.5 us
    pallas_call x2, Pallas kernels, sampled(): pl.pallas_call(functools.partial(sample_kernel, images), out_shape=jax.Sh...  9.64 us
    pallas_call x1, Pallas kernels, on_device(): pl.pallas_call(collide_kernel, out_shape=(jax.ShapeDtypeStruct((19, plane...  3.21 us
    pallas_call x1, Pallas kernels, on_device(): pl.pallas_call(functools.partial(assemble_kernel, sizes, groups, offsets)...  2.63 us
    pallas_call x1, Pallas kernels, on_device(): pl.pallas_call(renew_kernel, out_shape=jax.ShapeDtypeStruct((nx, ny, 19,...  2.37 us
    pallas_call x2, Pallas kernels, on_device(): pl.pallas_call(functools.partial(pack_kernel, capacity, slabs, crosses *...  2.19 us
  transfers between devices with their start and end apart: 15, of which 6 were waited for; matrix products, arithmetic and copies ran while one was open for 4% of the time, Pallas kernels for 31%

profile of v4, /device:TPU:0, one launch (start us, length us, event | category | flops | bytes accessed | tf_op | source)
XLA Modules:
  0.0 73.5 jit_solution(5699719287982106293)
XLA Ops:
  1.7 1.0 %maximum_maximum_fusion.refs_0_.refs_3_.refs_2_ = f32[3,16,768]{2,1,0:T(8,128)S(1)} fusion(f32[3,16,4]{2,1,0:T(8,128)S(1)} %broadcast_in_dim.16, f32[3,16,642]{2,1,0:T(8,128)} %bitcast.35, f32[768]{0:T(1024)S(1)} %pad.16.clone), kind=kLoop, calls=%fused_computation.5 | loop fusion | flops 73728 | bytes 274560 | tf_op jit(solution)/shard_map/concatenate | solution.py:609
  2.6 2.9 %collective-permute-start = (f32[3,16,768]{2,1,0:T(8,128)S(1)}, f32[3,16,768]{2,1,0:T(8,128)S(1)}, u32[]{:S(2)}, u32[]{:S(2)}) collective-permute-start(f32[3,16,768]{2,1,0:T(8,128)S(1)} %maximum_maximum_fusion.refs_0_.refs_3_.refs_2_), channel_id=1, source_target_pairs={{0,2},{2,0},{1,3},{3,1},{4,6},{6,4},{5,7},{7,5},{8,10},{10,8},{9,1... | collective-permute-start | bytes 442376 | tf_op jit(solution)/shard_map/ppermute | solution.py:595
  5.6 1.0 %fusion.2 = (f32[1,12,19,128]{3,2,1,0:T(8,128)S(1)}, f32[1,12,19,128]{3,2,1,0:T(8,128)S(1)}) fusion(f32[12,12,19,128]{3,2,1,0:T(8,128)} %bitcast.25), kind=kLoop, calls=%fused_computation.20 | loop fusion | bytes 466944 | tf_op jit(solution)/shard_map/slice | solution.py:628
  6.7 1.1 %pack.2 = (f32[440,128]{1,0:T(8,128)S(1)}, f32[440,128]{1,0:T(8,128)S(1)}) custom-call(s32[5]{0:T(128)S(1)} %stack.23.here.refs_0_, s32[16,4]{1,0:T(8,128)S(1)} %copy.41.infos, f32[3,16,768]{2,1,0:T(8,128)S(1)} %maximum_maximum_fusion.refs_0_.refs_3_.refs_2_, f32[2,12,19,128]{3,2,1,0:T(8,128)S(1)} %pad_maximum_fusion.refs_1_), custom_call_target="tpu_custom_call" | custom-call | tf_op jit(solution)/shard_map/pack/pallas_call | solution.py:632
  7.8 1.6 %collective-permute-done.refs_0_.refs_4_.refs_5_ = f32[3,16,768]{2,1,0:T(8,128)S(1)} collective-permute-done((f32[3,16,768]{2,1,0:T(8,128)S(1)}, f32[3,16,768]{2,1,0:T(8,128)S(1)}, u32[]{:S(2)}, u32[]{:S(2)}) %collective-permute-start) | collective-permute-done | bytes 147488 | tf_op jit(solution)/shard_map/ppermute | solution.py:595
  9.5 1.1 %pack.3 = (f32[440,128]{1,0:T(8,128)S(1)}, f32[440,128]{1,0:T(8,128)S(1)}) custom-call(s32[5]{0:T(128)S(1)} %stack.23.here.refs_0_, s32[16,4]{1,0:T(8,128)S(1)} %fusion.1.infos, f32[3,16,768]{2,1,0:T(8,128)S(1)} %collective-permute-done.refs_0_.refs_4_.refs_5_, f32[440,128]{1,0:T(8,128)S(1)} %get-tuple-element.29.refs_1_, ...), custom_call_target="tpu_custom_call" | custom-call | tf_op jit(solution)/shard_map/pack/pallas_call | solution.py:640
  10.6 1.9 %collective-permute-start.1 = (f32[440,128]{1,0:T(8,128)S(1)}, f32[440,128]{1,0:T(8,128)S(1)}, u32[]{:S(2)}, u32[]{:S(2)}) collective-permute-start(f32[440,128]{1,0:T(8,128)S(1)} %get-tuple-element.31), channel_id=1, source_target_pairs={{0,4},{4,8},{8,12},{12,0},{1,5},{5,9},{9,13},{13,1},{2,6},{6,10},{... | collective-permute-start | bytes 675848 | tf_op jit(solution)/shard_map/ppermute | solution.py:595
  12.5 2.1 %collective-permute-start.2 = (f32[440,128]{1,0:T(8,128)S(1)}, f32[440,128]{1,0:T(8,128)S(1)}, u32[]{:S(2)}, u32[]{:S(2)}) collective-permute-start(f32[440,128]{1,0:T(8,128)S(1)} %get-tuple-element.32), channel_id=1, source_target_pairs={{0,12},{4,0},{8,4},{12,8},{1,13},{5,1},{9,5},{13,9},{2,14},{6,2},{... | collective-permute-start | bytes 675848 | tf_op jit(solution)/shard_map/ppermute | solution.py:595
  14.6 10.8 %spread.2 = (f32[24,152,48]{2,1,0:T(8,128)S(1)}, f32[12,19,128]{2,1,0:T(8,128)S(1)}, f32[12,19,128]{2,1,0:T(8,128)S(1)}) custom-call(s32[5]{0:T(128)S(1)} %stack.23.here.refs_0_, s32[32,4]{1,0:T(8,128)S(1)} %pad_add_fusion.refs_1_, f32[16,768]{1,0:T(8,128)S(1)} %copy-done.1, f32[3,16,768]{2,1,0:T(8,128)S(1)} %maximum_maximum_fusion.refs_0_.refs_3_.refs_2_, ...), custom_call_target="tpu_custom_call" | custom-call | flops 4000000000 | bytes 4000000 | tf_op jit(solution)/shard_map/spread/pallas_call | solution.py:361
  25.6 4.5 %spread.3 = (f32[14,48,128]{2,1,0:T(8,128)S(1)}, f32[7,48,128]{2,1,0:T(8,128)S(1)}, f32[6,48,128]{2,1,0:T(8,128)S(1)}, f32[3,48,128]{2,1,0:T(8,128)S(1)}) custom-call(s32[5]{0:T(128)S(1)} %stack.23.here.refs_0_, s32[16,4]{1,0:T(8,128)S(1)} %pad_add_fusion.1.refs_1_, f32[16,768]{1,0:T(8,128)S(1)} %copy-done.1, ...), custom_call_target="tpu_custom_call" | custom-call | flops 4000000000 | bytes 4000000 | tf_op jit(solution)/shard_map/spread/pallas_call | solution.py:361
  30.9 1.7 %collective-permute-start.4 = (f32[14,19,128]{2,1,0:T(8,128)}, f32[14,19,128]{2,1,0:T(8,128)S(1)}, u32[]{:S(2)}, u32[]{:S(2)}) collective-permute-start(f32[14,19,128]{2,1,0:T(8,128)} %pad_maximum_fusion.2), channel_id=1, source_target_pairs={{0,2},{2,0},{1,3},{3,1},{4,6},{6,4},{5,7},{7,5},{8,10},{10,8},{9,1... | collective-permute-start | bytes 408584 | tf_op jit(solution)/shard_map/ppermute | solution.py:595
  32.6 0.9 %fold.1 = (f32[14,48,128]{2,1,0:T(8,128)S(1)}, f32[7,48,128]{2,1,0:T(8,128)}, f32[6,48,128]{2,1,0:T(8,128)}) custom-call(f32[14,48,128]{2,1,0:T(8,128)S(1)} %get-tuple-element.36.own_in, f32[7,48,128]{2,1,0:T(8,128)S(1)} %get-tuple-element.37.down_in, f32[6,48,128]{2,1,0:T(8,128)S(1)} %get-tuple-element.38.up_in, f32[3,48,128]{2,1,0:T(8,128)S(1)} %collective-permute-done.5.far), custom_call_target="tpu_custom_call" | custom-call | tf_op jit(solution)/shard_map/fold/pallas_call | solution.py:697
  33.5 3.8 %collective-permute-start.7 = (f32[7,48,128]{2,1,0:T(8,128)}, f32[7,48,128]{2,1,0:T(8,128)}, u32[]{:S(2)}, u32[]{:S(2)}) collective-permute-start(f32[7,48,128]{2,1,0:T(8,128)} %get-tuple-element.42), channel_id=1, source_target_pairs={{0,12},{4,0},{8,4},{12,8},{1,13},{5,1},{9,5},{13,9},{2,14},{6,2},{... | collective-permute-start | bytes 516104 | tf_op jit(solution)/shard_map/ppermute | solution.py:595
  39.1 2.6 %assemble.1 = (f32[3,24,768]{2,1,0:T(8,128)S(1)}, f32[3,24,768]{2,1,0:T(8,128)S(1)}, s32[24,3]{1,0:T(8,128)S(1)}, s32[24,3]{1,0:T(8,128)S(1)}) custom-call(s32[5]{0:T(128)S(1)} %stack.23.here.refs_0_, s32[48,4]{1,0:T(8,128)S(1)} %concatenate.39.refs_1_, f32[3,16,768]{2,1,0:T(8,128)S(1)} %maximum_maximum_fusion.refs_0_.refs_3_.refs_2_, ...), custom_call_target="tpu_custom_call" | custom-call | tf_op jit(solution)/shard_map/assemble/pallas_call | solution.py:708
  41.8 2.3 %collective-permute-done.3 = f32[14,19,128]{2,1,0:T(8,128)S(1)} collective-permute-done((f32[14,19,128]{2,1,0:T(8,128)}, f32[14,19,128]{2,1,0:T(8,128)S(1)}, u32[]{:S(2)}, u32[]{:S(2)}) %collective-permute-start.3) | collective-permute-done | bytes 136224 | tf_op jit(solution)/shard_map/ppermute | solution.py:595
  44.5 3.2 %collide.1 = (f32[19,14,16,128]{3,2,1,0:T(8,128)S(1)}, f32[14,48,128]{2,1,0:T(8,128)S(1)}, f32[5,14,16,128]{3,2,1,0:T(8,128)S(1)}) custom-call(f32[19,14,16,128]{3,2,1,0:T(8,128)S(1)} %extend.1.pops, f32[14,48,128]{2,1,0:T(8,128)S(1)} %get-tuple-element.40.refs_8_.own, f32[6,48,128]{2,1,0:T(8,128)} %collective-permute-done.6.from_low, ...), custom_call_target="tpu_custom_call" | custom-call | tf_op jit(solution)/shard_map/collide/pallas_call | solution.py:718
  47.8 2.0 %collective-permute-done.8.edge = f32[5,14,16,128]{3,2,1,0:T(8,128)S(1)} collective-permute-done((f32[5,14,16,128]{3,2,1,0:T(8,128)S(1)}, f32[5,14,16,128]{3,2,1,0:T(8,128)S(1)}, u32[]{:S(2)}, u32[]{:S(2)}) %collective-permute-start.8) | collective-permute-done | bytes 573472 | tf_op jit(solution)/shard_map/ppermute | solution.py:595
  49.7 1.4 %flow.1 = (f32[12,48,128]{2,1,0:T(8,128)S(1)}, f32[6,48,128]{2,1,0:T(8,128)S(1)}, f32[5,48,128]{2,1,0:T(8,128)S(1)}) custom-call(f32[19,14,16,128]{3,2,1,0:T(8,128)S(1)} %get-tuple-element.45.post, f32[5,14,16,128]{3,2,1,0:T(8,128)S(1)} %collective-permute-done.8.edge, f32[14,48,128]{2,1,0:T(8,128)S(1)} %get-tuple-element.47.force), custom_call_target="tpu_custom_call" | custom-call | tf_op jit(solution)/shard_map/flow/pallas_call | solution.py:731
  51.4 3.6 %collective-permute-start.10 = (f32[5,48,128]{2,1,0:T(8,128)S(1)}, f32[5,48,128]{2,1,0:T(8,128)S(1)}, u32[]{:S(2)}, u32[]{:S(2)}) collective-permute-start(f32[5,48,128]{2,1,0:T(8,128)S(1)} %get-tuple-element.49), channel_id=1, source_target_pairs={{0,12},{4,0},{8,4},{12,8},{1,13},{5,1},{9,5},{13,9},{2,14},{6,2},{... | collective-permute-start | bytes 368648 | tf_op jit(solution)/shard_map/ppermute | solution.py:595
  55.0 2.4 %renew.1 = f32[12,12,19,128]{3,2,1,0:T(8,128)} custom-call(f32[19,14,16,128]{3,2,1,0:T(8,128)S(1)} %get-tuple-element.45.post, f32[5,14,16,128]{3,2,1,0:T(8,128)S(1)} %collective-permute-done.8.edge, f32[12,48,128]{2,1,0:T(8,128)S(1)} %get-tuple-element.50.after.own), custom_call_target="tpu_custom_call" | custom-call | tf_op jit(solution)/shard_map/renew/pallas_call | solution.py:740
  57.4 2.9 %collective-permute-done.10.high_side = f32[5,48,128]{2,1,0:T(8,128)S(1)} collective-permute-done((f32[5,48,128]{2,1,0:T(8,128)S(1)}, f32[5,48,128]{2,1,0:T(8,128)S(1)}, u32[]{:S(2)}, u32[]{:S(2)}) %collective-permute-start.10) | collective-permute-done | bytes 122912 | tf_op jit(solution)/shard_map/ppermute | solution.py:595
  60.8 1.0 %collective-permute-done.13.high_far = f32[5,48,128]{2,1,0:T(8,128)S(1)} collective-permute-done((f32[5,48,128]{2,1,0:T(8,128)S(1)}, f32[5,48,128]{2,1,0:T(8,128)S(1)}, u32[]{:S(2)}, u32[]{:S(2)}) %collective-permute-start.13) | collective-permute-done | bytes 122912 | tf_op jit(solution)/shard_map/ppermute | solution.py:595
  61.8 4.8 %sample.3 = f32[3,16,768]{2,1,0:T(8,128)S(1)} custom-call(s32[24,3]{1,0:T(8,128)S(1)} %get-tuple-element.55.corner, f32[3,24,768]{2,1,0:T(8,128)S(1)} %get-tuple-element.44.refs_1_.pos, f32[6,48,128]{2,1,0:T(8,128)S(1)} %collective-permute-done.9.low_side, f32[12,48,128]{2,1,0:T(8,128)S(1)} %get-tuple-element.50.after.own, ...), custom_call_target="tpu_custom_call" | custom-call | flops 2000000000 | bytes 4000000 | tf_op jit(solution)/shard_map/sample/pallas_call | solution.py:456
  67.2 4.8 %sample.2 = f32[3,16,768]{2,1,0:T(8,128)S(1)} custom-call(s32[24,3]{1,0:T(8,128)S(1)} %get-tuple-element.52.corner, f32[3,24,768]{2,1,0:T(8,128)S(1)} %get-tuple-element.43.refs_0_.pos, f32[6,48,128]{2,1,0:T(8,128)S(1)} %collective-permute-done.9.low_side, f32[12,48,128]{2,1,0:T(8,128)S(1)} %get-tuple-element.50.after.own, ...), custom_call_target="tpu_custom_call" | custom-call | flops 2000000000 | bytes 4000000 | tf_op jit(solution)/shard_map/sample/pallas_call | solution.py:456
  (46 shorter events, 7.3 us)
Async XLA Ops:
  0.6 14.0 %copy-start.1 = (f32[16,768]{1,0:T(8,128)S(1)}, f32[16,768]{1,0:T(8,128)}, u32[]{:S(2)}) copy-start(f32[16,768]{1,0:T(8,128)} %constant.35.clone.refs_2_) | copy-start | bytes 147460
  0.6 14.0 %copy-start = (f32[19,12,12,128]{3,0,2,1:T(8,128)S(1)}, f32[19,12,12,128]{3,0,2,1:T(8,128)}, u32[]{:S(2)}) copy-start(f32[19,12,12,128]{3,0,2,1:T(8,128)} %param.5) | copy-start | bytes 4202500
  2.6 6.8 %collective-permute-start = (f32[3,16,768]{2,1,0:T(8,128)S(1)}, f32[3,16,768]{2,1,0:T(8,128)S(1)}, u32[]{:S(2)}, u32[]{:S(2)}) collective-permute-start(f32[3,16,768]{2,1,0:T(8,128)S(1)} %maximum_maximum_fusion.refs_0_.refs_3_.refs_2_), channel_id=1, source_target_pairs={{0,2},{2,0},{1,3},{3,1},{4,6},{6,4},{5,7},{7,5},{8,10},{10,8},{9,1... | collective-permute-start | bytes 442376 | tf_op jit(solution)/shard_map/ppermute | solution.py:595
  10.6 14.8 %collective-permute-start.1 = (f32[440,128]{1,0:T(8,128)S(1)}, f32[440,128]{1,0:T(8,128)S(1)}, u32[]{:S(2)}, u32[]{:S(2)}) collective-permute-start(f32[440,128]{1,0:T(8,128)S(1)} %get-tuple-element.31), channel_id=1, source_target_pairs={{0,4},{4,8},{8,12},{12,0},{1,5},{5,9},{9,13},{13,1},{2,6},{6,10},{... | collective-permute-start | bytes 675848 | tf_op jit(solution)/shard_map/ppermute | solution.py:595
  12.5 13.0 %collective-permute-start.2 = (f32[440,128]{1,0:T(8,128)S(1)}, f32[440,128]{1,0:T(8,128)S(1)}, u32[]{:S(2)}, u32[]{:S(2)}) collective-permute-start(f32[440,128]{1,0:T(8,128)S(1)} %get-tuple-element.32), channel_id=1, source_target_pairs={{0,12},{4,0},{8,4},{12,8},{1,13},{5,1},{9,5},{13,9},{2,14},{6,2},{... | collective-permute-start | bytes 675848 | tf_op jit(solution)/shard_map/ppermute | solution.py:595
  25.5 4.5 %copy-start.2 = (s32[4,4]{1,0:T(4,128)}, s32[4,4]{1,0:T(4,128)S(1)}, u32[]{:S(2)}) copy-start(s32[4,4]{1,0:T(4,128)S(1)} %get-tuple-element.61) | copy-start | bytes 196
  30.1 2.5 %collective-permute-start.5 = (f32[3,48,128]{2,1,0:T(8,128)S(1)}, f32[3,48,128]{2,1,0:T(8,128)S(1)}, u32[]{:S(2)}, u32[]{:S(2)}) collective-permute-start(f32[3,48,128]{2,1,0:T(8,128)S(1)} %get-tuple-element.39), channel_id=1, source_target_pairs={{0,1},{1,0},{2,3},{3,2},{4,5},{5,4},{6,7},{7,6},{8,9},{9,8},{10,11... | collective-permute-start | bytes 221192 | tf_op jit(solution)/shard_map/ppermute | solution.py:595
  30.9 10.9 %collective-permute-start.4 = (f32[14,19,128]{2,1,0:T(8,128)}, f32[14,19,128]{2,1,0:T(8,128)S(1)}, u32[]{:S(2)}, u32[]{:S(2)}) collective-permute-start(f32[14,19,128]{2,1,0:T(8,128)} %pad_maximum_fusion.2), channel_id=1, source_target_pairs={{0,2},{2,0},{1,3},{3,1},{4,6},{6,4},{5,7},{7,5},{8,10},{10,8},{9,1... | collective-permute-start | bytes 408584 | tf_op jit(solution)/shard_map/ppermute | solution.py:595
  33.4 11.0 %collective-permute-start.6 = (f32[6,48,128]{2,1,0:T(8,128)}, f32[6,48,128]{2,1,0:T(8,128)}, u32[]{:S(2)}, u32[]{:S(2)}) collective-permute-start(f32[6,48,128]{2,1,0:T(8,128)} %get-tuple-element.41), channel_id=1, source_target_pairs={{0,4},{4,8},{8,12},{12,0},{1,5},{5,9},{9,13},{13,1},{2,6},{6,10},{... | collective-permute-start | bytes 442376 | tf_op jit(solution)/shard_map/ppermute | solution.py:595
  33.5 11.0 %collective-permute-start.7 = (f32[7,48,128]{2,1,0:T(8,128)}, f32[7,48,128]{2,1,0:T(8,128)}, u32[]{:S(2)}, u32[]{:S(2)}) collective-permute-start(f32[7,48,128]{2,1,0:T(8,128)} %get-tuple-element.42), channel_id=1, source_target_pairs={{0,12},{4,0},{8,4},{12,8},{1,13},{5,1},{9,5},{13,9},{2,14},{6,2},{... | collective-permute-start | bytes 516104 | tf_op jit(solution)/shard_map/ppermute | solution.py:595
  37.9 6.1 %collective-permute-start.3 = (f32[14,19,128]{2,1,0:T(8,128)}, f32[14,19,128]{2,1,0:T(8,128)S(1)}, u32[]{:S(2)}, u32[]{:S(2)}) collective-permute-start(f32[14,19,128]{2,1,0:T(8,128)} %pad_maximum_fusion.1), channel_id=1, source_target_pairs={{0,2},{2,0},{1,3},{3,1},{4,6},{6,4},{5,7},{7,5},{8,10},{10,8},{9,1... | collective-permute-start | bytes 408584 | tf_op jit(solution)/shard_map/ppermute | solution.py:595
  47.7 2.0 %collective-permute-start.8 = (f32[5,14,16,128]{3,2,1,0:T(8,128)S(1)}, f32[5,14,16,128]{3,2,1,0:T(8,128)S(1)}, u32[]{:S(2)}, u32[]{:S(2)}) collective-permute-start(f32[5,14,16,128]{3,2,1,0:T(8,128)S(1)} %get-tuple-element.46), channel_id=1, source_target_pairs={{0,1},{1,0},{2,3},{3,2},{4,5},{5,4},{6,7},{7,6},{8,9},{9,8},{10,11... | collective-permute-start | bytes 1720328 | tf_op jit(solution)/shard_map/ppermute | solution.py:595
  51.1 9.1 %collective-permute-start.9 = (f32[6,48,128]{2,1,0:T(8,128)S(1)}, f32[6,48,128]{2,1,0:T(8,128)S(1)}, u32[]{:S(2)}, u32[]{:S(2)}) collective-permute-start(f32[6,48,128]{2,1,0:T(8,128)S(1)} %get-tuple-element.48), channel_id=1, source_target_pairs={{0,4},{4,8},{8,12},{12,0},{1,5},{5,9},{9,13},{13,1},{2,6},{6,10},{... | collective-permute-start | bytes 442376 | tf_op jit(solution)/shard_map/ppermute | solution.py:595
  51.3 10.5 %collective-permute-start.12 = (f32[12,48,128]{2,1,0:T(8,128)S(1)}, f32[12,48,128]{2,1,0:T(8,128)S(1)}, u32[]{:S(2)}, u32[]{:S(2)}) collective-permute-start(f32[12,48,128]{2,1,0:T(8,128)S(1)} %get-tuple-element.50.after.own), channel_id=1, source_target_pairs={{0,1},{1,0},{2,3},{3,2},{4,5},{5,4},{6,7},{7,6},{8,9},{9,8},{10,11... | collective-permute-start | bytes 884744 | tf_op jit(solution)/shard_map/ppermute | solution.py:595
  51.4 8.8 %collective-permute-start.10 = (f32[5,48,128]{2,1,0:T(8,128)S(1)}, f32[5,48,128]{2,1,0:T(8,128)S(1)}, u32[]{:S(2)}, u32[]{:S(2)}) collective-permute-start(f32[5,48,128]{2,1,0:T(8,128)S(1)} %get-tuple-element.49), channel_id=1, source_target_pairs={{0,12},{4,0},{8,4},{12,8},{1,13},{5,1},{9,5},{13,9},{2,14},{6,2},{... | collective-permute-start | bytes 368648 | tf_op jit(solution)/shard_map/ppermute | solution.py:595
  60.2 1.6 %collective-permute-start.11 = (f32[6,48,128]{2,1,0:T(8,128)S(1)}, f32[6,48,128]{2,1,0:T(8,128)S(1)}, u32[]{:S(2)}, u32[]{:S(2)}) collective-permute-start(f32[6,48,128]{2,1,0:T(8,128)S(1)} %collective-permute-done.9.low_side), channel_id=1, source_target_pairs={{0,1},{1,0},{2,3},{3,2},{4,5},{5,4},{6,7},{7,6},{8,9},{9,8},{10,11... | collective-permute-start | bytes 442376 | tf_op jit(solution)/shard_map/ppermute | solution.py:595
  60.2 1.5 %collective-permute-start.13 = (f32[5,48,128]{2,1,0:T(8,128)S(1)}, f32[5,48,128]{2,1,0:T(8,128)S(1)}, u32[]{:S(2)}, u32[]{:S(2)}) collective-permute-start(f32[5,48,128]{2,1,0:T(8,128)S(1)} %collective-permute-done.10.high_side), channel_id=1, source_target_pairs={{0,1},{1,0},{2,3},{3,2},{4,5},{5,4},{6,7},{7,6},{8,9},{9,8},{10,11... | collective-permute-start | bytes 368648 | tf_op jit(solution)/shard_map/ppermute | solution.py:595
  66.7 6.1 %collective-permute-start.14 = (f32[3,16,768]{2,1,0:T(8,128)S(1)}, f32[3,16,768]{2,1,0:T(8,128)S(1)}, u32[]{:S(2)}, u32[]{:S(2)}) collective-permute-start(f32[3,16,768]{2,1,0:T(8,128)S(1)} %sample.3), channel_id=1, source_target_pairs={{0,2},{2,0},{1,3},{3,1},{4,6},{6,4},{5,7},{7,5},{8,10},{10,8},{9,1... | collective-permute-start | bytes 442376 | tf_op jit(solution)/shard_map/ppermute | solution.py:595

commit v5 on v4

--- a/solution.py
+++ b/solution.py
@@ -115,8 +115,8 @@
         pos[a, :, width - 128 :] = jnp.where(lane < vertices, pos[a, :, width - 128 :], FAR)
 
 
-def assemble(capacity, vertices, extent, owner, infos, sources, pos, corner):
-    for first, block, offset, migrated in sources:
+def assemble(capacity, vertices, extent, owner, sources, pos, corner):
+    for infos, first, block, offset, migrated in sources:
         for r in range(cell_count(block)):
             target = infos[first + r, 0]
             wanted = target >= 0 if migrated else target // capacity == owner
@@ -130,17 +130,18 @@
 
 def assemble_kernel(sizes, groups, offsets, *refs):
     capacity, vertices, extent = sizes
-    here, infos = refs[:2]
+    here, home, came = refs[:3]
+    refs = refs[1:]
     cells = refs[2 : 2 + 3 * groups]
     positions, corners = refs[3 + 3 * groups : 3 + 4 * groups], refs[3 + 4 * groups :]
     for g in range(groups):
-        start = groups * capacity + g * 2 * MIG
+        start = g * 2 * MIG
         sources = [
-            (g * capacity, cells[3 * g], 0, False),
-            (start, cells[3 * g + 1], offsets[3 * g + 1], True),
-            (start + MIG, cells[3 * g + 2], offsets[3 * g + 2], True),
+            (home, g * capacity, cells[3 * g], 0, False),
+            (came, start, cells[3 * g + 1], offsets[3 * g + 1], True),
+            (came, start + MIG, cells[3 * g + 2], offsets[3 * g + 2], True),
         ]
-        assemble(capacity, vertices, extent, here[3 + g], infos, sources, positions[g], corners[g])
+        assemble(capacity, vertices, extent, here[3 + g], sources, positions[g], corners[g])
 
 
 def wide(tile, width):
@@ -671,11 +672,12 @@
     lane = vertices - (width - 128)
     starts = [g * held + (width // 128 - 1) * MIG for g in range(groups)]
     notes_in = [m[s : s + MIG, lane : lane + 4].astype(jnp.int32) for s in starts for m in (below, above)]
+    came = jnp.concatenate(notes_in)
     own, down_force, up_force, far = stage(
         sizes,
         [(n, None, images[g], g * held) for g in range(groups) for n in (0, 1)],
         here,
-        jnp.concatenate(notes_in),
+        came,
         table,
         [below, above],
         sums=(sum_1,),
@@ -709,11 +711,11 @@
         functools.partial(assemble_kernel, sizes, groups, offsets),
         out_shape=(jax.ShapeDtypeStruct((3, capacity + 8, width), F32),) * groups
         + (jax.ShapeDtypeStruct((capacity + 8, 3), jnp.int32),) * groups,
-        in_specs=[SMEM, SMEM] + [VMEM] * len(cells) + [pl.BlockSpec(memory_space=pl.ANY)],
+        in_specs=[SMEM] * 3 + [VMEM] * len(cells) + [pl.BlockSpec(memory_space=pl.ANY)],
         out_specs=(VMEM,) * groups + (SMEM,) * groups,
         compiler_params=params(),
         name="assemble",
-    )(here, jnp.concatenate([home] + notes_in), *cells, own)
+    )(here, home, came, *cells, own)
     positions, corners = placed[:groups], placed[groups:]
     post, force, edge = pl.pallas_call(
         collide_kernel,

time: 74.1 us -> 71.4 us (0.964)
  Pallas kernels: 37.9 us -> 35.9 us
  starting transfers between devices: 18 us -> 19.3 us
  other arithmetic: 4.13 us -> 2.86 us
    ppermute x15, starting transfers between devices: 18 us -> 19.3 us  [shifted(): lax.ppermute(x, axis, [(i, (i + distance) % count) for i in range(count)])]
    pallas_call x1, Pallas kernels: 3.21 us -> 2.21 us  [on_device(): pl.pallas_call(collide_kernel, out_shape=(jax.ShapeDtypeStruct((19, plane...]
    concatenate x2 -> x1, other arithmetic: 0.83 us -> 0.01 us  [on_device(): came = jnp.concatenate(notes_in)]
    convert_element_type x1, other arithmetic: 0.01 us -> 0.83 us  [on_device(): raw[0, :, vertices:vertices + 4].astype(jnp.int32)]
  transfers between devices with their start and end apart: 15 -> 15, of which waited for: 6 -> 7; matrix products, arithmetic and copies ran while one was open for 4% -> 2% of each run, Pallas kernels for 31% -> 29%
where the time goes in v5:
time: 71.4 us
  Pallas kernels  35.9 us (50%)
  starting transfers between devices  19.3 us (27%)
  waiting for transfers between devices  10.8 us (15%)
  other arithmetic  2.86 us (4%)
  local copies, waits for them, and re-layouts  1.64 us (2%)
  between operations  0.85 us (1%)
    ppermute x15, starting transfers between devices, shifted(): lax.ppermute(x, axis, [(i, (i + distance) % count) for i in range(count)])  19.3 us
    pallas_call x2, Pallas kernels, stage(): pl.pallas_call(functools.partial(stage_kernel, sizes, plan, last, copies,...  14.9 us
    ppermute x15, waiting for transfers between devices, shifted(): lax.ppermute(x, axis, [(i, (i + distance) % count) for i in range(count)])  10.8 us
    pallas_call x2, Pallas kernels, sampled(): pl.pallas_call(functools.partial(sample_kernel, images), out_shape=jax.Sh...  9.67 us
    pallas_call x1, Pallas kernels, on_device(): pl.pallas_call(functools.partial(assemble_kernel, sizes, groups, offsets)...  2.63 us
    pallas_call x1, Pallas kernels, on_device(): pl.pallas_call(renew_kernel, out_shape=jax.ShapeDtypeStruct((nx, ny, 19,...  2.37 us
    pallas_call x1, Pallas kernels, on_device(): pl.pallas_call(collide_kernel, out_shape=(jax.ShapeDtypeStruct((19, plane...  2.21 us
    pallas_call x2, Pallas kernels, on_device(): pl.pallas_call(functools.partial(pack_kernel, capacity, slabs, crosses *...  2.19 us
  transfers between devices with their start and end apart: 15, of which 7 were waited for; matrix products, arithmetic and copies ran while one was open for 2% of the time, Pallas kernels for 29%

profile of v5, /device:TPU:0, one launch (start us, length us, event | category | flops | bytes accessed | tf_op | source)
XLA Modules:
  0.0 71.4 jit_solution(7502369938536409025)
XLA Ops:
  2.6 2.9 %collective-permute-start = (f32[3,16,768]{2,1,0:T(8,128)S(1)}, f32[3,16,768]{2,1,0:T(8,128)S(1)}, u32[]{:S(2)}, u32[]{:S(2)}) collective-permute-start(f32[3,16,768]{2,1,0:T(8,128)S(1)} %maximum_maximum_fusion.refs_0_.refs_3_), channel_id=1, source_target_pairs={{0,2},{2,0},{1,3},{3,1},{4,6},{6,4},{5,7},{7,5},{8,10},{10,8},{9,1... | collective-permute-start | bytes 442376 | tf_op jit(solution)/shard_map/ppermute | solution.py:596
  6.8 1.1 %pack.2 = (f32[440,128]{1,0:T(8,128)S(1)}, f32[440,128]{1,0:T(8,128)S(1)}) custom-call(s32[5]{0:T(128)S(1)} %stack.23.here.refs_0_, s32[16,4]{1,0:T(8,128)S(1)} %copy.32.infos, f32[3,16,768]{2,1,0:T(8,128)S(1)} %maximum_maximum_fusion.refs_0_.refs_3_, f32[2,12,19,128]{3,2,1,0:T(8,128)S(1)} %pad_maximum_fusion.refs_1_), custom_call_target="tpu_custom_call" | custom-call | tf_op jit(solution)/shard_map/pack/pallas_call | solution.py:633
  7.9 1.5 %collective-permute-done.refs_0_.refs_4_.refs_6_ = f32[3,16,768]{2,1,0:T(8,128)S(1)} collective-permute-done((f32[3,16,768]{2,1,0:T(8,128)S(1)}, f32[3,16,768]{2,1,0:T(8,128)S(1)}, u32[]{:S(2)}, u32[]{:S(2)}) %collective-permute-start) | collective-permute-done | bytes 147488 | tf_op jit(solution)/shard_map/ppermute | solution.py:596
  9.9 1.1 %pack.3 = (f32[440,128]{1,0:T(8,128)S(1)}, f32[440,128]{1,0:T(8,128)S(1)}) custom-call(s32[5]{0:T(128)S(1)} %stack.23.here.refs_0_, s32[16,4]{1,0:T(8,128)S(1)} %copy.33.infos, f32[3,16,768]{2,1,0:T(8,128)S(1)} %collective-permute-done.refs_0_.refs_4_.refs_6_, f32[440,128]{1,0:T(8,128)S(1)} %get-tuple-element.29.refs_1_, ...), custom_call_target="tpu_custom_call" | custom-call | tf_op jit(solution)/shard_map/pack/pallas_call | solution.py:641
  11.0 1.9 %collective-permute-start.1 = (f32[440,128]{1,0:T(8,128)S(1)}, f32[440,128]{1,0:T(8,128)S(1)}, u32[]{:S(2)}, u32[]{:S(2)}) collective-permute-start(f32[440,128]{1,0:T(8,128)S(1)} %get-tuple-element.31), channel_id=1, source_target_pairs={{0,4},{4,8},{8,12},{12,0},{1,5},{5,9},{9,13},{13,1},{2,6},{6,10},{... | collective-permute-start | bytes 675848 | tf_op jit(solution)/shard_map/ppermute | solution.py:596
  12.8 2.1 %collective-permute-start.2 = (f32[440,128]{1,0:T(8,128)S(1)}, f32[440,128]{1,0:T(8,128)S(1)}, u32[]{:S(2)}, u32[]{:S(2)}) collective-permute-start(f32[440,128]{1,0:T(8,128)S(1)} %get-tuple-element.32), channel_id=1, source_target_pairs={{0,12},{4,0},{8,4},{12,8},{1,13},{5,1},{9,5},{13,9},{2,14},{6,2},{... | collective-permute-start | bytes 675848 | tf_op jit(solution)/shard_map/ppermute | solution.py:596
  14.9 9.3 %spread.2 = (f32[24,152,48]{2,1,0:T(8,128)S(1)}, f32[12,19,128]{2,1,0:T(8,128)S(1)}, f32[12,19,128]{2,1,0:T(8,128)S(1)}) custom-call(s32[5]{0:T(128)S(1)} %stack.23.here.refs_0_, s32[32,4]{1,0:T(8,128)S(1)} %copy.34.refs_1_, f32[16,768]{1,0:T(8,128)S(1)} %copy-done.1, f32[3,16,768]{2,1,0:T(8,128)S(1)} %maximum_maximum_fusion.refs_0_.refs_3_, ...), custom_call_target="tpu_custom_call" | custom-call | flops 4000000000 | bytes 4000000 | tf_op jit(solution)/shard_map/spread/pallas_call | solution.py:362
  24.4 5.6 %spread.3 = (f32[14,48,128]{2,1,0:T(8,128)S(1)}, f32[7,48,128]{2,1,0:T(8,128)S(1)}, f32[6,48,128]{2,1,0:T(8,128)S(1)}, f32[3,48,128]{2,1,0:T(8,128)S(1)}) custom-call(s32[5]{0:T(128)S(1)} %stack.23.here.refs_0_, s32[16,4]{1,0:T(8,128)S(1)} %pad_add_fusion.refs_1_.refs_2_, f32[16,768]{1,0:T(8,128)S(1)} %copy-done.1, ...), custom_call_target="tpu_custom_call" | custom-call | flops 4000000000 | bytes 4000000 | tf_op jit(solution)/shard_map/spread/pallas_call | solution.py:362
  30.1 1.7 %collective-permute-start.4 = (f32[14,19,128]{2,1,0:T(8,128)S(1)}, f32[14,19,128]{2,1,0:T(8,128)S(1)}, u32[]{:S(2)}, u32[]{:S(2)}) collective-permute-start(f32[14,19,128]{2,1,0:T(8,128)S(1)} %pad_maximum_fusion.2), channel_id=1, source_target_pairs={{0,2},{2,0},{1,3},{3,1},{4,6},{6,4},{5,7},{7,5},{8,10},{10,8},{9,1... | collective-permute-start | bytes 408584 | tf_op jit(solution)/shard_map/ppermute | solution.py:596
  32.1 1.8 %collective-permute-start.6 = (f32[6,48,128]{2,1,0:T(8,128)S(1)}, f32[6,48,128]{2,1,0:T(8,128)S(1)}, u32[]{:S(2)}, u32[]{:S(2)}) collective-permute-start(f32[6,48,128]{2,1,0:T(8,128)S(1)} %get-tuple-element.41), channel_id=1, source_target_pairs={{0,4},{4,8},{8,12},{12,0},{1,5},{5,9},{9,13},{13,1},{2,6},{6,10},{... | collective-permute-start | bytes 442376 | tf_op jit(solution)/shard_map/ppermute | solution.py:596
  33.8 2.1 %collective-permute-start.7 = (f32[7,48,128]{2,1,0:T(8,128)S(1)}, f32[7,48,128]{2,1,0:T(8,128)S(1)}, u32[]{:S(2)}, u32[]{:S(2)}) collective-permute-start(f32[7,48,128]{2,1,0:T(8,128)S(1)} %get-tuple-element.42), channel_id=1, source_target_pairs={{0,12},{4,0},{8,4},{12,8},{1,13},{5,1},{9,5},{13,9},{2,14},{6,2},{... | collective-permute-start | bytes 516104 | tf_op jit(solution)/shard_map/ppermute | solution.py:596
  36.0 1.2 %collective-permute-start.3 = (f32[14,19,128]{2,1,0:T(8,128)S(1)}, f32[14,19,128]{2,1,0:T(8,128)S(1)}, u32[]{:S(2)}, u32[]{:S(2)}) collective-permute-start(f32[14,19,128]{2,1,0:T(8,128)S(1)} %pad_maximum_fusion.1), channel_id=1, source_target_pairs={{0,2},{2,0},{1,3},{3,1},{4,6},{6,4},{5,7},{7,5},{8,10},{10,8},{9,1... | collective-permute-start | bytes 408584 | tf_op jit(solution)/shard_map/ppermute | solution.py:596
  37.1 2.6 %assemble.1 = (f32[3,24,768]{2,1,0:T(8,128)S(1)}, f32[3,24,768]{2,1,0:T(8,128)S(1)}, s32[24,3]{1,0:T(8,128)S(1)}, s32[24,3]{1,0:T(8,128)S(1)}) custom-call(s32[5]{0:T(128)S(1)} %stack.23.here.refs_0_, s32[32,4]{1,0:T(8,128)S(1)} %copy.34.refs_1_, s32[16,4]{1,0:T(8,128)S(1)} %pad_add_fusion.refs_1_.refs_2_, ...), custom_call_target="tpu_custom_call" | custom-call | tf_op jit(solution)/shard_map/assemble/pallas_call | solution.py:710
  39.8 2.2 %collective-permute-done.3 = f32[14,19,128]{2,1,0:T(8,128)S(1)} collective-permute-done((f32[14,19,128]{2,1,0:T(8,128)S(1)}, f32[14,19,128]{2,1,0:T(8,128)S(1)}, u32[]{:S(2)}, u32[]{:S(2)}) %collective-permute-start.3) | collective-permute-done | bytes 136224 | tf_op jit(solution)/shard_map/ppermute | solution.py:596
  43.2 2.2 %collide.1 = (f32[19,14,16,128]{3,2,1,0:T(8,128)S(1)}, f32[14,48,128]{2,1,0:T(8,128)S(1)}, f32[5,14,16,128]{3,2,1,0:T(8,128)S(1)}) custom-call(f32[19,14,16,128]{3,2,1,0:T(8,128)S(1)} %extend.1.pops, f32[14,48,128]{2,1,0:T(8,128)S(1)} %get-tuple-element.40.refs_9_.own, f32[6,48,128]{2,1,0:T(8,128)S(1)} %collective-permute-done.6.from_low, ...), custom_call_target="tpu_custom_call" | custom-call | tf_op jit(solution)/shard_map/collide/pallas_call | solution.py:720
  45.5 2.0 %collective-permute-done.8.edge = f32[5,14,16,128]{3,2,1,0:T(8,128)S(1)} collective-permute-done((f32[5,14,16,128]{3,2,1,0:T(8,128)S(1)}, f32[5,14,16,128]{3,2,1,0:T(8,128)S(1)}, u32[]{:S(2)}, u32[]{:S(2)}) %collective-permute-start.8) | collective-permute-done | bytes 573472 | tf_op jit(solution)/shard_map/ppermute | solution.py:596
  47.5 1.4 %flow.1 = (f32[12,48,128]{2,1,0:T(8,128)S(1)}, f32[6,48,128]{2,1,0:T(8,128)S(1)}, f32[5,48,128]{2,1,0:T(8,128)S(1)}) custom-call(f32[19,14,16,128]{3,2,1,0:T(8,128)S(1)} %get-tuple-element.45.post, f32[5,14,16,128]{3,2,1,0:T(8,128)S(1)} %collective-permute-done.8.edge, f32[14,48,128]{2,1,0:T(8,128)S(1)} %get-tuple-element.47.force), custom_call_target="tpu_custom_call" | custom-call | tf_op jit(solution)/shard_map/flow/pallas_call | solution.py:733
  49.3 3.5 %collective-permute-start.10 = (f32[5,48,128]{2,1,0:T(8,128)S(1)}, f32[5,48,128]{2,1,0:T(8,128)S(1)}, u32[]{:S(2)}, u32[]{:S(2)}) collective-permute-start(f32[5,48,128]{2,1,0:T(8,128)S(1)} %get-tuple-element.49), channel_id=1, source_target_pairs={{0,12},{4,0},{8,4},{12,8},{1,13},{5,1},{9,5},{13,9},{2,14},{6,2},{... | collective-permute-start | bytes 368648 | tf_op jit(solution)/shard_map/ppermute | solution.py:596
  52.8 2.4 %renew.1 = f32[12,12,19,128]{3,2,1,0:T(8,128)} custom-call(f32[19,14,16,128]{3,2,1,0:T(8,128)S(1)} %get-tuple-element.45.post, f32[5,14,16,128]{3,2,1,0:T(8,128)S(1)} %collective-permute-done.8.edge, f32[12,48,128]{2,1,0:T(8,128)S(1)} %get-tuple-element.50.after.own), custom_call_target="tpu_custom_call" | custom-call | tf_op jit(solution)/shard_map/renew/pallas_call | solution.py:742
  55.1 3.0 %collective-permute-done.10.high_side = f32[5,48,128]{2,1,0:T(8,128)S(1)} collective-permute-done((f32[5,48,128]{2,1,0:T(8,128)S(1)}, f32[5,48,128]{2,1,0:T(8,128)S(1)}, u32[]{:S(2)}, u32[]{:S(2)}) %collective-permute-start.10) | collective-permute-done | bytes 122912 | tf_op jit(solution)/shard_map/ppermute | solution.py:596
  58.7 1.0 %collective-permute-done.13.high_far = f32[5,48,128]{2,1,0:T(8,128)S(1)} collective-permute-done((f32[5,48,128]{2,1,0:T(8,128)S(1)}, f32[5,48,128]{2,1,0:T(8,128)S(1)}, u32[]{:S(2)}, u32[]{:S(2)}) %collective-permute-start.13) | collective-permute-done | bytes 122912 | tf_op jit(solution)/shard_map/ppermute | solution.py:596
  59.7 4.9 %sample.3 = f32[3,16,768]{2,1,0:T(8,128)S(1)} custom-call(s32[24,3]{1,0:T(8,128)S(1)} %get-tuple-element.55.corner, f32[3,24,768]{2,1,0:T(8,128)S(1)} %get-tuple-element.44.refs_1_.pos, f32[6,48,128]{2,1,0:T(8,128)S(1)} %collective-permute-done.9.low_side, f32[12,48,128]{2,1,0:T(8,128)S(1)} %get-tuple-element.50.after.own, ...), custom_call_target="tpu_custom_call" | custom-call | flops 2000000000 | bytes 4000000 | tf_op jit(solution)/shard_map/sample/pallas_call | solution.py:457
  64.6 1.1 %collective-permute-start.14 = (f32[3,16,768]{2,1,0:T(8,128)S(1)}, f32[3,16,768]{2,1,0:T(8,128)S(1)}, u32[]{:S(2)}, u32[]{:S(2)}) collective-permute-start(f32[3,16,768]{2,1,0:T(8,128)S(1)} %sample.3), channel_id=1, source_target_pairs={{0,2},{2,0},{1,3},{3,1},{4,6},{6,4},{5,7},{7,5},{8,10},{10,8},{9,1... | collective-permute-start | bytes 442376 | tf_op jit(solution)/shard_map/ppermute | solution.py:596
  65.7 4.8 %sample.2 = f32[3,16,768]{2,1,0:T(8,128)S(1)} custom-call(s32[24,3]{1,0:T(8,128)S(1)} %get-tuple-element.52.corner, f32[3,24,768]{2,1,0:T(8,128)S(1)} %get-tuple-element.43.refs_0_.pos, f32[6,48,128]{2,1,0:T(8,128)S(1)} %collective-permute-done.9.low_side, f32[12,48,128]{2,1,0:T(8,128)S(1)} %get-tuple-element.50.after.own, ...), custom_call_target="tpu_custom_call" | custom-call | flops 2000000000 | bytes 4000000 | tf_op jit(solution)/shard_map/sample/pallas_call | solution.py:457
  (47 shorter events, 7.2 us)
Async XLA Ops:
  0.6 14.3 %copy-start.1 = (f32[16,768]{1,0:T(8,128)S(1)}, f32[16,768]{1,0:T(8,128)}, u32[]{:S(2)}) copy-start(f32[16,768]{1,0:T(8,128)} %constant.35.clone.refs_2_) | copy-start | bytes 147460
  0.6 14.3 %copy-start = (f32[19,12,12,128]{3,0,2,1:T(8,128)S(1)}, f32[19,12,12,128]{3,0,2,1:T(8,128)}, u32[]{:S(2)}) copy-start(f32[19,12,12,128]{3,0,2,1:T(8,128)} %param.5) | copy-start | bytes 4202500
  2.6 6.8 %collective-permute-start = (f32[3,16,768]{2,1,0:T(8,128)S(1)}, f32[3,16,768]{2,1,0:T(8,128)S(1)}, u32[]{:S(2)}, u32[]{:S(2)}) collective-permute-start(f32[3,16,768]{2,1,0:T(8,128)S(1)} %maximum_maximum_fusion.refs_0_.refs_3_), channel_id=1, source_target_pairs={{0,2},{2,0},{1,3},{3,1},{4,6},{6,4},{5,7},{7,5},{8,10},{10,8},{9,1... | collective-permute-start | bytes 442376 | tf_op jit(solution)/shard_map/ppermute | solution.py:596
  11.0 13.2 %collective-permute-start.1 = (f32[440,128]{1,0:T(8,128)S(1)}, f32[440,128]{1,0:T(8,128)S(1)}, u32[]{:S(2)}, u32[]{:S(2)}) collective-permute-start(f32[440,128]{1,0:T(8,128)S(1)} %get-tuple-element.31), channel_id=1, source_target_pairs={{0,4},{4,8},{8,12},{12,0},{1,5},{5,9},{9,13},{13,1},{2,6},{6,10},{... | collective-permute-start | bytes 675848 | tf_op jit(solution)/shard_map/ppermute | solution.py:596
  12.8 11.4 %collective-permute-start.2 = (f32[440,128]{1,0:T(8,128)S(1)}, f32[440,128]{1,0:T(8,128)S(1)}, u32[]{:S(2)}, u32[]{:S(2)}) collective-permute-start(f32[440,128]{1,0:T(8,128)S(1)} %get-tuple-element.32), channel_id=1, source_target_pairs={{0,12},{4,0},{8,4},{12,8},{1,13},{5,1},{9,5},{13,9},{2,14},{6,2},{... | collective-permute-start | bytes 675848 | tf_op jit(solution)/shard_map/ppermute | solution.py:596
  30.0 1.9 %collective-permute-start.5 = (f32[3,48,128]{2,1,0:T(8,128)S(1)}, f32[3,48,128]{2,1,0:T(8,128)S(1)}, u32[]{:S(2)}, u32[]{:S(2)}) collective-permute-start(f32[3,48,128]{2,1,0:T(8,128)S(1)} %get-tuple-element.39), channel_id=1, source_target_pairs={{0,1},{1,0},{2,3},{3,2},{4,5},{5,4},{6,7},{7,6},{8,9},{9,8},{10,11... | collective-permute-start | bytes 221192 | tf_op jit(solution)/shard_map/ppermute | solution.py:596
  30.1 9.7 %collective-permute-start.4 = (f32[14,19,128]{2,1,0:T(8,128)S(1)}, f32[14,19,128]{2,1,0:T(8,128)S(1)}, u32[]{:S(2)}, u32[]{:S(2)}) collective-permute-start(f32[14,19,128]{2,1,0:T(8,128)S(1)} %pad_maximum_fusion.2), channel_id=1, source_target_pairs={{0,2},{2,0},{1,3},{3,1},{4,6},{6,4},{5,7},{7,5},{8,10},{10,8},{9,1... | collective-permute-start | bytes 408584 | tf_op jit(solution)/shard_map/ppermute | solution.py:596
  32.1 10.3 %collective-permute-start.6 = (f32[6,48,128]{2,1,0:T(8,128)S(1)}, f32[6,48,128]{2,1,0:T(8,128)S(1)}, u32[]{:S(2)}, u32[]{:S(2)}) collective-permute-start(f32[6,48,128]{2,1,0:T(8,128)S(1)} %get-tuple-element.41), channel_id=1, source_target_pairs={{0,4},{4,8},{8,12},{12,0},{1,5},{5,9},{9,13},{13,1},{2,6},{6,10},{... | collective-permute-start | bytes 442376 | tf_op jit(solution)/shard_map/ppermute | solution.py:596
  33.8 9.4 %collective-permute-start.7 = (f32[7,48,128]{2,1,0:T(8,128)S(1)}, f32[7,48,128]{2,1,0:T(8,128)S(1)}, u32[]{:S(2)}, u32[]{:S(2)}) collective-permute-start(f32[7,48,128]{2,1,0:T(8,128)S(1)} %get-tuple-element.42), channel_id=1, source_target_pairs={{0,12},{4,0},{8,4},{12,8},{1,13},{5,1},{9,5},{13,9},{2,14},{6,2},{... | collective-permute-start | bytes 516104 | tf_op jit(solution)/shard_map/ppermute | solution.py:596
  36.0 6.0 %collective-permute-start.3 = (f32[14,19,128]{2,1,0:T(8,128)S(1)}, f32[14,19,128]{2,1,0:T(8,128)S(1)}, u32[]{:S(2)}, u32[]{:S(2)}) collective-permute-start(f32[14,19,128]{2,1,0:T(8,128)S(1)} %pad_maximum_fusion.1), channel_id=1, source_target_pairs={{0,2},{2,0},{1,3},{3,1},{4,6},{6,4},{5,7},{7,5},{8,10},{10,8},{9,1... | collective-permute-start | bytes 408584 | tf_op jit(solution)/shard_map/ppermute | solution.py:596
  45.4 2.0 %collective-permute-start.8 = (f32[5,14,16,128]{3,2,1,0:T(8,128)S(1)}, f32[5,14,16,128]{3,2,1,0:T(8,128)S(1)}, u32[]{:S(2)}, u32[]{:S(2)}) collective-permute-start(f32[5,14,16,128]{3,2,1,0:T(8,128)S(1)} %get-tuple-element.46), channel_id=1, source_target_pairs={{0,1},{1,0},{2,3},{3,2},{4,5},{5,4},{6,7},{7,6},{8,9},{9,8},{10,11... | collective-permute-start | bytes 1720328 | tf_op jit(solution)/shard_map/ppermute | solution.py:596
  48.9 9.3 %collective-permute-start.9 = (f32[6,48,128]{2,1,0:T(8,128)S(1)}, f32[6,48,128]{2,1,0:T(8,128)S(1)}, u32[]{:S(2)}, u32[]{:S(2)}) collective-permute-start(f32[6,48,128]{2,1,0:T(8,128)S(1)} %get-tuple-element.48), channel_id=1, source_target_pairs={{0,4},{4,8},{8,12},{12,0},{1,5},{5,9},{9,13},{13,1},{2,6},{6,10},{... | collective-permute-start | bytes 442376 | tf_op jit(solution)/shard_map/ppermute | solution.py:596
  49.3 10.5 %collective-permute-start.12 = (f32[12,48,128]{2,1,0:T(8,128)S(1)}, f32[12,48,128]{2,1,0:T(8,128)S(1)}, u32[]{:S(2)}, u32[]{:S(2)}) collective-permute-start(f32[12,48,128]{2,1,0:T(8,128)S(1)} %get-tuple-element.50.after.own), channel_id=1, source_target_pairs={{0,1},{1,0},{2,3},{3,2},{4,5},{5,4},{6,7},{7,6},{8,9},{9,8},{10,11... | collective-permute-start | bytes 884744 | tf_op jit(solution)/shard_map/ppermute | solution.py:596
  49.3 8.9 %collective-permute-start.10 = (f32[5,48,128]{2,1,0:T(8,128)S(1)}, f32[5,48,128]{2,1,0:T(8,128)S(1)}, u32[]{:S(2)}, u32[]{:S(2)}) collective-permute-start(f32[5,48,128]{2,1,0:T(8,128)S(1)} %get-tuple-element.49), channel_id=1, source_target_pairs={{0,12},{4,0},{8,4},{12,8},{1,13},{5,1},{9,5},{13,9},{2,14},{6,2},{... | collective-permute-start | bytes 368648 | tf_op jit(solution)/shard_map/ppermute | solution.py:596
  58.2 1.6 %collective-permute-start.11 = (f32[6,48,128]{2,1,0:T(8,128)S(1)}, f32[6,48,128]{2,1,0:T(8,128)S(1)}, u32[]{:S(2)}, u32[]{:S(2)}) collective-permute-start(f32[6,48,128]{2,1,0:T(8,128)S(1)} %collective-permute-done.9.low_side), channel_id=1, source_target_pairs={{0,1},{1,0},{2,3},{3,2},{4,5},{5,4},{6,7},{7,6},{8,9},{9,8},{10,11... | collective-permute-start | bytes 442376 | tf_op jit(solution)/shard_map/ppermute | solution.py:596
  58.2 1.5 %collective-permute-start.13 = (f32[5,48,128]{2,1,0:T(8,128)S(1)}, f32[5,48,128]{2,1,0:T(8,128)S(1)}, u32[]{:S(2)}, u32[]{:S(2)}) collective-permute-start(f32[5,48,128]{2,1,0:T(8,128)S(1)} %collective-permute-done.10.high_side), channel_id=1, source_target_pairs={{0,1},{1,0},{2,3},{3,2},{4,5},{5,4},{6,7},{7,6},{8,9},{9,8},{10,11... | collective-permute-start | bytes 368648 | tf_op jit(solution)/shard_map/ppermute | solution.py:596
  64.6 6.1 %collective-permute-start.14 = (f32[3,16,768]{2,1,0:T(8,128)S(1)}, f32[3,16,768]{2,1,0:T(8,128)S(1)}, u32[]{:S(2)}, u32[]{:S(2)}) collective-permute-start(f32[3,16,768]{2,1,0:T(8,128)S(1)} %sample.3), channel_id=1, source_target_pairs={{0,2},{2,0},{1,3},{3,1},{4,6},{6,4},{5,7},{7,5},{8,10},{10,8},{9,1... | collective-permute-start | bytes 442376 | tf_op jit(solution)/shard_map/ppermute | solution.py:596

commit v6 on v5

--- a/solution.py
+++ b/solution.py
@@ -445,11 +445,11 @@
             out[a, pl.ds(c, 1), :] = jnp.sum(mixed[16 * a : 16 * a + 16] * wy, axis=0, keepdims=True)
 
     def sample_some(i, carry):
-        for b in range(4):
-            sample(4 * i + b, b)
+        for b in range(8):
+            sample(8 * i + b, b)
         return carry
 
-    lax.fori_loop(0, cells // 4, sample_some, 0)
+    lax.fori_loop(0, cells // 8, sample_some, 0)
 
 
 def sampled(cells, images, corner, pos, parts):
@@ -463,8 +463,8 @@
             pltpu.VMEM((24, 48, 128), F32),
             pltpu.VMEM((24, 48, 128), F32),
             pltpu.VMEM((6, cells, width), F32),
-            pltpu.VMEM((4, 144, width), jnp.bfloat16),
-            pltpu.VMEM((4, 144, width), jnp.bfloat16),
+            pltpu.VMEM((8, 144, width), jnp.bfloat16),
+            pltpu.VMEM((8, 144, width), jnp.bfloat16),
         ],
         compiler_params=params(),
         name="sample",
@@ -682,6 +682,7 @@
         [below, above],
         sums=(sum_1,),
         last=True,
+        together=4,
     )
     cells = []
     for block in [raw] + guests:

time: 71.4 us -> 70.5 us (0.987)
  Pallas kernels: 35.9 us -> 34.3 us
    pallas_call x2, Pallas kernels: 14.9 us -> 13.3 us  [stage(): pl.pallas_call(functools.partial(stage_kernel, sizes, plan, last, copies,...]
where the time goes in v6:
time: 70.5 us; the launch traced here: 70.4 us
  Pallas kernels  34.3 us (49%)
  starting transfers between devices  19.3 us (27%)
  waiting for transfers between devices  11.5 us (16%)
  other arithmetic  2.86 us (4%)
  local copies, waits for them, and re-layouts  1.64 us (2%)
  between operations  0.85 us (1%)
    ppermute x15, starting transfers between devices, shifted(): lax.ppermute(x, axis, [(i, (i + distance) % count) for i in range(count)])  19.3 us
    pallas_call x2, Pallas kernels, stage(): pl.pallas_call(functools.partial(stage_kernel, sizes, plan, last, copies,...  13.3 us
    ppermute x15, waiting for transfers between devices, shifted(): lax.ppermute(x, axis, [(i, (i + distance) % count) for i in range(count)])  11.5 us
    pallas_call x2, Pallas kernels, sampled(): pl.pallas_call(functools.partial(sample_kernel, images), out_shape=jax.Sh...  9.61 us
    pallas_call x1, Pallas kernels, on_device(): pl.pallas_call(functools.partial(assemble_kernel, sizes, groups, offsets)...  2.63 us
    pallas_call x1, Pallas kernels, on_device(): pl.pallas_call(renew_kernel, out_shape=jax.ShapeDtypeStruct((nx, ny, 19,...  2.37 us
    pallas_call x1, Pallas kernels, on_device(): pl.pallas_call(collide_kernel, out_shape=(jax.ShapeDtypeStruct((19, plane...  2.21 us
    pallas_call x2, Pallas kernels, on_device(): pl.pallas_call(functools.partial(pack_kernel, capacity, slabs, crosses *...  2.19 us
  transfers between devices with their start and end apart: 15, of which 7 were waited for; matrix products, arithmetic and copies ran while one was open for 2% of the time, Pallas kernels for 29%

profile of v6, /device:TPU:0, one launch (start us, length us, event | category | flops | bytes accessed | tf_op | source)
XLA Modules:
  0.0 70.4 jit_solution(8970639819728992600)
XLA Ops:
  2.6 2.9 %collective-permute-start = (f32[3,16,768]{2,1,0:T(8,128)S(1)}, f32[3,16,768]{2,1,0:T(8,128)S(1)}, u32[]{:S(2)}, u32[]{:S(2)}) collective-permute-start(f32[3,16,768]{2,1,0:T(8,128)S(1)} %maximum_maximum_fusion.refs_0_.refs_3_), channel_id=1, source_target_pairs={{0,2},{2,0},{1,3},{3,1},{4,6},{6,4},{5,7},{7,5},{8,10},{10,8},{9,1... | collective-permute-start | bytes 442376 | tf_op jit(solution)/shard_map/ppermute | solution.py:596
  6.8 1.1 %pack.2 = (f32[440,128]{1,0:T(8,128)S(1)}, f32[440,128]{1,0:T(8,128)S(1)}) custom-call(s32[5]{0:T(128)S(1)} %stack.23.here.refs_0_, s32[16,4]{1,0:T(8,128)S(1)} %copy.32.infos, f32[3,16,768]{2,1,0:T(8,128)S(1)} %maximum_maximum_fusion.refs_0_.refs_3_, f32[2,12,19,128]{3,2,1,0:T(8,128)S(1)} %pad_maximum_fusion.refs_1_), custom_call_target="tpu_custom_call" | custom-call | tf_op jit(solution)/shard_map/pack/pallas_call | solution.py:633
  7.9 1.5 %collective-permute-done.refs_0_.refs_4_.refs_6_ = f32[3,16,768]{2,1,0:T(8,128)S(1)} collective-permute-done((f32[3,16,768]{2,1,0:T(8,128)S(1)}, f32[3,16,768]{2,1,0:T(8,128)S(1)}, u32[]{:S(2)}, u32[]{:S(2)}) %collective-permute-start) | collective-permute-done | bytes 147488 | tf_op jit(solution)/shard_map/ppermute | solution.py:596
  9.9 1.1 %pack.3 = (f32[440,128]{1,0:T(8,128)S(1)}, f32[440,128]{1,0:T(8,128)S(1)}) custom-call(s32[5]{0:T(128)S(1)} %stack.23.here.refs_0_, s32[16,4]{1,0:T(8,128)S(1)} %copy.33.infos, f32[3,16,768]{2,1,0:T(8,128)S(1)} %collective-permute-done.refs_0_.refs_4_.refs_6_, f32[440,128]{1,0:T(8,128)S(1)} %get-tuple-element.29.refs_1_, ...), custom_call_target="tpu_custom_call" | custom-call | tf_op jit(solution)/shard_map/pack/pallas_call | solution.py:641
  11.0 1.9 %collective-permute-start.1 = (f32[440,128]{1,0:T(8,128)S(1)}, f32[440,128]{1,0:T(8,128)S(1)}, u32[]{:S(2)}, u32[]{:S(2)}) collective-permute-start(f32[440,128]{1,0:T(8,128)S(1)} %get-tuple-element.31), channel_id=1, source_target_pairs={{0,4},{4,8},{8,12},{12,0},{1,5},{5,9},{9,13},{13,1},{2,6},{6,10},{... | collective-permute-start | bytes 675848 | tf_op jit(solution)/shard_map/ppermute | solution.py:596
  12.8 2.1 %collective-permute-start.2 = (f32[440,128]{1,0:T(8,128)S(1)}, f32[440,128]{1,0:T(8,128)S(1)}, u32[]{:S(2)}, u32[]{:S(2)}) collective-permute-start(f32[440,128]{1,0:T(8,128)S(1)} %get-tuple-element.32), channel_id=1, source_target_pairs={{0,12},{4,0},{8,4},{12,8},{1,13},{5,1},{9,5},{13,9},{2,14},{6,2},{... | collective-permute-start | bytes 675848 | tf_op jit(solution)/shard_map/ppermute | solution.py:596
  14.9 9.3 %spread.2 = (f32[24,152,48]{2,1,0:T(8,128)S(1)}, f32[12,19,128]{2,1,0:T(8,128)S(1)}, f32[12,19,128]{2,1,0:T(8,128)S(1)}) custom-call(s32[5]{0:T(128)S(1)} %stack.23.here.refs_0_, s32[32,4]{1,0:T(8,128)S(1)} %copy.34.refs_1_, f32[16,768]{1,0:T(8,128)S(1)} %copy-done.1, f32[3,16,768]{2,1,0:T(8,128)S(1)} %maximum_maximum_fusion.refs_0_.refs_3_, ...), custom_call_target="tpu_custom_call" | custom-call | flops 4000000000 | bytes 4000000 | tf_op jit(solution)/shard_map/spread/pallas_call | solution.py:362
  24.4 4.0 %spread.3 = (f32[14,48,128]{2,1,0:T(8,128)S(1)}, f32[7,48,128]{2,1,0:T(8,128)S(1)}, f32[6,48,128]{2,1,0:T(8,128)S(1)}, f32[3,48,128]{2,1,0:T(8,128)S(1)}) custom-call(s32[5]{0:T(128)S(1)} %stack.23.here.refs_0_, s32[16,4]{1,0:T(8,128)S(1)} %pad_add_fusion.refs_1_.refs_2_, f32[16,768]{1,0:T(8,128)S(1)} %copy-done.1, ...), custom_call_target="tpu_custom_call" | custom-call | flops 4000000000 | bytes 4000000 | tf_op jit(solution)/shard_map/spread/pallas_call | solution.py:362
  28.6 1.7 %collective-permute-start.4 = (f32[14,19,128]{2,1,0:T(8,128)S(1)}, f32[14,19,128]{2,1,0:T(8,128)S(1)}, u32[]{:S(2)}, u32[]{:S(2)}) collective-permute-start(f32[14,19,128]{2,1,0:T(8,128)S(1)} %pad_maximum_fusion.2), channel_id=1, source_target_pairs={{0,2},{2,0},{1,3},{3,1},{4,6},{6,4},{5,7},{7,5},{8,10},{10,8},{9,1... | collective-permute-start | bytes 408584 | tf_op jit(solution)/shard_map/ppermute | solution.py:596
  30.5 2.0 %collective-permute-start.6 = (f32[6,48,128]{2,1,0:T(8,128)S(1)}, f32[6,48,128]{2,1,0:T(8,128)S(1)}, u32[]{:S(2)}, u32[]{:S(2)}) collective-permute-start(f32[6,48,128]{2,1,0:T(8,128)S(1)} %get-tuple-element.41), channel_id=1, source_target_pairs={{0,4},{4,8},{8,12},{12,0},{1,5},{5,9},{9,13},{13,1},{2,6},{6,10},{... | collective-permute-start | bytes 442376 | tf_op jit(solution)/shard_map/ppermute | solution.py:596
  32.5 1.9 %collective-permute-start.7 = (f32[7,48,128]{2,1,0:T(8,128)S(1)}, f32[7,48,128]{2,1,0:T(8,128)S(1)}, u32[]{:S(2)}, u32[]{:S(2)}) collective-permute-start(f32[7,48,128]{2,1,0:T(8,128)S(1)} %get-tuple-element.42), channel_id=1, source_target_pairs={{0,12},{4,0},{8,4},{12,8},{1,13},{5,1},{9,5},{13,9},{2,14},{6,2},{... | collective-permute-start | bytes 516104 | tf_op jit(solution)/shard_map/ppermute | solution.py:596
  34.4 1.2 %collective-permute-start.3 = (f32[14,19,128]{2,1,0:T(8,128)S(1)}, f32[14,19,128]{2,1,0:T(8,128)S(1)}, u32[]{:S(2)}, u32[]{:S(2)}) collective-permute-start(f32[14,19,128]{2,1,0:T(8,128)S(1)} %pad_maximum_fusion.1), channel_id=1, source_target_pairs={{0,2},{2,0},{1,3},{3,1},{4,6},{6,4},{5,7},{7,5},{8,10},{10,8},{9,1... | collective-permute-start | bytes 408584 | tf_op jit(solution)/shard_map/ppermute | solution.py:596
  35.6 2.6 %assemble.1 = (f32[3,24,768]{2,1,0:T(8,128)S(1)}, f32[3,24,768]{2,1,0:T(8,128)S(1)}, s32[24,3]{1,0:T(8,128)S(1)}, s32[24,3]{1,0:T(8,128)S(1)}) custom-call(s32[5]{0:T(128)S(1)} %stack.23.here.refs_0_, s32[32,4]{1,0:T(8,128)S(1)} %copy.34.refs_1_, s32[16,4]{1,0:T(8,128)S(1)} %pad_add_fusion.refs_1_.refs_2_, ...), custom_call_target="tpu_custom_call" | custom-call | tf_op jit(solution)/shard_map/assemble/pallas_call | solution.py:711
  38.2 2.2 %collective-permute-done.3 = f32[14,19,128]{2,1,0:T(8,128)S(1)} collective-permute-done((f32[14,19,128]{2,1,0:T(8,128)S(1)}, f32[14,19,128]{2,1,0:T(8,128)S(1)}, u32[]{:S(2)}, u32[]{:S(2)}) %collective-permute-start.3) | collective-permute-done | bytes 136224 | tf_op jit(solution)/shard_map/ppermute | solution.py:596
  40.8 1.1 %collective-permute-done.7.from_high = f32[7,48,128]{2,1,0:T(8,128)S(1)} collective-permute-done((f32[7,48,128]{2,1,0:T(8,128)S(1)}, f32[7,48,128]{2,1,0:T(8,128)S(1)}, u32[]{:S(2)}, u32[]{:S(2)}) %collective-permute-start.7) | collective-permute-done | bytes 172064 | tf_op jit(solution)/shard_map/ppermute | solution.py:596
  41.9 2.2 %collide.1 = (f32[19,14,16,128]{3,2,1,0:T(8,128)S(1)}, f32[14,48,128]{2,1,0:T(8,128)S(1)}, f32[5,14,16,128]{3,2,1,0:T(8,128)S(1)}) custom-call(f32[19,14,16,128]{3,2,1,0:T(8,128)S(1)} %extend.1.pops, f32[14,48,128]{2,1,0:T(8,128)S(1)} %get-tuple-element.40.refs_9_.own, f32[6,48,128]{2,1,0:T(8,128)S(1)} %collective-permute-done.6.from_low, ...), custom_call_target="tpu_custom_call" | custom-call | tf_op jit(solution)/shard_map/collide/pallas_call | solution.py:721
  44.2 2.0 %collective-permute-done.8.edge = f32[5,14,16,128]{3,2,1,0:T(8,128)S(1)} collective-permute-done((f32[5,14,16,128]{3,2,1,0:T(8,128)S(1)}, f32[5,14,16,128]{3,2,1,0:T(8,128)S(1)}, u32[]{:S(2)}, u32[]{:S(2)}) %collective-permute-start.8) | collective-permute-done | bytes 573472 | tf_op jit(solution)/shard_map/ppermute | solution.py:596
  46.1 1.4 %flow.1 = (f32[12,48,128]{2,1,0:T(8,128)S(1)}, f32[6,48,128]{2,1,0:T(8,128)S(1)}, f32[5,48,128]{2,1,0:T(8,128)S(1)}) custom-call(f32[19,14,16,128]{3,2,1,0:T(8,128)S(1)} %get-tuple-element.45.post, f32[5,14,16,128]{3,2,1,0:T(8,128)S(1)} %collective-permute-done.8.edge, f32[14,48,128]{2,1,0:T(8,128)S(1)} %get-tuple-element.47.force), custom_call_target="tpu_custom_call" | custom-call | tf_op jit(solution)/shard_map/flow/pallas_call | solution.py:734
  48.3 3.1 %collective-permute-start.10 = (f32[5,48,128]{2,1,0:T(8,128)S(1)}, f32[5,48,128]{2,1,0:T(8,128)S(1)}, u32[]{:S(2)}, u32[]{:S(2)}) collective-permute-start(f32[5,48,128]{2,1,0:T(8,128)S(1)} %get-tuple-element.49), channel_id=1, source_target_pairs={{0,12},{4,0},{8,4},{12,8},{1,13},{5,1},{9,5},{13,9},{2,14},{6,2},{... | collective-permute-start | bytes 368648 | tf_op jit(solution)/shard_map/ppermute | solution.py:596
  51.4 2.4 %renew.1 = f32[12,12,19,128]{3,2,1,0:T(8,128)} custom-call(f32[19,14,16,128]{3,2,1,0:T(8,128)S(1)} %get-tuple-element.45.post, f32[5,14,16,128]{3,2,1,0:T(8,128)S(1)} %collective-permute-done.8.edge, f32[12,48,128]{2,1,0:T(8,128)S(1)} %get-tuple-element.50.after.own), custom_call_target="tpu_custom_call" | custom-call | tf_op jit(solution)/shard_map/renew/pallas_call | solution.py:743
  53.8 3.4 %collective-permute-done.10.high_side = f32[5,48,128]{2,1,0:T(8,128)S(1)} collective-permute-done((f32[5,48,128]{2,1,0:T(8,128)S(1)}, f32[5,48,128]{2,1,0:T(8,128)S(1)}, u32[]{:S(2)}, u32[]{:S(2)}) %collective-permute-start.10) | collective-permute-done | bytes 122912 | tf_op jit(solution)/shard_map/ppermute | solution.py:596
  58.7 4.9 %sample.3 = f32[3,16,768]{2,1,0:T(8,128)S(1)} custom-call(s32[24,3]{1,0:T(8,128)S(1)} %get-tuple-element.55.corner, f32[3,24,768]{2,1,0:T(8,128)S(1)} %get-tuple-element.44.refs_1_.pos, f32[6,48,128]{2,1,0:T(8,128)S(1)} %collective-permute-done.9.low_side, f32[12,48,128]{2,1,0:T(8,128)S(1)} %get-tuple-element.50.after.own, ...), custom_call_target="tpu_custom_call" | custom-call | flops 2000000000 | bytes 4000000 | tf_op jit(solution)/shard_map/sample/pallas_call | solution.py:457
  63.6 1.1 %collective-permute-start.14 = (f32[3,16,768]{2,1,0:T(8,128)S(1)}, f32[3,16,768]{2,1,0:T(8,128)S(1)}, u32[]{:S(2)}, u32[]{:S(2)}) collective-permute-start(f32[3,16,768]{2,1,0:T(8,128)S(1)} %sample.3), channel_id=1, source_target_pairs={{0,2},{2,0},{1,3},{3,1},{4,6},{6,4},{5,7},{7,5},{8,10},{10,8},{9,1... | collective-permute-start | bytes 442376 | tf_op jit(solution)/shard_map/ppermute | solution.py:596
  64.7 4.7 %sample.2 = f32[3,16,768]{2,1,0:T(8,128)S(1)} custom-call(s32[24,3]{1,0:T(8,128)S(1)} %get-tuple-element.52.corner, f32[3,24,768]{2,1,0:T(8,128)S(1)} %get-tuple-element.43.refs_0_.pos, f32[6,48,128]{2,1,0:T(8,128)S(1)} %collective-permute-done.9.low_side, f32[12,48,128]{2,1,0:T(8,128)S(1)} %get-tuple-element.50.after.own, ...), custom_call_target="tpu_custom_call" | custom-call | flops 2000000000 | bytes 4000000 | tf_op jit(solution)/shard_map/sample/pallas_call | solution.py:457
  (47 shorter events, 7.8 us)
Async XLA Ops:
  0.6 14.3 %copy-start.1 = (f32[16,768]{1,0:T(8,128)S(1)}, f32[16,768]{1,0:T(8,128)}, u32[]{:S(2)}) copy-start(f32[16,768]{1,0:T(8,128)} %constant.35.clone.refs_2_) | copy-start | bytes 147460
  0.6 14.3 %copy-start = (f32[19,12,12,128]{3,0,2,1:T(8,128)S(1)}, f32[19,12,12,128]{3,0,2,1:T(8,128)}, u32[]{:S(2)}) copy-start(f32[19,12,12,128]{3,0,2,1:T(8,128)} %param.5) | copy-start | bytes 4202500
  2.6 6.8 %collective-permute-start = (f32[3,16,768]{2,1,0:T(8,128)S(1)}, f32[3,16,768]{2,1,0:T(8,128)S(1)}, u32[]{:S(2)}, u32[]{:S(2)}) collective-permute-start(f32[3,16,768]{2,1,0:T(8,128)S(1)} %maximum_maximum_fusion.refs_0_.refs_3_), channel_id=1, source_target_pairs={{0,2},{2,0},{1,3},{3,1},{4,6},{6,4},{5,7},{7,5},{8,10},{10,8},{9,1... | collective-permute-start | bytes 442376 | tf_op jit(solution)/shard_map/ppermute | solution.py:596
  11.0 13.3 %collective-permute-start.1 = (f32[440,128]{1,0:T(8,128)S(1)}, f32[440,128]{1,0:T(8,128)S(1)}, u32[]{:S(2)}, u32[]{:S(2)}) collective-permute-start(f32[440,128]{1,0:T(8,128)S(1)} %get-tuple-element.31), channel_id=1, source_target_pairs={{0,4},{4,8},{8,12},{12,0},{1,5},{5,9},{9,13},{13,1},{2,6},{6,10},{... | collective-permute-start | bytes 675848 | tf_op jit(solution)/shard_map/ppermute | solution.py:596
  12.8 11.5 %collective-permute-start.2 = (f32[440,128]{1,0:T(8,128)S(1)}, f32[440,128]{1,0:T(8,128)S(1)}, u32[]{:S(2)}, u32[]{:S(2)}) collective-permute-start(f32[440,128]{1,0:T(8,128)S(1)} %get-tuple-element.32), channel_id=1, source_target_pairs={{0,12},{4,0},{8,4},{12,8},{1,13},{5,1},{9,5},{13,9},{2,14},{6,2},{... | collective-permute-start | bytes 675848 | tf_op jit(solution)/shard_map/ppermute | solution.py:596
  28.4 1.9 %collective-permute-start.5 = (f32[3,48,128]{2,1,0:T(8,128)S(1)}, f32[3,48,128]{2,1,0:T(8,128)S(1)}, u32[]{:S(2)}, u32[]{:S(2)}) collective-permute-start(f32[3,48,128]{2,1,0:T(8,128)S(1)} %get-tuple-element.39), channel_id=1, source_target_pairs={{0,1},{1,0},{2,3},{3,2},{4,5},{5,4},{6,7},{7,6},{8,9},{9,8},{10,11... | collective-permute-start | bytes 221192 | tf_op jit(solution)/shard_map/ppermute | solution.py:596
  28.6 9.6 %collective-permute-start.4 = (f32[14,19,128]{2,1,0:T(8,128)S(1)}, f32[14,19,128]{2,1,0:T(8,128)S(1)}, u32[]{:S(2)}, u32[]{:S(2)}) collective-permute-start(f32[14,19,128]{2,1,0:T(8,128)S(1)} %pad_maximum_fusion.2), channel_id=1, source_target_pairs={{0,2},{2,0},{1,3},{3,1},{4,6},{6,4},{5,7},{7,5},{8,10},{10,8},{9,1... | collective-permute-start | bytes 408584 | tf_op jit(solution)/shard_map/ppermute | solution.py:596
  30.5 10.3 %collective-permute-start.6 = (f32[6,48,128]{2,1,0:T(8,128)S(1)}, f32[6,48,128]{2,1,0:T(8,128)S(1)}, u32[]{:S(2)}, u32[]{:S(2)}) collective-permute-start(f32[6,48,128]{2,1,0:T(8,128)S(1)} %get-tuple-element.41), channel_id=1, source_target_pairs={{0,4},{4,8},{8,12},{12,0},{1,5},{5,9},{9,13},{13,1},{2,6},{6,10},{... | collective-permute-start | bytes 442376 | tf_op jit(solution)/shard_map/ppermute | solution.py:596
  32.5 9.4 %collective-permute-start.7 = (f32[7,48,128]{2,1,0:T(8,128)S(1)}, f32[7,48,128]{2,1,0:T(8,128)S(1)}, u32[]{:S(2)}, u32[]{:S(2)}) collective-permute-start(f32[7,48,128]{2,1,0:T(8,128)S(1)} %get-tuple-element.42), channel_id=1, source_target_pairs={{0,12},{4,0},{8,4},{12,8},{1,13},{5,1},{9,5},{13,9},{2,14},{6,2},{... | collective-permute-start | bytes 516104 | tf_op jit(solution)/shard_map/ppermute | solution.py:596
  34.4 6.0 %collective-permute-start.3 = (f32[14,19,128]{2,1,0:T(8,128)S(1)}, f32[14,19,128]{2,1,0:T(8,128)S(1)}, u32[]{:S(2)}, u32[]{:S(2)}) collective-permute-start(f32[14,19,128]{2,1,0:T(8,128)S(1)} %pad_maximum_fusion.1), channel_id=1, source_target_pairs={{0,2},{2,0},{1,3},{3,1},{4,6},{6,4},{5,7},{7,5},{8,10},{10,8},{9,1... | collective-permute-start | bytes 408584 | tf_op jit(solution)/shard_map/ppermute | solution.py:596
  44.1 2.0 %collective-permute-start.8 = (f32[5,14,16,128]{3,2,1,0:T(8,128)S(1)}, f32[5,14,16,128]{3,2,1,0:T(8,128)S(1)}, u32[]{:S(2)}, u32[]{:S(2)}) collective-permute-start(f32[5,14,16,128]{3,2,1,0:T(8,128)S(1)} %get-tuple-element.46), channel_id=1, source_target_pairs={{0,1},{1,0},{2,3},{3,2},{4,5},{5,4},{6,7},{7,6},{8,9},{9,8},{10,11... | collective-permute-start | bytes 1720328 | tf_op jit(solution)/shard_map/ppermute | solution.py:596
  47.5 9.6 %collective-permute-start.9 = (f32[6,48,128]{2,1,0:T(8,128)S(1)}, f32[6,48,128]{2,1,0:T(8,128)S(1)}, u32[]{:S(2)}, u32[]{:S(2)}) collective-permute-start(f32[6,48,128]{2,1,0:T(8,128)S(1)} %get-tuple-element.48), channel_id=1, source_target_pairs={{0,4},{4,8},{8,12},{12,0},{1,5},{5,9},{9,13},{13,1},{2,6},{6,10},{... | collective-permute-start | bytes 442376 | tf_op jit(solution)/shard_map/ppermute | solution.py:596
  48.3 10.5 %collective-permute-start.12 = (f32[12,48,128]{2,1,0:T(8,128)S(1)}, f32[12,48,128]{2,1,0:T(8,128)S(1)}, u32[]{:S(2)}, u32[]{:S(2)}) collective-permute-start(f32[12,48,128]{2,1,0:T(8,128)S(1)} %get-tuple-element.50.after.own), channel_id=1, source_target_pairs={{0,1},{1,0},{2,3},{3,2},{4,5},{5,4},{6,7},{7,6},{8,9},{9,8},{10,11... | collective-permute-start | bytes 884744 | tf_op jit(solution)/shard_map/ppermute | solution.py:596
  48.3 8.9 %collective-permute-start.10 = (f32[5,48,128]{2,1,0:T(8,128)S(1)}, f32[5,48,128]{2,1,0:T(8,128)S(1)}, u32[]{:S(2)}, u32[]{:S(2)}) collective-permute-start(f32[5,48,128]{2,1,0:T(8,128)S(1)} %get-tuple-element.49), channel_id=1, source_target_pairs={{0,12},{4,0},{8,4},{12,8},{1,13},{5,1},{9,5},{13,9},{2,14},{6,2},{... | collective-permute-start | bytes 368648 | tf_op jit(solution)/shard_map/ppermute | solution.py:596
  57.2 1.6 %collective-permute-start.11 = (f32[6,48,128]{2,1,0:T(8,128)S(1)}, f32[6,48,128]{2,1,0:T(8,128)S(1)}, u32[]{:S(2)}, u32[]{:S(2)}) collective-permute-start(f32[6,48,128]{2,1,0:T(8,128)S(1)} %collective-permute-done.9.low_side), channel_id=1, source_target_pairs={{0,1},{1,0},{2,3},{3,2},{4,5},{5,4},{6,7},{7,6},{8,9},{9,8},{10,11... | collective-permute-start | bytes 442376 | tf_op jit(solution)/shard_map/ppermute | solution.py:596
  57.2 1.5 %collective-permute-start.13 = (f32[5,48,128]{2,1,0:T(8,128)S(1)}, f32[5,48,128]{2,1,0:T(8,128)S(1)}, u32[]{:S(2)}, u32[]{:S(2)}) collective-permute-start(f32[5,48,128]{2,1,0:T(8,128)S(1)} %collective-permute-done.10.high_side), channel_id=1, source_target_pairs={{0,1},{1,0},{2,3},{3,2},{4,5},{5,4},{6,7},{7,6},{8,9},{9,8},{10,11... | collective-permute-start | bytes 368648 | tf_op jit(solution)/shard_map/ppermute | solution.py:596
  63.6 6.1 %collective-permute-start.14 = (f32[3,16,768]{2,1,0:T(8,128)S(1)}, f32[3,16,768]{2,1,0:T(8,128)S(1)}, u32[]{:S(2)}, u32[]{:S(2)}) collective-permute-start(f32[3,16,768]{2,1,0:T(8,128)S(1)} %sample.3), channel_id=1, source_target_pairs={{0,2},{2,0},{1,3},{3,1},{4,6},{6,4},{5,7},{7,5},{8,10},{10,8},{9,1... | collective-permute-start | bytes 442376 | tf_op jit(solution)/shard_map/ppermute | solution.py:596
